TPU v7x, 32 devices: a whole 2x2x4 slice. The times are simulated.
32 devices in a mesh: feat: 16 (over z, x, core), tok: 2 (over y).
Axes of the slice: x: 2, y: 2, z: 4, core: 2. Of those that a mesh axis runs over, the one named last changes fastest.
Arguments:
- acts_in: bfloat16 [768, 2, 2304], P(('tok', 'feat')), may hold values from -6 to 6
- targets: bfloat16 [768, 2, 2304], P(('tok', 'feat')), may hold values from -6 to 6
- enc_weight: bfloat16 [2, 2304, 16384], P(None, None, 'feat'), may hold values from -0.125 to 0.125
- enc_bias: float32 [2, 16384], P(None, 'feat'), may hold values from -3 to 3
- dec_weight: bfloat16 [3, 16384, 2304], P(None, 'feat'), may hold values from -0.046875 to 0.046875
Outputs:
- grad_enc: bfloat16 [2, 2304, 16384], P(None, 'tok', 'feat')
- grad_enc_bias: float32 [2, 16384], P(None, ('feat', 'tok'))
- grad_dec: bfloat16 [3, 16384, 2304], P(None, ('feat', 'tok'))
All inputs are finite; a program needn't handle non-finite values.
Results may differ from a plain program's by a relative error of at most 0.02.
Values may be sent and summed in bfloat16 or wider, within the bound.
No kernel may reach another device: no remote copies, remote signals or barrier semaphores. Data moves between devices by JAX's collectives and lax.ppermute only.
A program may use at most 128 MiB of HBM per device.

v0:
```python
import math

import jax
import jax.numpy as jnp
from jax import lax
from jax.sharding import PartitionSpec as P


def pair_slot(source, target, layers):
    return sum((layers - k for k in range(source))) + (target - source)


def shards(acts_in, targets, enc_weight, enc_bias, dec_weight):
    layers = enc_weight.shape[0]
    inputs = lax.all_gather(acts_in, "feat", axis=0, tiled=True)
    tok_rows = inputs.shape[0]
    loss_scale = 1.0 / math.sqrt(tok_rows * lax.axis_size("tok"))
    preacts = []
    coded = []
    for source in range(layers):
        value = (
            jnp.dot(inputs[:, source, :], enc_weight[source], preferred_element_type=jnp.float32)
            + enc_bias[source]
        )
        preacts.append(value)
        coded.append((0.5 * jnp.maximum(value, 0.0) ** 2).astype(jnp.bfloat16))
    pieces = [code for code in coded]
    rebuilt = []
    for decode_target in range(layers):
        total = jnp.dot(
            pieces[0],
            dec_weight[pair_slot(0, decode_target, layers)],
            preferred_element_type=jnp.float32,
        )
        for decode_source in range(1, decode_target + 1):
            total = total + jnp.dot(
                pieces[decode_source],
                dec_weight[pair_slot(decode_source, decode_target, layers)],
                preferred_element_type=jnp.float32,
            )
        rebuilt.append(total)
    own_rows = lax.psum_scatter(
        jnp.stack(rebuilt, axis=1).astype(jnp.bfloat16), "feat", scatter_dimension=0, tiled=True
    ).astype(jnp.float32)
    own_error = (own_rows - targets.astype(jnp.float32)).astype(jnp.bfloat16)
    errors = lax.all_gather(own_error, "feat", axis=0, tiled=True)
    dec_parts = []
    for source in range(layers):
        for target in range(source, layers):
            dec_parts.append(
                lax.dot_general(
                    coded[source],
                    errors[:, target, :],
                    (((0,), (0,)), ((), ())),
                    preferred_element_type=jnp.float32,
                )
                * loss_scale
            )
    dec_terms = jnp.stack(dec_parts)
    enc_parts = []
    bias_parts = []
    for source in range(layers):
        dcoded = lax.dot_general(
            errors[:, source, :],
            dec_weight[pair_slot(source, source, layers)],
            (((1,), (1,)), ((), ())),
            preferred_element_type=jnp.float32,
        )
        for target in range(source + 1, layers):
            dcoded = dcoded + lax.dot_general(
                errors[:, target, :],
                dec_weight[pair_slot(source, target, layers)],
                (((1,), (1,)), ((), ())),
                preferred_element_type=jnp.float32,
            )
        dpreact = (dcoded * jnp.maximum(preacts[source], 0.0)).astype(jnp.bfloat16)
        enc_parts.append(
            lax.dot_general(
                inputs[:, source, :],
                dpreact,
                (((0,), (0,)), ((), ())),
                preferred_element_type=jnp.float32,
            )
            * loss_scale
        )
        bias_parts.append(jnp.sum(dpreact.astype(jnp.float32), axis=0) * loss_scale)
    enc_terms = jnp.stack(enc_parts)
    bias_terms = jnp.stack(bias_parts)
    enc_summed, bias_summed, dec_summed = (
        lax.psum_scatter(
            enc_terms.astype(jnp.bfloat16), "tok", scatter_dimension=1, tiled=True
        ).astype(jnp.float32),
        lax.psum_scatter(
            bias_terms.astype(jnp.bfloat16), "tok", scatter_dimension=1, tiled=True
        ).astype(jnp.float32),
        lax.psum_scatter(
            dec_terms.astype(jnp.bfloat16), "tok", scatter_dimension=1, tiled=True
        ).astype(jnp.float32),
    )
    return (enc_summed.astype(jnp.bfloat16), bias_summed, dec_summed.astype(jnp.bfloat16))


def solution(mesh):
    return jax.shard_map(
        shards,
        mesh=mesh,
        in_specs=(
            P(("tok", "feat"), None, None),
            P(("tok", "feat"), None, None),
            P(None, None, "feat"),
            P(None, "feat"),
            P(None, "feat", None),
        ),
        out_specs=(
            P(None, "tok", "feat"),
            P(None, ("feat", "tok")),
            P(None, ("feat", "tok"), None),
        ),
        check_vma=False,
    )
```

profile of v0, /device:TPU:0, one launch (start us, length us, event | category | flops | bytes accessed | tf_op | source)
XLA Modules:
  0.0 550.0 jit_solution(7841515606033468183)
XLA Ops:
  7.2 1.6 copy.13
  9.7 51.0 %all-gather.3.cloned.1.call-done = bf16[384,2,2304]{2,0,1:T(8,128)(2,1)} async-done(((bf16[24,2,2304]{2,0,1:T(8,128)(2,1)}), bf16[384,2,2304]{2,0,1:T(8,128)(2,1)}) %all-gather.3.cloned.1.call-update) | async-done | bytes 3538960 | tf_op jit(solution)/shard_map/all_gather | solution.py:15
  60.7 6.2 %multiply_convert_fusion.8 = (bf16[384,1024]{1,0:T(8,128)(2,1)S(1)}, f32[384,1024]{1,0:T(8,128)}) fusion(f32[1024]{0:T(1024)S(1)} %bitcast.121, bf16[2,2304,1024]{2,1,0:T(8,128)(2,1)} %param.7, bf16[384,2,2304]{2,0,1:T(8,128)(2,1)} %all-gather.3.cloned.1.call-done), kind=kOutput, calls=%fused_computation.52 | convolution fusion | flops 1813905408 | bytes 8851456 | tf_op jit(solution)/shard_map/dot_general | solution.py:22
  67.0 1.5 copy-done.1
  68.5 2.0 fusion.41
  70.5 1.7 copy-done.2
  72.2 3.5 add_maximum_fusion
  75.7 2.0 fusion.7
  77.8 2.0 fusion.38
  80.1 2.1 copy.24
  82.3 67.1 %reduce-scatter.13.cloned.1.call-done = bf16[24,4608]{1,0:T(8,128)(2,1)} async-done(((bf16[384,4608]{1,0:T(8,128)(2,1)}), bf16[24,4608]{1,0:T(8,128)(2,1)}) %reduce-scatter.13.cloned.1.call-update) | async-done | bytes 221200
  149.4 1.7 subtract_convert_fusion
  151.3 47.0 %all-gather.5.cloned.1.call-done = bf16[384,2,2304]{2,0,1:T(8,128)(2,1)} async-done(((bf16[24,2,2304]{2,0,1:T(8,128)(2,1)}), bf16[384,2,2304]{2,0,1:T(8,128)(2,1)}) %all-gather.5.cloned.1.call-update) | async-done | bytes 3538960 | tf_op jit(solution)/shard_map/all_gather | solution.py:46
  198.3 5.9 %convert_reduce_fusion = (f32[1024]{0:T(1024)S(1)}, bf16[384,1024]{1,0:T(8,128)(2,1)}) fusion(f32[384,1024]{1,0:T(8,128)S(1)} %add_maximum_fusion, bf16[3,1024,2304]{2,1,0:T(8,128)(2,1)} %param.9, bf16[384,2,2304]{2,0,1:T(8,128)(2,1)} %all-gather.5.cloned.1.call-done), kind=kOutput, calls=%fused_computation.46 | convolution fusion | flops 1813511168 | bytes 8851456 | tf_op jit(solution)/shard_map/dot_general | solution.py:63
  204.3 4.5 fusion.15
  208.8 5.4 convert_reduce_fusion.1
  214.2 0.9 copy.20
  215.2 6.1 %fusion = bf16[1,2304,1024]{1,2,0:T(8,128)(2,1)} fusion(bf16[384,1024]{1,0:T(8,128)(2,1)} %get-tuple-element.19, bf16[384,2,2304]{2,0,1:T(8,128)(2,1)S(1)} %copy-done.3), kind=kOutput, calls=%fused_computation.7 | convolution fusion | flops 1816657920 | bytes 7274496 | tf_op jit(solution)/shard_map/dot_general | solution.py:78
  221.3 4.3 fusion.1
  225.6 8.3 %pad_maximum_fusion.1 = bf16[2,2304,1024]{1,2,0:T(8,128)(2,1)} fusion(bf16[1,2304,1024]{1,2,0:T(8,128)(2,1)} %fusion.1, bf16[1,2304,1024]{1,2,0:T(8,128)(2,1)} %fusion), kind=kLoop, calls=%fused_computation.1 | loop fusion | flops 4718592 | bytes 18874368 | tf_op jit(solution)/shard_map/stack | solution.py:87
  233.9 24.0 %copy.18 = bf16[2,2304,1024]{2,0,1:T(2,128)(2,1)} copy(bf16[2,2304,1024]{1,2,0:T(8,128)(2,1)} %pad_maximum_fusion.1) | data formatting | bytes 18874368
  257.9 11.3 %copy.25 = bf16[288,8,2,1024]{3,1,2,0:T(8,128)(2,1)} copy(bf16[288,8,2,1024]{3,2,1,0:T(2,128)(2,1)} %bitcast.114) | data formatting | bytes 18874368
  269.4 1.7 copy-done.5
  271.1 3.9 fusion.3
  275.0 2.9 fusion.2
  277.9 2.9 fusion.4
  280.9 6.5 %pad_maximum_fusion = bf16[3,1024,2304]{2,1,0:T(8,128)(2,1)} fusion(bf16[1,1024,2304]{2,1,0:T(8,128)(2,1)S(1)} %fusion.4, bf16[1,1024,2304]{2,1,0:T(8,128)(2,1)S(1)} %fusion.3, bf16[1,1024,2304]{2,1,0:T(8,128)(2,1)S(1)} %fusion.2), kind=kLoop, calls=%fused_computation | loop fusion | flops 14155776 | bytes 28311552 | tf_op jit(solution)/shard_map/stack | solution.py:59
  287.4 1.0 copy.21
  289.0 89.9 %reduce-scatter.15.cloned.1.call-done = bf16[1152,2048]{1,0:T(8,128)(2,1)} async-done(((bf16[2304,2048]{1,0:T(8,128)(2,1)}), bf16[1152,2048]{1,0:T(8,128)(2,1)}) %reduce-scatter.15.cloned.1.call-update) | async-done | bytes 4718608
  378.9 8.8 %reshape.29 = bf16[1152,2,1024]{2,1,0:T(2,128)(2,1)} reshape(bf16[1152,2048]{1,0:T(8,128)(2,1)} %reduce-scatter.15.cloned.1.call-done) | data formatting | bytes 9437184
  387.7 6.6 %copy.15 = bf16[2,1152,1024]{2,1,0:T(8,128)(2,1)} copy(bf16[2,1152,1024]{2,0,1:T(2,128)(2,1)} %bitcast.115) | data formatting | bytes 9437184
  394.3 148.9 %reduce-scatter.11.cloned.1.call-done = bf16[3,512,2304]{2,1,0:T(8,128)(2,1)} async-done(((bf16[3,1024,2304]{2,1,0:T(8,128)(2,1)}), bf16[3,512,2304]{2,1,0:T(8,128)(2,1)}) %reduce-scatter.11.cloned.1.call-update) | async-done | bytes 7077904 | tf_op jit(solution)/shard_map/reduce_scatter | solution.py:96
  (42 shorter events, 2.6 us)
Async XLA Ops:
  7.2 53.6 %all-gather.3.cloned.1.call-start = ((), (), s32[]{:S(2)}) async-start(), calls=%async_computation.4 | async-start | bytes 3760128 | tf_op jit(solution)/shard_map/all_gather | solution.py:15
  8.9 140.5 %reduce-scatter.13.cloned.1.call-start = ((), (), s32[]{:S(2)}) async-start(), calls=%async_computation.7 | async-start | bytes 3760128
  60.7 7.8 %copy-start.1 = (bf16[3,1024,2304]{2,1,0:T(8,128)(2,1)S(1)}, bf16[3,1024,2304]{2,1,0:T(8,128)(2,1)}, u32[]{:S(2)}) copy-start(bf16[3,1024,2304]{2,1,0:T(8,128)(2,1)} %param.9) | copy-start | bytes 42467332
  67.0 10.8 %copy-start.8 = (bf16[384,1024]{1,0:T(8,128)(2,1)}, bf16[384,1024]{1,0:T(8,128)(2,1)S(1)}, u32[]{:S(2)}) copy-start(bf16[384,1024]{1,0:T(8,128)(2,1)S(1)} %get-tuple-element.14) | copy-start | bytes 2359300
  68.5 3.7 copy-start.2
  75.7 122.6 %copy-start.6 = (f32[384,1024]{1,0:T(8,128)}, f32[384,1024]{1,0:T(8,128)S(1)}, u32[]{:S(2)}) copy-start(f32[384,1024]{1,0:T(8,128)S(1)} %add_maximum_fusion) | copy-start | bytes 4718596
  82.2 67.2 %copy-start = (bf16[24,2,2304]{2,1,0:T(2,128)(2,1)S(1)}, bf16[24,2,2304]{2,1,0:T(2,128)(2,1)}, u32[]{:S(2)}) copy-start(bf16[24,2,2304]{2,1,0:T(2,128)(2,1)} %param.6) | copy-start | bytes 663556
  82.2 116.1 %all-gather.5.cloned.1.call-start = ((), (), s32[]{:S(2)}) async-start(), calls=%async_computation.5 | async-start | bytes 3760128 | tf_op jit(solution)/shard_map/all_gather | solution.py:46
  151.1 136.3 %reduce-scatter.17.cloned.1.call-start = ((), (), s32[]{:S(2)}) async-start(), calls=%async_computation.9 | async-start | bytes 393216
  198.3 6.0 %copy-start.4 = (bf16[384,2,2304]{2,0,1:T(8,128)(2,1)S(1)}, bf16[384,2,2304]{2,0,1:T(8,128)(2,1)}, u32[]{:S(2)}) copy-start(bf16[384,2,2304]{2,0,1:T(8,128)(2,1)} %all-gather.5.cloned.1.call-done) | copy-start | bytes 10616836
  204.3 4.5 copy-start.11
  208.8 6.4 %copy-start.3 = (bf16[384,2,2304]{2,0,1:T(8,128)(2,1)S(1)}, bf16[384,2,2304]{2,0,1:T(8,128)(2,1)}, u32[]{:S(2)}) copy-start(bf16[384,2,2304]{2,0,1:T(8,128)(2,1)} %all-gather.3.cloned.1.call-done) | copy-start | bytes 10616836
  215.2 163.7 %reduce-scatter.15.cloned.1.call-start = ((), (), s32[]{:S(2)}) async-start(), calls=%async_computation.8 | async-start | bytes 14155776
  215.2 6.1 %copy-start.10 = (bf16[384,1024]{1,0:T(8,128)(2,1)S(1)}, bf16[384,1024]{1,0:T(8,128)(2,1)}, u32[]{:S(2)}) copy-start(bf16[384,1024]{1,0:T(8,128)(2,1)} %get-tuple-element.17) | copy-start | bytes 2359300
  269.1 2.0 copy-start.5
  269.2 274.0 %reduce-scatter.11.cloned.1.call-start = ((), (), s32[]{:S(2)}) async-start(), calls=%async_computation.6 | async-start | bytes 21233664 | tf_op jit(solution)/shard_map/reduce_scatter | solution.py:96
  271.1 3.9 copy-start.9
  275.0 2.9 copy-start.7
Sparse Core Ops, SparseCore 0:
  10.8 49.9 all-gather.2
  82.3 66.9 reduce-scatter.12
  152.1 46.1 all-gather.4
  215.3 10.6 reduce-scatter.16
  269.3 109.5 reduce-scatter.14
  381.7 161.3 reduce-scatter.10
where the time goes:
time: 551 us; the launch traced here: 550 us
  waiting for transfers between devices  404 us (73%)
  local copies, waits for them, and re-layouts  62 us (11%)
  matrix products  51.6 us (9%)
  other arithmetic  17.4 us (3%)
  between operations  14.3 us (3%)
    unnamed x9, waiting for transfers between devices  157 us
    reduce_scatter x1, waiting for transfers between devices, shards(): lax.psum_scatter(dec_terms.astype(jnp.bfloat16), 'tok', scatter_dimension...  149 us
    unnamed x32, local copies, waits for them, and re-layouts  61.2 us
    all_gather x1, waiting for transfers between devices, shards(): inputs = lax.all_gather(acts_in, 'feat', axis=0, tiled=True)  51 us
    all_gather x1, waiting for transfers between devices, shards(): errors = lax.all_gather(own_error, 'feat', axis=0, tiled=True)  47 us
  transfers between devices with their start and end apart: 6, of which 5 were waited for; matrix products, arithmetic and copies ran while one was open for 16% of the time, Pallas kernels for 0%

commit v1 on v0

v1 whole, which is shorter than its diff:
```python
import math

import jax
import jax.numpy as jnp
from jax import lax
from jax.sharding import PartitionSpec as P


def pair_slot(source, target, layers):
    return sum((layers - k for k in range(source))) + (target - source)


def swap(value, axis, bits):
    return lax.ppermute(value, axis, [(i, i ^ bits) for i in range(lax.axis_size(axis))])


def rows(value, start, count):
    return lax.slice_in_dim(value, start, start + count, axis=-2)


def dot(a, b, dims):
    return lax.dot_general(a, b, (dims, ((), ())), preferred_element_type=jnp.float32)


def shards(acts_in, targets, enc_weight, enc_bias, dec_weight):
    layers, width, feats = enc_weight.shape
    n = acts_in.shape[0]
    feat, tok = lax.axis_size("feat"), lax.axis_size("tok")
    half = feat // 2
    quart = feat // 4
    tok_rows = n * feat
    scale = 1.0 / math.sqrt(tok_rows * tok)
    me = lax.axis_index("tok")
    own_width, own_feats = width // tok, feats // tok

    def near(value):
        first = [value] + [swap(value, "feat", 4 * k) for k in range(1, quart)]
        return first + [swap(v, "feat", 2) for v in first]

    def both(column):
        return jnp.concatenate([column, swap(column, "feat", 1)], axis=-2)

    def encode(inputs):
        pre = []
        for s in range(layers):
            value = dot(inputs[s], enc_weight[s], ((1,), (0,))) + enc_bias[s]
            pre.append(jnp.maximum(value, 0.0))
        return pre, [(0.5 * p * p).astype(jnp.bfloat16) for p in pre]

    acts = jnp.swapaxes(acts_in, 0, 1)
    column = jnp.concatenate(near(acts), axis=-2)
    inputs = [both(column)]
    pre, coded = [], []
    p, c = encode(inputs[0])
    pre.append(p)
    coded.append(c)

    own = []
    for t in range(layers):
        total = None
        for s in range(t + 1):
            term = dot(c[s], dec_weight[pair_slot(s, t, layers)], ((1,), (0,)))
            total = term if total is None else total + term
        part = total.astype(jnp.bfloat16)
        got = swap(rows(part, half * n, half * n), "feat", 1)
        part = (rows(part, 0, half * n).astype(jnp.float32) + got.astype(jnp.float32)).astype(jnp.bfloat16)
        blocks = []
        for k in reversed(range(quart)):
            got = swap(rows(part, (quart + k) * n, n), "feat", 2)
            block = rows(part, k * n, n).astype(jnp.float32) + got.astype(jnp.float32)
            if k:
                block = swap(block.astype(jnp.bfloat16), "feat", 4 * k).astype(jnp.float32)
            blocks.append(block)
        own.append(sum(blocks[1:], blocks[0]))

    error = jnp.stack(
        [(own[t] - targets[:, t, :].astype(jnp.float32)).astype(jnp.bfloat16) for t in range(layers)]
    )

    for k in range(1, tok):
        inputs.append(both(swap(column, "tok", k)))
        p, c = encode(inputs[-1])
        pre.append(p)
        coded.append(c)

    blocks = near(error)
    errors = [both(jnp.concatenate(blocks, axis=-2))]
    for k in range(1, tok):
        z_part = [swap(b, "tok", k) for b in blocks[:quart]]
        x_part = [swap(b, "tok", k) for b in blocks[quart:quart + quart // 2]]
        x_part += [swap(b, "feat", 2) for b in z_part[quart // 2:]]
        errors.append(both(jnp.concatenate(z_part + x_part, axis=-2)))

    dpre = []
    for g in range(tok):
        group = []
        for s in range(layers):
            total = None
            for t in range(s, layers):
                term = dot(errors[g][t], dec_weight[pair_slot(s, t, layers)], ((1,), (1,)))
                total = term if total is None else total + term
            group.append((total * pre[g][s]).astype(jnp.bfloat16))
        dpre.append(group)

    def whole(parts):
        return jnp.concatenate(parts, axis=0)

    dec_out = []
    for s in range(layers):
        codes = whole([lax.dynamic_slice_in_dim(coded[g][s], me * own_feats, own_feats, axis=1) for g in range(tok)])
        for t in range(s, layers):
            out = dot(codes, whole([errors[g][t] for g in range(tok)]), ((0,), (0,)))
            dec_out.append((out * scale).astype(jnp.bfloat16))
    enc_out, bias_out = [], []
    for s in range(layers):
        seen = whole([lax.dynamic_slice_in_dim(inputs[g][s], me * own_width, own_width, axis=1) for g in range(tok)])
        grads = whole([dpre[g][s] for g in range(tok)])
        enc_out.append((dot(seen, grads, ((0,), (0,))) * scale).astype(jnp.bfloat16))
        mine = lax.dynamic_slice_in_dim(grads, me * own_feats, own_feats, axis=1)
        bias_out.append(jnp.sum(mine.astype(jnp.float32), axis=0) * scale)
    return jnp.stack(enc_out), jnp.stack(bias_out), jnp.stack(dec_out)


def solution(mesh):
    return jax.shard_map(
        shards,
        mesh=mesh,
        in_specs=(
            P(("tok", "feat"), None, None),
            P(("tok", "feat"), None, None),
            P(None, None, "feat"),
            P(None, "feat"),
            P(None, "feat", None),
        ),
        out_specs=(
            P(None, "tok", "feat"),
            P(None, ("feat", "tok")),
            P(None, ("feat", "tok"), None),
        ),
        check_vma=False,
    )
```

time: 551 us -> 228 us (0.41)
  waiting for transfers between devices: 404 us -> 89.4 us
  local copies, waits for them, and re-layouts: 62 us -> 13.2 us
  starting transfers between devices: 0.65 us -> 48.8 us
  matrix products: 51.6 us -> 67.2 us
  between operations: 14.3 us -> 1.18 us
  other arithmetic: 17.4 us -> 7.97 us
    unnamed x9 -> x0, waiting for transfers between devices: 157 us -> none
    reduce_scatter x1 -> x0, waiting for transfers between devices: 149 us -> none  [shards(): lax.psum_scatter(dec_terms.astype(jnp.bfloat16), 'tok', scatter_dimension...]
    all_gather x2 -> x0, waiting for transfers between devices: 98.1 us -> none  [the longest x1 51 us: shards(): inputs = lax.all_gather(acts_in, 'feat', axis=0, tiled=True)]
    ppermute x0 -> x43, waiting for transfers between devices: none -> 89.4 us  [swap(): lax.ppermute(value, axis, [(i, i ^ bits) for i in range(lax.axis_size(axi...]
    unnamed x32 -> x25, local copies, waits for them, and re-layouts: 61.2 us -> 8.13 us
    ppermute x0 -> x43, starting transfers between devices: none -> 48.8 us  [swap(): lax.ppermute(value, axis, [(i, i ^ bits) for i in range(lax.axis_size(axi...]
    dot_general x13 -> x18, matrix products: 51.6 us -> 67.2 us  [dot(): lax.dot_general(a, b, (dims, ((), ())), preferred_element_type=jnp.float32)]
    another operation x5, other arithmetic: 14.8 us -> 6.78 us  [the longest x3 6.6 us: shards(): return (jnp.stack(enc_out), jnp.stack(bias_out), jnp.stack(dec_out))]
  transfers between devices with their start and end apart: 6 -> 43, of which waited for: 5 -> 22; matrix products, arithmetic and copies ran while one was open for 16% -> 25% of each run, Pallas kernels for 0% -> 0%
where the time goes in v1:
time: 228 us
  waiting for transfers between devices  89.4 us (39%)
  matrix products  67.2 us (29%)
  starting transfers between devices  48.8 us (21%)
  local copies, waits for them, and re-layouts  13.2 us (6%)
  other arithmetic  7.97 us (3%)
    ppermute x43, waiting for transfers between devices, swap(): lax.ppermute(value, axis, [(i, i ^ bits) for i in range(lax.axis_size(axi...  89.4 us
    dot_general x18, matrix products, dot(): lax.dot_general(a, b, (dims, ((), ())), preferred_element_type=jnp.float32)  67.2 us
    ppermute x43, starting transfers between devices, swap(): lax.ppermute(value, axis, [(i, i ^ bits) for i in range(lax.axis_size(axi...  48.8 us
    unnamed x25, local copies, waits for them, and re-layouts  8.13 us
    another operation x3, other arithmetic, shards(): return (jnp.stack(enc_out), jnp.stack(bias_out), jnp.stack(dec_out))  6.6 us
  transfers between devices with their start and end apart: 43, of which 22 were waited for; matrix products, arithmetic and copies ran while one was open for 25% of the time, Pallas kernels for 0%

profile of v1, /device:TPU:0, one launch (start us, length us, event | category | flops | bytes accessed | tf_op | source)
XLA Modules:
  0.0 227.7 jit_solution(10255343341262892159)
XLA Ops:
  1.6 3.0 %collective-permute-start.3 = (bf16[2,24,2304]{2,1,0:T(8,128)(2,1)S(1)}, bf16[2,24,2304]{2,1,0:T(8,128)(2,1)S(1)}, u32[]{:S(2)}, u32[]{:S(2)}) collective-permute-start(bf16[2,24,2304]{2,1,0:T(8,128)(2,1)S(1)} %bitcast.141), channel_id=1, source_target_pairs={{0,4},{2,6},{4,0},{6,2},{8,12},{10,14},{12,8},{14,10},{16,20},{18,... | collective-permute-start | bytes 663560 | tf_op jit(solution)/shard_map/ppermute | solution.py:14
  4.6 3.6 %collective-permute-start.2 = (bf16[2,24,2304]{2,1,0:T(8,128)(2,1)S(1)}, bf16[2,24,2304]{2,1,0:T(8,128)(2,1)S(1)}, u32[]{:S(2)}, u32[]{:S(2)}) collective-permute-start(bf16[2,24,2304]{2,1,0:T(8,128)(2,1)S(1)} %bitcast.142), channel_id=1, source_target_pairs={{0,24},{2,26},{4,28},{6,30},{8,16},{10,18},{12,20},{14,22},{16,8},... | collective-permute-start | bytes 663560 | tf_op jit(solution)/shard_map/ppermute | solution.py:14
  10.6 4.2 %collective-permute-done.2 = bf16[2,24,2304]{2,1,0:T(8,128)(2,1)S(1)} collective-permute-done((bf16[2,24,2304]{2,1,0:T(8,128)(2,1)S(1)}, bf16[2,24,2304]{2,1,0:T(8,128)(2,1)S(1)}, u32[]{:S(2)}, u32[]{:S(2)}) %collective-permute-start.2) | collective-permute-done | bytes 221216 | tf_op jit(solution)/shard_map/ppermute | solution.py:14
  15.1 11.6 %collective-permute-done.1 = bf16[2,24,2304]{2,1,0:T(8,128)(2,1)S(1)} collective-permute-done((bf16[2,24,2304]{2,1,0:T(8,128)(2,1)S(1)}, bf16[2,24,2304]{2,1,0:T(8,128)(2,1)S(1)}, u32[]{:S(2)}, u32[]{:S(2)}) %collective-permute-start.1) | collective-permute-done | bytes 221216 | tf_op jit(solution)/shard_map/ppermute | solution.py:14
  31.6 6.3 %collective-permute-done.4 = bf16[2,24,2304]{2,1,0:T(8,128)(2,1)S(1)} collective-permute-done((bf16[2,24,2304]{2,1,0:T(8,128)(2,1)S(1)}, bf16[2,24,2304]{2,1,0:T(8,128)(2,1)S(1)}, u32[]{:S(2)}, u32[]{:S(2)}) %collective-permute-start.4) | collective-permute-done | bytes 221216 | tf_op jit(solution)/shard_map/ppermute | solution.py:14
  45.7 4.4 %fusion.72 = (bf16[384,1024]{1,0:T(8,128)(2,1)S(1)}, f32[384,1024]{1,0:T(8,128)S(1)}) fusion(f32[1024]{0:T(1024)S(1)} %bitcast.149, bf16[2,2304,1024]{2,1,0:T(8,128)(2,1)} %param.7, bf16[2,384,2304]{2,1,0:T(8,128)(2,1)S(1)} %constant_dynamic-update-slice_fusion.8), kind=kOutput, calls=%fused_computation.88 | convolution fusion | flops 1813905408 | bytes 8851456 | tf_op jit(solution)/shard_map/dot_general | solution.py:22
  50.1 4.4 %fusion.71 = (bf16[384,1024]{1,0:T(8,128)(2,1)S(1)}, f32[384,1024]{1,0:T(8,128)S(1)}) fusion(f32[1024]{0:T(1024)S(1)} %bitcast.147, bf16[2,2304,1024]{2,1,0:T(8,128)(2,1)} %param.7, bf16[2,384,2304]{2,1,0:T(8,128)(2,1)S(1)} %constant_dynamic-update-slice_fusion.8), kind=kOutput, calls=%fused_computation.87 | convolution fusion | flops 1813905408 | bytes 8851456 | tf_op jit(solution)/shard_map/dot_general | solution.py:22
  54.5 4.3 %fusion.35 = bf16[384,2304]{1,0:T(8,128)(2,1)S(1)} fusion(bf16[384,1024]{1,0:T(8,128)(2,1)S(1)} %get-tuple-element.80, bf16[3,1024,2304]{2,1,0:T(8,128)(2,1)} %param.9), kind=kOutput, calls=%fused_computation.38 | convolution fusion | flops 1812824064 | bytes 7274496 | tf_op jit(solution)/shard_map/dot_general | solution.py:22
  59.1 4.3 %fusion.4 = f32[384,2304]{1,0:T(8,128)S(1)} fusion(bf16[384,1024]{1,0:T(8,128)(2,1)S(1)} %get-tuple-element.78, bf16[3,1024,2304]{2,1,0:T(8,128)(2,1)} %param.9), kind=kOutput, calls=%fused_computation.11 | convolution fusion | flops 1811939328 | bytes 9043968 | tf_op jit(solution)/shard_map/dot_general | solution.py:22
  63.4 4.3 %fusion.32 = bf16[384,2304]{1,0:T(8,128)(2,1)S(1)} fusion(f32[384,2304]{1,0:T(8,128)S(1)} %fusion.4, bf16[384,1024]{1,0:T(8,128)(2,1)S(1)} %get-tuple-element.80, bf16[3,1024,2304]{2,1,0:T(8,128)(2,1)} %param.9), kind=kOutput, calls=%fused_computation.37 | convolution fusion | flops 1813708800 | bytes 10813440 | tf_op jit(solution)/shard_map/dot_general | solution.py:22
  68.4 14.5 %collective-permute-done.8 = bf16[2,192,2304]{2,1,0:T(8,128)(2,1)S(1)} collective-permute-done((bf16[2,192,2304]{2,1,0:T(8,128)(2,1)}, bf16[2,192,2304]{2,1,0:T(8,128)(2,1)S(1)}, u32[]{:S(2)}, u32[]{:S(2)}) %collective-permute-start.8) | collective-permute-done | bytes 1769504 | tf_op jit(solution)/shard_map/ppermute | solution.py:14
  89.9 4.2 %collective-permute-done.15 = bf16[24,2304]{1,0:T(8,128)(2,1)S(1)} collective-permute-done((bf16[24,2304]{1,0:T(8,128)(2,1)S(1)}, bf16[24,2304]{1,0:T(8,128)(2,1)S(1)}, u32[]{:S(2)}, u32[]{:S(2)}) %collective-permute-start.15) | collective-permute-done | bytes 110624 | tf_op jit(solution)/shard_map/ppermute | solution.py:14
  106.3 2.1 collective-permute-start.20
  108.8 5.8 %collective-permute-done.14 = bf16[24,2304]{1,0:T(8,128)(2,1)S(1)} collective-permute-done((bf16[24,2304]{1,0:T(8,128)(2,1)S(1)}, bf16[24,2304]{1,0:T(8,128)(2,1)S(1)}, u32[]{:S(2)}, u32[]{:S(2)}) %collective-permute-start.14) | collective-permute-done | bytes 110624 | tf_op jit(solution)/shard_map/ppermute | solution.py:14
  115.6 6.2 %collective-permute-done.22 = bf16[24,2304]{1,0:T(8,128)(2,1)S(1)} collective-permute-done((bf16[24,2304]{1,0:T(8,128)(2,1)S(1)}, bf16[24,2304]{1,0:T(8,128)(2,1)S(1)}, u32[]{:S(2)}, u32[]{:S(2)}) %collective-permute-start.22) | collective-permute-done | bytes 110624 | tf_op jit(solution)/shard_map/ppermute | solution.py:14
  121.9 2.9 %collective-permute-start.28 = (bf16[2,24,2304]{2,1,0:T(8,128)(2,1)S(1)}, bf16[2,24,2304]{2,1,0:T(8,128)(2,1)S(1)}, u32[]{:S(2)}, u32[]{:S(2)}) collective-permute-start(bf16[2,24,2304]{2,1,0:T(8,128)(2,1)S(1)} %get-tuple-element.41), channel_id=1, source_target_pairs={{0,24},{2,26},{4,28},{6,30},{8,16},{10,18},{12,20},{14,22},{16,8},... | collective-permute-start | bytes 663560 | tf_op jit(solution)/shard_map/ppermute | solution.py:14
  127.2 2.7 %collective-permute-done.28 = bf16[2,24,2304]{2,1,0:T(8,128)(2,1)S(1)} collective-permute-done((bf16[2,24,2304]{2,1,0:T(8,128)(2,1)S(1)}, bf16[2,24,2304]{2,1,0:T(8,128)(2,1)S(1)}, u32[]{:S(2)}, u32[]{:S(2)}) %collective-permute-start.28) | collective-permute-done | bytes 221216 | tf_op jit(solution)/shard_map/ppermute | solution.py:14
  129.9 7.7 %collective-permute-start.26 = (bf16[2,24,2304]{2,1,0:T(8,128)(2,1)S(1)}, bf16[2,24,2304]{2,1,0:T(8,128)(2,1)S(1)}, u32[]{:S(2)}, u32[]{:S(2)}) collective-permute-start(bf16[2,24,2304]{2,1,0:T(8,128)(2,1)S(1)} %get-tuple-element.41), channel_id=1, source_target_pairs={{0,8},{2,10},{4,12},{6,14},{8,0},{10,2},{12,4},{14,6},{16,24},{18,... | collective-permute-start | bytes 663560 | tf_op jit(solution)/shard_map/ppermute | solution.py:14
  139.2 5.3 %collective-permute-done.26 = bf16[2,24,2304]{2,1,0:T(8,128)(2,1)S(1)} collective-permute-done((bf16[2,24,2304]{2,1,0:T(8,128)(2,1)S(1)}, bf16[2,24,2304]{2,1,0:T(8,128)(2,1)S(1)}, u32[]{:S(2)}, u32[]{:S(2)}) %collective-permute-start.26) | collective-permute-done | bytes 221216 | tf_op jit(solution)/shard_map/ppermute | solution.py:14
  148.2 7.6 %collective-permute-done.30 = bf16[2,24,2304]{2,1,0:T(8,128)(2,1)S(1)} collective-permute-done((bf16[2,24,2304]{2,1,0:T(8,128)(2,1)S(1)}, bf16[2,24,2304]{2,1,0:T(8,128)(2,1)S(1)}, u32[]{:S(2)}, u32[]{:S(2)}) %collective-permute-start.30) | collective-permute-done | bytes 221216 | tf_op jit(solution)/shard_map/ppermute | solution.py:14
  156.6 5.2 %collective-permute-done.31 = bf16[2,24,2304]{2,1,0:T(8,128)(2,1)S(1)} collective-permute-done((bf16[2,24,2304]{2,1,0:T(8,128)(2,1)S(1)}, bf16[2,24,2304]{2,1,0:T(8,128)(2,1)S(1)}, u32[]{:S(2)}, u32[]{:S(2)}) %collective-permute-start.31) | collective-permute-done | bytes 221216 | tf_op jit(solution)/shard_map/ppermute | solution.py:14
  164.0 4.7 %collective-permute-done.36 = bf16[2,24,2304]{2,1,0:T(8,128)(2,1)S(1)} collective-permute-done((bf16[2,24,2304]{2,1,0:T(8,128)(2,1)S(1)}, bf16[2,24,2304]{2,1,0:T(8,128)(2,1)S(1)}, u32[]{:S(2)}, u32[]{:S(2)}) %collective-permute-start.36) | collective-permute-done | bytes 221216 | tf_op jit(solution)/shard_map/ppermute | solution.py:14
  173.7 4.3 %add_maximum_fusion = f32[384,1024]{1,0:T(8,128)S(1)} fusion(bf16[2,2304,1024]{2,1,0:T(8,128)(2,1)} %param.7, f32[1024]{0:T(1024)S(1)} %bitcast.150, bf16[2,384,2304]{2,1,0:T(8,128)(2,1)S(1)} %constant_dynamic-update-slice_fusion.17), kind=kOutput, calls=%fused_computation.92 | convolution fusion | flops 1812725760 | bytes 8065024 | tf_op jit(solution)/shard_map/dot_general | solution.py:22
  178.3 4.3 %add_maximum_fusion.1 = f32[384,1024]{1,0:T(8,128)S(1)} fusion(bf16[2,2304,1024]{2,1,0:T(8,128)(2,1)} %param.7, f32[1024]{0:T(1024)S(1)} %bitcast.148, bf16[2,384,2304]{2,1,0:T(8,128)(2,1)S(1)} %constant_dynamic-update-slice_fusion.17), kind=kOutput, calls=%fused_computation.95 | convolution fusion | flops 1812725760 | bytes 8065024 | tf_op jit(solution)/shard_map/dot_general | solution.py:22
  183.3 4.4 %multiply_convert_fusion.1 = bf16[384,1024]{1,0:T(8,128)(2,1)S(1)} fusion(f32[384,1024]{1,0:T(8,128)S(1)} %get-tuple-element.79, bf16[3,1024,2304]{2,1,0:T(8,128)(2,1)} %param.9, bf16[2,384,2304]{2,1,0:T(8,128)(2,1)S(1)} %constant_dynamic-update-slice_fusion.27), kind=kOutput, calls=%fused_computation.93 | convolution fusion | flops 1812725760 | bytes 8847360 | tf_op jit(solution)/shard_map/dot_general | solution.py:22
  187.7 4.4 %fusion.12 = f32[384,1024]{1,0:T(8,128)S(1)} fusion(bf16[3,1024,2304]{2,1,0:T(8,128)(2,1)} %param.9, bf16[2,384,2304]{2,1,0:T(8,128)(2,1)S(1)} %constant_dynamic-update-slice_fusion.27), kind=kOutput, calls=%fused_computation.19 | convolution fusion | flops 1811939328 | bytes 8060928 | tf_op jit(solution)/shard_map/dot_general | solution.py:22
  192.1 4.4 %multiply_convert_fusion.3 = bf16[384,1024]{1,0:T(8,128)(2,1)S(1)} fusion(f32[384,1024]{1,0:T(8,128)S(1)} %get-tuple-element.81, f32[384,1024]{1,0:T(8,128)S(1)} %fusion.12, bf16[3,1024,2304]{2,1,0:T(8,128)(2,1)} %param.9, bf16[2,384,2304]{2,1,0:T(8,128)(2,1)S(1)} %constant_dynamic-update-slice_fusion.27), kind=kOutput, calls=%fused_computation.96 | convolution fusion | flops 1813118976 | bytes 10420224 | tf_op jit(solution)/shard_map/dot_general | solution.py:22
  196.9 4.4 %multiply_convert_fusion = bf16[384,1024]{1,0:T(8,128)(2,1)S(1)} fusion(f32[384,1024]{1,0:T(8,128)S(1)} %add_maximum_fusion, bf16[3,1024,2304]{2,1,0:T(8,128)(2,1)} %param.9, bf16[2,384,2304]{2,1,0:T(8,128)(2,1)S(1)} %constant_dynamic-update-slice_fusion.44), kind=kOutput, calls=%fused_computation.91 | convolution fusion | flops 1812725760 | bytes 8847360 | tf_op jit(solution)/shard_map/dot_general | solution.py:22
  201.2 4.4 %fusion.10 = f32[384,1024]{1,0:T(8,128)S(1)} fusion(bf16[3,1024,2304]{2,1,0:T(8,128)(2,1)} %param.9, bf16[2,384,2304]{2,1,0:T(8,128)(2,1)S(1)} %constant_dynamic-update-slice_fusion.44), kind=kOutput, calls=%fused_computation.17 | convolution fusion | flops 1811939328 | bytes 8060928 | tf_op jit(solution)/shard_map/dot_general | solution.py:22
  205.8 4.6 %multiply_convert_fusion.2 = bf16[384,1024]{1,0:T(8,128)(2,1)S(1)} fusion(f32[384,1024]{1,0:T(8,128)S(1)} %add_maximum_fusion.1, f32[384,1024]{1,0:T(8,128)S(1)} %fusion.10, bf16[3,1024,2304]{2,1,0:T(8,128)(2,1)} %param.9, bf16[2,384,2304]{2,1,0:T(8,128)(2,1)S(1)} %constant_dynamic-update-slice_fusion.44), kind=kOutput, calls=%fused_computation.94 | convolution fusion | flops 1813118976 | bytes 10420224 | tf_op jit(solution)/shard_map/dot_general | solution.py:22
  214.9 2.6 %pad_maximum_fusion.1 = bf16[2,1152,1024]{2,1,0:T(8,128)(2,1)} fusion(bf16[1,1152,1024]{2,1,0:T(8,128)(2,1)S(1)} %fusion.59, bf16[1,1152,1024]{2,1,0:T(8,128)(2,1)S(1)} %fusion.60), kind=kLoop, calls=%fused_computation.6 | loop fusion | flops 2359296 | bytes 9437184 | tf_op jit(solution)/shard_map/stack | solution.py:121
  224.3 3.4 %pad_maximum_fusion = bf16[3,512,2304]{2,1,0:T(8,128)(2,1)} fusion(bf16[1,512,2304]{2,1,0:T(8,128)(2,1)S(1)} %fusion.42, bf16[1,512,2304]{2,1,0:T(8,128)(2,1)S(1)} %fusion.43, bf16[1,512,2304]{2,1,0:T(8,128)(2,1)S(1)} %fusion.44), kind=kLoop, calls=%fused_computation | loop fusion | flops 7077888 | bytes 14155776 | tf_op jit(solution)/shard_map/stack | solution.py:121
  (131 shorter events, 66.1 us)
Async XLA Ops:
  1.6 29.3 %collective-permute-start.3 = (bf16[2,24,2304]{2,1,0:T(8,128)(2,1)S(1)}, bf16[2,24,2304]{2,1,0:T(8,128)(2,1)S(1)}, u32[]{:S(2)}, u32[]{:S(2)}) collective-permute-start(bf16[2,24,2304]{2,1,0:T(8,128)(2,1)S(1)} %bitcast.141), channel_id=1, source_target_pairs={{0,4},{2,6},{4,0},{6,2},{8,12},{10,14},{12,8},{14,10},{16,20},{18,... | collective-permute-start | bytes 663560 | tf_op jit(solution)/shard_map/ppermute | solution.py:14
  4.6 10.2 %collective-permute-start.2 = (bf16[2,24,2304]{2,1,0:T(8,128)(2,1)S(1)}, bf16[2,24,2304]{2,1,0:T(8,128)(2,1)S(1)}, u32[]{:S(2)}, u32[]{:S(2)}) collective-permute-start(bf16[2,24,2304]{2,1,0:T(8,128)(2,1)S(1)} %bitcast.142), channel_id=1, source_target_pairs={{0,24},{2,26},{4,28},{6,30},{8,16},{10,18},{12,20},{14,22},{16,8},... | collective-permute-start | bytes 663560 | tf_op jit(solution)/shard_map/ppermute | solution.py:14
  8.2 18.5 %collective-permute-start.1 = (bf16[2,24,2304]{2,1,0:T(8,128)(2,1)S(1)}, bf16[2,24,2304]{2,1,0:T(8,128)(2,1)S(1)}, u32[]{:S(2)}, u32[]{:S(2)}) collective-permute-start(bf16[2,24,2304]{2,1,0:T(8,128)(2,1)S(1)} %bitcast.143), channel_id=1, source_target_pairs={{0,16},{2,18},{4,20},{6,22},{8,24},{10,26},{12,28},{14,30},{16,0},... | collective-permute-start | bytes 663560 | tf_op jit(solution)/shard_map/ppermute | solution.py:14
  8.2 19.1 %collective-permute-start = (bf16[2,24,2304]{2,1,0:T(8,128)(2,1)S(1)}, bf16[2,24,2304]{2,1,0:T(8,128)(2,1)S(1)}, u32[]{:S(2)}, u32[]{:S(2)}) collective-permute-start(bf16[2,24,2304]{2,1,0:T(8,128)(2,1)S(1)} %bitcast.144), channel_id=1, source_target_pairs={{0,8},{2,10},{4,12},{6,14},{8,0},{10,2},{12,4},{14,6},{16,24},{18,... | collective-permute-start | bytes 663560 | tf_op jit(solution)/shard_map/ppermute | solution.py:14
  14.8 24.5 %collective-permute-start.6 = (bf16[2,24,2304]{2,1,0:T(8,128)(2,1)S(1)}, bf16[2,24,2304]{2,1,0:T(8,128)(2,1)S(1)}, u32[]{:S(2)}, u32[]{:S(2)}) collective-permute-start(bf16[2,24,2304]{2,1,0:T(8,128)(2,1)S(1)} %collective-permute-done.2), channel_id=1, source_target_pairs={{0,4},{2,6},{4,0},{6,2},{8,12},{10,14},{12,8},{14,10},{16,20},{18,... | collective-permute-start | bytes 663560 | tf_op jit(solution)/shard_map/ppermute | solution.py:14
  26.7 11.9 %collective-permute-start.5 = (bf16[2,24,2304]{2,1,0:T(8,128)(2,1)S(1)}, bf16[2,24,2304]{2,1,0:T(8,128)(2,1)S(1)}, u32[]{:S(2)}, u32[]{:S(2)}) collective-permute-start(bf16[2,24,2304]{2,1,0:T(8,128)(2,1)S(1)} %collective-permute-done.1), channel_id=1, source_target_pairs={{0,4},{2,6},{4,0},{6,2},{8,12},{10,14},{12,8},{14,10},{16,20},{18,... | collective-permute-start | bytes 663560 | tf_op jit(solution)/shard_map/ppermute | solution.py:14
  27.3 10.6 %collective-permute-start.4 = (bf16[2,24,2304]{2,1,0:T(8,128)(2,1)S(1)}, bf16[2,24,2304]{2,1,0:T(8,128)(2,1)S(1)}, u32[]{:S(2)}, u32[]{:S(2)}) collective-permute-start(bf16[2,24,2304]{2,1,0:T(8,128)(2,1)S(1)} %collective-permute-done), channel_id=1, source_target_pairs={{0,4},{2,6},{4,0},{6,2},{8,12},{10,14},{12,8},{14,10},{16,20},{18,... | collective-permute-start | bytes 663560 | tf_op jit(solution)/shard_map/ppermute | solution.py:14
  41.5 41.3 %collective-permute-start.8 = (bf16[2,192,2304]{2,1,0:T(8,128)(2,1)}, bf16[2,192,2304]{2,1,0:T(8,128)(2,1)S(1)}, u32[]{:S(2)}, u32[]{:S(2)}) collective-permute-start(bf16[2,192,2304]{2,1,0:T(8,128)(2,1)} %get-tuple-element.61), channel_id=1, source_target_pairs={{0,1},{1,0},{2,3},{3,2},{4,5},{5,4},{6,7},{7,6},{8,9},{9,8},{10,11... | collective-permute-start | bytes 5308424 | tf_op jit(solution)/shard_map/ppermute | solution.py:14
  58.9 24.3 %collective-permute-start.10 = (bf16[192,2304]{1,0:T(8,128)(2,1)S(1)}, bf16[192,2304]{1,0:T(8,128)(2,1)S(1)}, u32[]{:S(2)}, u32[]{:S(2)}) collective-permute-start(bf16[192,2304]{1,0:T(8,128)(2,1)S(1)} %slice.173), channel_id=1, source_target_pairs={{0,2},{2,0},{4,6},{6,4},{8,10},{10,8},{12,14},{14,12},{16,18},{18,... | collective-permute-start | bytes 2654216 | tf_op jit(solution)/shard_map/ppermute | solution.py:14
  67.8 18.2 %collective-permute-start.18 = (bf16[192,2304]{1,0:T(8,128)(2,1)S(1)}, bf16[192,2304]{1,0:T(8,128)(2,1)S(1)}, u32[]{:S(2)}, u32[]{:S(2)}) collective-permute-start(bf16[192,2304]{1,0:T(8,128)(2,1)S(1)} %slice.184), channel_id=1, source_target_pairs={{0,2},{2,0},{4,6},{6,4},{8,10},{10,8},{12,14},{14,12},{16,18},{18,... | collective-permute-start | bytes 2654216 | tf_op jit(solution)/shard_map/ppermute | solution.py:14
  82.8 90.7 %collective-permute-start.9 = (bf16[2,192,2304]{2,1,0:T(8,128)(2,1)S(1)}, bf16[2,192,2304]{2,1,0:T(8,128)(2,1)S(1)}, u32[]{:S(2)}, u32[]{:S(2)}) collective-permute-start(bf16[2,192,2304]{2,1,0:T(8,128)(2,1)S(1)} %collective-permute-done.8), channel_id=1, source_target_pairs={{0,2},{2,0},{4,6},{6,4},{8,10},{10,8},{12,14},{14,12},{16,18},{18,... | collective-permute-start | bytes 5308424 | tf_op jit(solution)/shard_map/ppermute | solution.py:14
  84.0 21.2 %collective-permute-start.17 = (bf16[24,2304]{1,0:T(8,128)(2,1)S(1)}, bf16[24,2304]{1,0:T(8,128)(2,1)S(1)}, u32[]{:S(2)}, u32[]{:S(2)}) collective-permute-start(bf16[24,2304]{1,0:T(8,128)(2,1)S(1)} %get-tuple-element.15), channel_id=1, source_target_pairs={{0,4},{2,6},{4,0},{6,2},{8,12},{10,14},{12,8},{14,10},{16,20},{18,... | collective-permute-start | bytes 331784 | tf_op jit(solution)/shard_map/ppermute | solution.py:14
  85.5 8.6 %collective-permute-start.15 = (bf16[24,2304]{1,0:T(8,128)(2,1)S(1)}, bf16[24,2304]{1,0:T(8,128)(2,1)S(1)}, u32[]{:S(2)}, u32[]{:S(2)}) collective-permute-start(bf16[24,2304]{1,0:T(8,128)(2,1)S(1)} %get-tuple-element.16), channel_id=1, source_target_pairs={{0,4},{2,6},{4,0},{6,2},{8,12},{10,14},{12,8},{14,10},{16,20},{18,... | collective-permute-start | bytes 331784 | tf_op jit(solution)/shard_map/ppermute | solution.py:14
  86.1 10.4 %collective-permute-start.13 = (bf16[24,2304]{1,0:T(8,128)(2,1)S(1)}, bf16[24,2304]{1,0:T(8,128)(2,1)S(1)}, u32[]{:S(2)}, u32[]{:S(2)}) collective-permute-start(bf16[24,2304]{1,0:T(8,128)(2,1)S(1)} %get-tuple-element.17), channel_id=1, source_target_pairs={{0,4},{2,6},{4,0},{6,2},{8,12},{10,14},{12,8},{14,10},{16,20},{18,... | collective-permute-start | bytes 331784 | tf_op jit(solution)/shard_map/ppermute | solution.py:14
  89.3 9.5 %collective-permute-start.19 = (bf16[24,2304]{1,0:T(8,128)(2,1)S(1)}, bf16[24,2304]{1,0:T(8,128)(2,1)S(1)}, u32[]{:S(2)}, u32[]{:S(2)}) collective-permute-start(bf16[24,2304]{1,0:T(8,128)(2,1)S(1)} %get-tuple-element.21), channel_id=1, source_target_pairs={{0,4},{2,6},{4,0},{6,2},{8,12},{10,14},{12,8},{14,10},{16,20},{18,... | collective-permute-start | bytes 331784 | tf_op jit(solution)/shard_map/ppermute | solution.py:14
  103.2 11.4 %collective-permute-start.14 = (bf16[24,2304]{1,0:T(8,128)(2,1)S(1)}, bf16[24,2304]{1,0:T(8,128)(2,1)S(1)}, u32[]{:S(2)}, u32[]{:S(2)}) collective-permute-start(bf16[24,2304]{1,0:T(8,128)(2,1)S(1)} %get-tuple-element.13), channel_id=1, source_target_pairs={{0,16},{2,18},{4,20},{6,22},{8,24},{10,26},{12,28},{14,30},{16,0},... | collective-permute-start | bytes 331784 | tf_op jit(solution)/shard_map/ppermute | solution.py:14
  105.2 9.5 %collective-permute-start.25 = (bf16[24,2304]{1,0:T(8,128)(2,1)S(1)}, bf16[24,2304]{1,0:T(8,128)(2,1)S(1)}, u32[]{:S(2)}, u32[]{:S(2)}) collective-permute-start(bf16[24,2304]{1,0:T(8,128)(2,1)S(1)} %get-tuple-element.22), channel_id=1, source_target_pairs={{0,4},{2,6},{4,0},{6,2},{8,12},{10,14},{12,8},{14,10},{16,20},{18,... | collective-permute-start | bytes 331784 | tf_op jit(solution)/shard_map/ppermute | solution.py:14
  106.3 8.4 %collective-permute-start.20 = (bf16[24,2304]{1,0:T(8,128)(2,1)S(1)}, bf16[24,2304]{1,0:T(8,128)(2,1)S(1)}, u32[]{:S(2)}, u32[]{:S(2)}) collective-permute-start(bf16[24,2304]{1,0:T(8,128)(2,1)S(1)} %get-tuple-element.18), channel_id=1, source_target_pairs={{0,24},{2,26},{4,28},{6,30},{8,16},{10,18},{12,20},{14,22},{16,8},... | collective-permute-start | bytes 331784 | tf_op jit(solution)/shard_map/ppermute | solution.py:14
  124.8 12.8 %collective-permute-start.34 = (bf16[2,24,2304]{2,1,0:T(8,128)(2,1)S(1)}, bf16[2,24,2304]{2,1,0:T(8,128)(2,1)S(1)}, u32[]{:S(2)}, u32[]{:S(2)}) collective-permute-start(bf16[2,24,2304]{2,1,0:T(8,128)(2,1)S(1)} %get-tuple-element.41), channel_id=1, source_target_pairs={{0,1},{1,0},{2,3},{3,2},{4,5},{5,4},{6,7},{7,6},{8,9},{9,8},{10,11... | collective-permute-start | bytes 663560 | tf_op jit(solution)/shard_map/ppermute | solution.py:14
  126.7 18.5 %collective-permute-start.29 = (bf16[2,24,2304]{2,1,0:T(8,128)(2,1)S(1)}, bf16[2,24,2304]{2,1,0:T(8,128)(2,1)S(1)}, u32[]{:S(2)}, u32[]{:S(2)}) collective-permute-start(bf16[2,24,2304]{2,1,0:T(8,128)(2,1)S(1)} %get-tuple-element.41), channel_id=1, source_target_pairs={{0,4},{2,6},{4,0},{6,2},{8,12},{10,14},{12,8},{14,10},{16,20},{18,... | collective-permute-start | bytes 663560 | tf_op jit(solution)/shard_map/ppermute | solution.py:14
  127.2 19.4 %collective-permute-start.27 = (bf16[2,24,2304]{2,1,0:T(8,128)(2,1)S(1)}, bf16[2,24,2304]{2,1,0:T(8,128)(2,1)S(1)}, u32[]{:S(2)}, u32[]{:S(2)}) collective-permute-start(bf16[2,24,2304]{2,1,0:T(8,128)(2,1)S(1)} %get-tuple-element.41), channel_id=1, source_target_pairs={{0,16},{2,18},{4,20},{6,22},{8,24},{10,26},{12,28},{14,30},{16,0},... | collective-permute-start | bytes 663560 | tf_op jit(solution)/shard_map/ppermute | solution.py:14
  129.9 14.6 %collective-permute-start.26 = (bf16[2,24,2304]{2,1,0:T(8,128)(2,1)S(1)}, bf16[2,24,2304]{2,1,0:T(8,128)(2,1)S(1)}, u32[]{:S(2)}, u32[]{:S(2)}) collective-permute-start(bf16[2,24,2304]{2,1,0:T(8,128)(2,1)S(1)} %get-tuple-element.41), channel_id=1, source_target_pairs={{0,8},{2,10},{4,12},{6,14},{8,0},{10,2},{12,4},{14,6},{16,24},{18,... | collective-permute-start | bytes 663560 | tf_op jit(solution)/shard_map/ppermute | solution.py:14
  137.6 26.3 %collective-permute-start.37 = (bf16[2,24,2304]{2,1,0:T(8,128)(2,1)S(1)}, bf16[2,24,2304]{2,1,0:T(8,128)(2,1)S(1)}, u32[]{:S(2)}, u32[]{:S(2)}) collective-permute-start(bf16[2,24,2304]{2,1,0:T(8,128)(2,1)S(1)} %collective-permute-done.28), channel_id=1, source_target_pairs={{0,1},{1,0},{2,3},{3,2},{4,5},{5,4},{6,7},{7,6},{8,9},{9,8},{10,11... | collective-permute-start | bytes 663560 | tf_op jit(solution)/shard_map/ppermute | solution.py:14
  144.5 18.9 %collective-permute-start.32 = (bf16[2,24,2304]{2,1,0:T(8,128)(2,1)S(1)}, bf16[2,24,2304]{2,1,0:T(8,128)(2,1)S(1)}, u32[]{:S(2)}, u32[]{:S(2)}) collective-permute-start(bf16[2,24,2304]{2,1,0:T(8,128)(2,1)S(1)} %collective-permute-done.28), channel_id=1, source_target_pairs={{0,4},{2,6},{4,0},{6,2},{8,12},{10,14},{12,8},{14,10},{16,20},{18,... | collective-permute-start | bytes 663560 | tf_op jit(solution)/shard_map/ppermute | solution.py:14
  145.2 10.7 %collective-permute-start.30 = (bf16[2,24,2304]{2,1,0:T(8,128)(2,1)S(1)}, bf16[2,24,2304]{2,1,0:T(8,128)(2,1)S(1)}, u32[]{:S(2)}, u32[]{:S(2)}) collective-permute-start(bf16[2,24,2304]{2,1,0:T(8,128)(2,1)S(1)} %collective-permute-done.26), channel_id=1, source_target_pairs={{0,4},{2,6},{4,0},{6,2},{8,12},{10,14},{12,8},{14,10},{16,20},{18,... | collective-permute-start | bytes 663560 | tf_op jit(solution)/shard_map/ppermute | solution.py:14
  146.6 25.3 %collective-permute-start.38 = (bf16[2,24,2304]{2,1,0:T(8,128)(2,1)S(1)}, bf16[2,24,2304]{2,1,0:T(8,128)(2,1)S(1)}, u32[]{:S(2)}, u32[]{:S(2)}) collective-permute-start(bf16[2,24,2304]{2,1,0:T(8,128)(2,1)S(1)} %collective-permute-done.29), channel_id=1, source_target_pairs={{0,1},{1,0},{2,3},{3,2},{4,5},{5,4},{6,7},{7,6},{8,9},{9,8},{10,11... | collective-permute-start | bytes 663560 | tf_op jit(solution)/shard_map/ppermute | solution.py:14
  163.3 8.1 %collective-permute-start.35 = (bf16[2,24,2304]{2,1,0:T(8,128)(2,1)S(1)}, bf16[2,24,2304]{2,1,0:T(8,128)(2,1)S(1)}, u32[]{:S(2)}, u32[]{:S(2)}) collective-permute-start(bf16[2,24,2304]{2,1,0:T(8,128)(2,1)S(1)} %collective-permute-done.26), channel_id=1, source_target_pairs={{0,1},{1,0},{2,3},{3,2},{4,5},{5,4},{6,7},{7,6},{8,9},{9,8},{10,11... | collective-permute-start | bytes 663560 | tf_op jit(solution)/shard_map/ppermute | solution.py:14
  164.0 19.3 %collective-permute-start.33 = (bf16[2,192,2304]{2,1,0:T(8,128)(2,1)S(1)}, bf16[2,192,2304]{2,1,0:T(8,128)(2,1)S(1)}, u32[]{:S(2)}, u32[]{:S(2)}) collective-permute-start(bf16[2,192,2304]{2,1,0:T(8,128)(2,1)S(1)} %get-tuple-element.25), channel_id=1, source_target_pairs={{0,2},{2,0},{4,6},{6,4},{8,10},{10,8},{12,14},{14,12},{16,18},{18,... | collective-permute-start | bytes 5308424 | tf_op jit(solution)/shard_map/ppermute | solution.py:14
  168.7 14.4 %collective-permute-start.41 = (bf16[2,24,2304]{2,1,0:T(8,128)(2,1)S(1)}, bf16[2,24,2304]{2,1,0:T(8,128)(2,1)S(1)}, u32[]{:S(2)}, u32[]{:S(2)}) collective-permute-start(bf16[2,24,2304]{2,1,0:T(8,128)(2,1)S(1)} %collective-permute-done.37), channel_id=1, source_target_pairs={{0,4},{2,6},{4,0},{6,2},{8,12},{10,14},{12,8},{14,10},{16,20},{18,... | collective-permute-start | bytes 663560 | tf_op jit(solution)/shard_map/ppermute | solution.py:14
  171.4 11.6 %collective-permute-start.40 = (bf16[2,24,2304]{2,1,0:T(8,128)(2,1)S(1)}, bf16[2,24,2304]{2,1,0:T(8,128)(2,1)S(1)}, u32[]{:S(2)}, u32[]{:S(2)}) collective-permute-start(bf16[2,24,2304]{2,1,0:T(8,128)(2,1)S(1)} %collective-permute-done.36), channel_id=1, source_target_pairs={{0,4},{2,6},{4,0},{6,2},{8,12},{10,14},{12,8},{14,10},{16,20},{18,... | collective-permute-start | bytes 663560 | tf_op jit(solution)/shard_map/ppermute | solution.py:14
  171.9 11.1 %collective-permute-start.39 = (bf16[2,24,2304]{2,1,0:T(8,128)(2,1)S(1)}, bf16[2,24,2304]{2,1,0:T(8,128)(2,1)S(1)}, u32[]{:S(2)}, u32[]{:S(2)}) collective-permute-start(bf16[2,24,2304]{2,1,0:T(8,128)(2,1)S(1)} %collective-permute-done.30), channel_id=1, source_target_pairs={{0,1},{1,0},{2,3},{3,2},{4,5},{5,4},{6,7},{7,6},{8,9},{9,8},{10,11... | collective-permute-start | bytes 663560 | tf_op jit(solution)/shard_map/ppermute | solution.py:14
  183.1 13.6 %collective-permute-start.42 = (bf16[2,192,2304]{2,1,0:T(8,128)(2,1)S(1)}, bf16[2,192,2304]{2,1,0:T(8,128)(2,1)S(1)}, u32[]{:S(2)}, u32[]{:S(2)}) collective-permute-start(bf16[2,192,2304]{2,1,0:T(8,128)(2,1)S(1)} %get-tuple-element.42), channel_id=1, source_target_pairs={{0,2},{2,0},{4,6},{6,4},{8,10},{10,8},{12,14},{14,12},{16,18},{18,... | collective-permute-start | bytes 5308424 | tf_op jit(solution)/shard_map/ppermute | solution.py:14
  (12 other events, 103.0 us)

commit v2 on v1

v2 whole, which is shorter than its diff:
```python
import functools
import math

import jax
import jax.numpy as jnp
from jax import lax
from jax.experimental import pallas as pl
from jax.experimental.pallas import tpu as pltpu
from jax.sharding import PartitionSpec as P

MIB = 1 << 20


def pair_slot(source, target, layers):
    return sum((layers - k for k in range(source))) + (target - source)


def swap(value, axis, bits):
    return lax.ppermute(value, axis, [(i, i ^ bits) for i in range(lax.axis_size(axis))])


def cat(parts):
    return parts[0] if len(parts) == 1 else jnp.concatenate(parts, axis=0)


def dot(a, b, dims):
    return lax.dot_general(a, b, (dims, ((), ())), preferred_element_type=jnp.float32)


def piece(size, most):
    for c in range(most - most % 128, 0, -128):
        if size % c == 0:
            return c
    return size


def share(parts, own, me):
    if own % 128:
        return [(lax.dynamic_slice_in_dim(p, me[0] * own, own, axis=1), (p.shape[0], own), lambda j, me: (0, 0)) for p in parts]
    return [(p, (p.shape[0], own), lambda j, me: (0, me[0])) for p in parts]


def view(ref, block, index):
    at = []
    for size, most, i in zip(block, ref.shape, index):
        start = i * size
        at.append(slice(None) if size == most else pl.ds(start if isinstance(start, int) else pl.multiple_of(start, size), size))
    return ref.at[tuple(at)]


def inside(count):
    return [pl.BlockSpec(memory_space=pltpu.VMEM)] * count


def local(kernel, name, arrays, outs, after=(), scalars=(), extra=0):
    skip = len(after)
    return pl.pallas_call(
        lambda *refs: kernel(*refs[skip:]),
        name=name,
        out_shape=[pltpu.VMEM(s, d) for s, d in outs],
        in_specs=[pl.BlockSpec(memory_space=pl.ANY)] * skip
        + [pl.BlockSpec(memory_space=pltpu.SMEM)] * len(scalars)
        + inside(len(arrays)),
        out_specs=inside(len(outs)),
        compiler_params=pltpu.CompilerParams(vmem_limit_bytes=4 * MIB + extra),
        cost_estimate=pl.CostEstimate(flops=0, bytes_accessed=0, transcendentals=0),
    )(*after, *scalars, *[pltpu.with_memory_space_constraint(a, pltpu.VMEM) for a in arrays])


def steps_body(kernel, steps, ins, outs, *refs):
    for j in range(steps):
        kernel(*[view(r, b, m(j)) for r, (b, m) in zip(refs, ins + outs)])


def call(kernel, name, steps, ins, outs, flops, scalars=(), resident=False, after=()):
    if resident:
        body = functools.partial(steps_body, kernel, steps, [i[1:] for i in ins], [o[2:] for o in outs])
        return local(body, name, [i[0] for i in ins], [o[:2] for o in outs], after)
    moved = sum(math.prod(a.shape) * a.dtype.itemsize for a, _, _ in ins)
    moved += sum(math.prod(s) * jnp.dtype(d).itemsize for s, d, _, _ in outs)
    return pl.pallas_call(
        kernel,
        name=name,
        out_shape=[jax.ShapeDtypeStruct(s, d) for s, d, _, _ in outs],
        grid_spec=pltpu.PrefetchScalarGridSpec(
            num_scalar_prefetch=len(scalars),
            grid=(steps,),
            in_specs=[pl.BlockSpec(b, m) for _, b, m in ins],
            out_specs=[pl.BlockSpec(b, m) for _, _, b, m in outs],
        ),
        compiler_params=pltpu.CompilerParams(vmem_limit_bytes=32 * MIB),
        cost_estimate=pl.CostEstimate(flops=flops, bytes_accessed=moved, transcendentals=0),
    )(*scalars, *[i[0] for i in ins])


def load_kernel(count, *refs):
    sources, places, sems = refs[:count], refs[count:2 * count], refs[2 * count]
    copies = [pltpu.make_async_copy(sources[i], places[i], sems.at[i]) for i in range(count)]
    for copy in copies:
        copy.start()
    for copy in copies:
        copy.wait()


def load(arrays, after=()):
    count, skip = len(arrays), len(after)
    return pl.pallas_call(
        lambda *refs: load_kernel(count, *refs[skip:]),
        name="load",
        out_shape=[pltpu.VMEM(a.shape, a.dtype) for a in arrays],
        in_specs=[pl.BlockSpec(memory_space=pl.ANY)] * skip + [pl.BlockSpec(memory_space=pltpu.HBM)] * count,
        out_specs=inside(count),
        scratch_shapes=[pltpu.SemaphoreType.DMA((count,))],
        compiler_params=pltpu.CompilerParams(vmem_limit_bytes=MIB),
        cost_estimate=pl.CostEstimate(flops=0, bytes_accessed=0, transcendentals=0),
    )(*after, *[pltpu.with_memory_space_constraint(a, pltpu.HBM) for a in arrays])


def wide(ref):
    return ref[...].astype(jnp.float32)


def join_kernel(groups, *refs):
    ins, outs = refs[:sum(groups)], refs[sum(groups):]
    for count, out in zip(groups, outs):
        out[...] = cat([wide(r) for r in ins[:count]]).astype(out.dtype)
        ins = ins[count:]


def join(lists, after=(), resident=True):
    if not resident:
        return [cat(parts) for parts in lists]
    outs = [((sum(p.shape[0] for p in parts), parts[0].shape[1]), parts[0].dtype) for parts in lists]
    kernel = functools.partial(join_kernel, [len(parts) for parts in lists])
    return local(kernel, "join", [p for parts in lists for p in parts], outs, after)


def pair_kernel(n, keep, got, low, high_rest, high_own):
    part = wide(keep) + wide(got)
    half = part.shape[0] // 2
    low[...] = part[:half]
    high_own[...] = part[half:half + n].astype(high_own.dtype)
    high_rest[...] = part[half + n:].astype(high_rest.dtype)


def line_kernel(n, low, got, *outs):
    part = low[n:] + wide(got)
    for k, out in enumerate(outs):
        out[...] = part[k * n:(k + 1) * n].astype(out.dtype)


def error_kernel(n, low, *refs):
    refs, target, out = refs[:-2], refs[-2], refs[-1]
    value = low[:n]
    for r in refs:
        value = value + wide(r)
    out[...] = (value - wide(target)).astype(out.dtype)


def run(kernel, name, arrays, outs, after, resident):
    if resident:
        return local(kernel, name, arrays, outs, after)
    cells = [Cell(a) for a in arrays] + [Cell(None, d) for _, d in outs]
    kernel(*cells)
    return [c.value for c in cells[len(arrays):]]


class Cell:
    def __init__(self, value, dtype=None):
        self.value, self.dtype = value, dtype

    def __getitem__(self, at):
        return self.value[at]

    def __setitem__(self, at, value):
        self.value = value


def encode_kernel(parts, *refs):
    x = cat([r[...] for r in refs[:parts]])
    w, b, pre, code = refs[parts:]
    value = jnp.maximum(dot(x, w[0], ((1,), (0,))) + b[0], 0.0)
    pre[...] = value
    code[...] = (0.5 * value * value).astype(code.dtype)


def encode(source, parts, weight, bias, resident, after=()):
    _, width, feats = weight.shape
    m = sum(p.shape[0] for p in parts)
    c = piece(feats, 256)
    ins = [(p, p.shape, lambda j: (0, 0)) for p in parts]
    ins.append((weight, (1, width, c), lambda j: (source, 0, j)))
    ins.append((bias, (1, 1, c), lambda j: (source, 0, j)))
    outs = [((m, feats), d, (m, c), lambda j: (0, j)) for d in (jnp.float32, jnp.bfloat16)]
    return call(
        functools.partial(encode_kernel, len(parts)), "encode", feats // c, ins, outs, 2 * m * width * feats, (), resident, after
    )


def decode_kernel(sources, *refs):
    total = None
    for s in range(sources):
        term = dot(refs[s][...], refs[sources + s][0], ((1,), (0,)))
        total = term if total is None else total + term
    keep, give = refs[2 * sources:]
    half = keep.shape[0]
    keep[...] = total[:half].astype(keep.dtype)
    give[...] = total[half:].astype(give.dtype)


def decode(target, codes, weight, layers, resident, after=()):
    _, feats, width = weight.shape
    m = codes[0].shape[0]
    c = piece(width, 768)
    used = codes[: target + 1]
    ins = [(a, a.shape, lambda j: (0, 0)) for a in used]
    for s in range(target + 1):
        slot = pair_slot(s, target, layers)
        ins.append((weight, (1, feats, c), lambda j, slot=slot: (slot, 0, j)))
    outs = [((m // 2, width), jnp.bfloat16, (m // 2, c), lambda j: (0, j))] * 2
    return call(
        functools.partial(decode_kernel, target + 1),
        "decode",
        width // c,
        ins,
        outs,
        2 * m * width * feats * (target + 1),
        (),
        resident,
        after,
    )


def back_kernel(layers, parts, *refs):
    errors = [cat([r[...] for r in refs[t * parts:(t + 1) * parts]]) for t in range(layers)]
    refs = refs[layers * parts:]
    pre, refs = refs[:layers], refs[layers:]
    pairs = layers * (layers + 1) // 2
    weight, refs = refs[:pairs], refs[pairs:]
    out, total = refs[:layers], refs[layers]
    for s in range(layers):
        value = None
        for t in range(s, layers):
            term = dot(errors[t], weight[pair_slot(s, t, layers)][0], ((1,), (1,)))
            value = term if value is None else value + term
        value = (value * pre[s][...]).astype(out[s].dtype)
        out[s][...] = value
        total[s] = jnp.sum(value.astype(jnp.float32), axis=0, keepdims=True)


def back(errors, pre, weight, layers, resident, after=()):
    pairs, feats, width = weight.shape
    m = pre[0].shape[0]
    c = piece(feats, 256)
    ins = [(e, e.shape, lambda j: (0, 0)) for t in range(layers) for e in errors[t]]
    ins += [(p, (m, c), lambda j: (0, j)) for p in pre]
    ins += [(weight, (1, c, width), lambda j, k=k: (k, j, 0)) for k in range(pairs)]
    outs = [((m, feats), jnp.bfloat16, (m, c), lambda j: (0, j))] * layers
    outs.append(((layers, 1, feats), jnp.float32, (layers, 1, c), lambda j: (0, 0, j)))
    got = call(
        functools.partial(back_kernel, layers, len(errors[0])),
        "back",
        feats // c,
        ins,
        outs,
        2 * m * width * feats * pairs,
        (),
        resident,
        after,
    )
    return got[:layers], got[layers]


def dec_kernel(layers, scale, counts, me, *refs):
    a, b = counts
    codes = [cat([r[...] for r in refs[s * a:(s + 1) * a]]) for s in range(layers)]
    refs = refs[layers * a:]
    errors = [cat([r[...] for r in refs[t * b:(t + 1) * b]]) for t in range(layers)]
    out = refs[layers * b]
    for s in range(layers):
        for t in range(s, layers):
            value = dot(codes[s], errors[t], ((0,), (0,))) * scale
            out[pair_slot(s, t, layers)] = value.astype(out.dtype)


def dec_grads(codes, errors, me, own, scale, layers):
    width = errors[0][0].shape[1]
    pairs = layers * (layers + 1) // 2
    m = sum(p.shape[0] for p in codes[0])
    c = piece(width, 768)
    ins = [i for s in range(layers) for i in share(codes[s], own, me)]
    ins += [(p, (p.shape[0], c), lambda j, me: (0, j)) for t in range(layers) for p in errors[t]]
    outs = [((pairs, own, width), jnp.bfloat16, (pairs, own, c), lambda j, me: (0, 0, j))]
    return call(
        functools.partial(dec_kernel, layers, scale, (len(codes[0]), len(errors[0]))),
        "dec_grads",
        width // c,
        ins,
        outs,
        2 * m * width * own * pairs,
        (me,),
    )[0]


def enc_kernel(layers, scale, counts, me, *refs):
    a, b = counts
    inputs = [cat([r[...] for r in refs[s * a:(s + 1) * a]]) for s in range(layers)]
    refs = refs[layers * a:]
    grads = [cat([r[...] for r in refs[s * b:(s + 1) * b]]) for s in range(layers)]
    out = refs[layers * b]
    for s in range(layers):
        out[s] = (dot(inputs[s], grads[s], ((0,), (0,))) * scale).astype(out.dtype)


def enc_grads(inputs, grads, me, own, scale, layers):
    feats = grads[0][0].shape[1]
    m = sum(p.shape[0] for p in inputs[0])
    c = piece(feats, 256)
    ins = [i for s in range(layers) for i in share(inputs[s], own, me)]
    ins += [(p, (p.shape[0], c), lambda j, me: (0, j)) for s in range(layers) for p in grads[s]]
    outs = [((layers, own, feats), jnp.bfloat16, (layers, own, c), lambda j, me: (0, 0, j))]
    return call(
        functools.partial(enc_kernel, layers, scale, (len(inputs[0]), len(grads[0]))),
        "enc_grads",
        feats // c,
        ins,
        outs,
        2 * m * own * feats * layers,
        (me,),
    )[0]


def grads_body(layers, scale, counts, own, *refs):
    lists = []
    for count in counts:
        lists.append([refs[s * count:(s + 1) * count] for s in range(layers)])
        refs = refs[layers * count:]
    codes, errors, inputs, grads = lists
    sums, refs = refs[:counts[-1]], refs[counts[-1]:]
    dec_out, enc_out, bias_out, dec_held, enc_held, dec_sems, enc_sems = refs
    copies = []
    me = lax.axis_index("tok")

    def mine(size):
        return pl.ds(pl.multiple_of(me * size, 128), size)

    def leave(held, out, sems, slot, left, right):
        width = right.shape[1]
        size = piece(width, 768)
        for j in range(width // size):
            value = dot(left, right[:, j * size:(j + 1) * size], ((0,), (0,)))
            held[slot, :, j * size:(j + 1) * size] = (value * scale).astype(held.dtype)
        copy = pltpu.make_async_copy(held.at[slot], out.at[slot], sems.at[slot])
        copy.start()
        copies.append(copy)

    def columns(parts, size):
        if parts[0].shape[1] == size:
            return cat([p[...] for p in parts])
        return cat([p[:, mine(size)] for p in parts])

    for s in range(layers):
        left = columns(codes[s], own[0])
        for t in range(s, layers):
            right = cat([e[...] for e in errors[t]])
            leave(dec_held, dec_out, dec_sems, pair_slot(s, t, layers), left, right)
    for s in range(layers):
        leave(enc_held, enc_out, enc_sems, s, columns(inputs[s], own[1]), cat([g[...] for g in grads[s]]))
        total = sums[0][s, :, mine(own[0])]
        for more in sums[1:]:
            total = total + more[s, :, mine(own[0])]
        bias_out[pl.ds(s, 1)] = total * scale
    for copy in copies:
        copy.wait()


def all_grads(codes, errors, inputs, grads, sums, own, scale, layers):
    lists = (codes, errors, inputs, grads)
    dec = (layers * (layers + 1) // 2, own[0], errors[0][0].shape[1])
    enc = (layers, own[1], grads[0][0].shape[1])
    arrays = [pltpu.with_memory_space_constraint(p, pltpu.VMEM) for parts in lists for s in parts for p in s]
    arrays += [pltpu.with_memory_space_constraint(p, pltpu.VMEM) for p in sums]
    return pl.pallas_call(
        functools.partial(grads_body, layers, scale, [len(parts[0]) for parts in lists], own),
        name="grads",
        out_shape=[
            jax.ShapeDtypeStruct(dec, jnp.bfloat16),
            jax.ShapeDtypeStruct(enc, jnp.bfloat16),
            jax.ShapeDtypeStruct((layers, own[0]), jnp.float32),
        ],
        in_specs=inside(len(arrays)),
        out_specs=[pl.BlockSpec(memory_space=pltpu.HBM)] * 2 + inside(1),
        scratch_shapes=[
            pltpu.VMEM(dec, jnp.bfloat16),
            pltpu.VMEM(enc, jnp.bfloat16),
            pltpu.SemaphoreType.DMA((dec[0],)),
            pltpu.SemaphoreType.DMA((enc[0],)),
        ],
        compiler_params=pltpu.CompilerParams(vmem_limit_bytes=2 * (math.prod(dec) + math.prod(enc)) + 8 * MIB),
        cost_estimate=pl.CostEstimate(flops=0, bytes_accessed=0, transcendentals=0),
    )(*arrays)


def shards(acts_in, targets, enc_weight, enc_bias, dec_weight):
    layers, width, feats = enc_weight.shape
    n = acts_in.shape[0]
    feat, tok = lax.axis_size("feat"), lax.axis_size("tok")
    scale = 1.0 / math.sqrt(n * feat * tok)
    bias = enc_bias.reshape(layers, 1, feats)
    held = 2 * (math.prod(enc_weight.shape) + math.prod(dec_weight.shape))
    held += 4 * layers * n * feat * tok * (width + 2 * feats)
    resident = held <= 54 * MIB and n % 8 == 0
    line = [4 * k for k in range(1, feat // 4)]
    quart = n * (feat // 4)
    half = 2 * quart
    small = ((n, width), jnp.bfloat16)

    def swap_line(value):
        return [swap(value, "feat", bits) for bits in line]

    own_acts = [acts_in[:, s, :] for s in range(layers)]
    enc_held, dec_held = load([enc_weight, dec_weight]) if resident else (enc_weight, dec_weight)
    found = [swap_line(own_acts[0])]
    across_own = swap(cat(own_acts), "feat", 2)
    columns = []
    pre, codes = [[]], [[]]
    inputs = [[]]
    parts = []
    lines, crossed = [], []
    for s in range(layers):
        lists = [found[s]] + ([[own_acts[s + 1]]] if s + 1 < layers else [])
        made = join(lists, [dec_held] if s == 0 else (), resident)
        lines.append(made[0])
        crossed.append(swap(made[0], "feat", 2))
        if s + 1 < layers:
            found.append(swap_line(made[1]))
    last = ()
    for s in range(layers):
        there = lax.slice_in_dim(across_own, s * n, (s + 1) * n, axis=0)
        gate = found[s + 1] if s + 1 < layers else ()
        column = join([[own_acts[s], lines[s], there, crossed[s]]], gate, resident)[0]
        columns.append(column)
        inputs[0].append([column, swap(column, "feat", 1)])
        p, c = encode(s, inputs[0][s], enc_held, bias, resident, last)
        pre[0].append(p)
        codes[0].append(c)
        keep, give = decode(s, codes[0], dec_held, layers, resident, last)
        got = swap(give, "feat", 1)
        shapes = [((quart, width), jnp.float32), ((quart - n, width), jnp.bfloat16), small]
        low, rest, own = run(functools.partial(pair_kernel, n), "pair", [keep, got], shapes, (), resident)
        parts.append([low, swap(rest, "feat", 2), swap(own, "feat", 2)])
        last = (rest,)

    away = [[swap(columns[s], "tok", g) for s in range(layers)] for g in range(1, tok)]

    for s in range(layers):
        parts[s] += run(functools.partial(line_kernel, n), "line", parts[s][:2], [small] * len(line), (), resident)

    errors = [[] for _ in range(tok)]
    sent, found = [], []
    for t in range(layers):
        got = [swap(v, "feat", bits) for v, bits in zip(parts[t][3:], line)]
        target = targets[:, t, :]
        sent.append(
            run(
                functools.partial(error_kernel, n),
                "error",
                [parts[t][0], parts[t][2]] + got + [target],
                [small],
                found[t - 1] if t else (),
                resident,
            )[0]
        )
        found.append(swap_line(sent[t]))

    last = ()
    for g in range(1, tok):
        inputs.append([])
        pre.append([])
        codes.append([])
        for s in range(layers):
            column = join([[away[g - 1][s]]], sent, resident)[0]
            inputs[g].append([column, swap(column, "feat", 1)])
            p, c = encode(s, inputs[g][s], enc_held, bias, resident, last)
            pre[g].append(p)
            codes[g].append(c)
            last = (c,)

    wholes = []
    for t in range(layers):
        there = swap(sent[t], "feat", 2)
        column, rest = join([[sent[t]] + found[t], found[t]], (), resident)
        crossed = swap(rest, "feat", 2)
        others = [swap(column, "tok", g) for g in range(1, tok)]
        full, side = join([[column, there, crossed], [there, crossed]], others + list(last), resident)
        errors[0].append([full, swap(full, "feat", 1)])
        if t % 2 == 0:
            wholes.append([(o, swap(side, "tok", g)) for g, o in enumerate(others, 1)])
        else:
            wholes.append([(o, swap(o, "feat", 2)) for o in others])
    grads, sums = [], []
    last = ()
    for g in range(tok):
        if g:
            for t in range(layers):
                full = join([list(wholes[t][g - 1])], last, resident)[0]
                errors[g].append([full, swap(full, "feat", 1)])
        d, total = back(errors[g], pre[g], dec_held, layers, resident)
        grads.append(d)
        sums.append(total)
        last = (d[0],)

    def every(parts):
        return [
            [q for g in range(tok) for q in (parts[g][s] if isinstance(parts[g][s], list) else [parts[g][s]])]
            for s in range(layers)
        ]

    lists = [every(codes), every(errors), every(inputs), every(grads)]
    own = (feats // tok, width // tok)
    if resident:
        dec_out, enc_out, bias_out = all_grads(*lists, sums, own, scale, layers)
        return enc_out, bias_out, dec_out
    me = lax.axis_index("tok")
    index = me.reshape(1).astype(jnp.int32)
    dec_out = dec_grads(*lists[:2], index, own[0], scale, layers)
    enc_out = enc_grads(*lists[2:], index, own[1], scale, layers)
    total = sum(sums[1:], sums[0]).reshape(layers, feats) * scale
    return enc_out, lax.dynamic_slice_in_dim(total, me * own[0], own[0], axis=1), dec_out


def solution(mesh):
    return jax.shard_map(
        shards,
        mesh=mesh,
        in_specs=(
            P(("tok", "feat"), None, None),
            P(("tok", "feat"), None, None),
            P(None, None, "feat"),
            P(None, "feat"),
            P(None, "feat", None),
        ),
        out_specs=(
            P(None, "tok", "feat"),
            P(None, ("feat", "tok")),
            P(None, ("feat", "tok"), None),
        ),
        check_vma=False,
    )
```

time: 228 us -> 168 us (0.74)
  matrix products: 67.2 us -> 0 us
  Pallas kernels: 0 us -> 47.2 us
  waiting for transfers between devices: 89.4 us -> 72.8 us
  local copies, waits for them, and re-layouts: 13.2 us -> 1.83 us
  other arithmetic: 7.97 us -> 0.02 us
  starting transfers between devices: 48.8 us -> 44.6 us
    dot_general x18 -> x0, matrix products: 67.2 us -> none  [dot(): lax.dot_general(a, b, (dims, ((), ())), preferred_element_type=jnp.float32)]
    pallas_call x0 -> x28, Pallas kernels: none -> 47.2 us  [the longest x26 27.7 us: local(): pl.pallas_call(lambda *refs: kernel(*refs[skip:]), name=name, out_shape=[...]
    ppermute x43 -> x45, waiting for transfers between devices: 89.4 us -> 72.8 us  [swap(): lax.ppermute(value, axis, [(i, i ^ bits) for i in range(lax.axis_size(axi...]
    unnamed x25 -> x8, local copies, waits for them, and re-layouts: 8.13 us -> 0.07 us
    another operation x5 -> x0, other arithmetic: 6.78 us -> none  [the longest x3 6.6 us: shards(): return (jnp.stack(enc_out), jnp.stack(bias_out), jnp.stack(dec_out))]
    ppermute x43 -> x45, starting transfers between devices: 48.8 us -> 44.6 us  [swap(): lax.ppermute(value, axis, [(i, i ^ bits) for i in range(lax.axis_size(axi...]
  transfers between devices with their start and end apart: 43 -> 45, of which waited for: 22 -> 24; matrix products, arithmetic and copies ran while one was open for 25% -> 0% of each run, Pallas kernels for 0% -> 14%
where the time goes in v2:
time: 168 us
  waiting for transfers between devices  72.8 us (43%)
  Pallas kernels  47.2 us (28%)
  starting transfers between devices  44.6 us (27%)
  local copies, waits for them, and re-layouts  1.83 us (1%)
    ppermute x45, waiting for transfers between devices, swap(): lax.ppermute(value, axis, [(i, i ^ bits) for i in range(lax.axis_size(axi...  72.8 us
    ppermute x45, starting transfers between devices, swap(): lax.ppermute(value, axis, [(i, i ^ bits) for i in range(lax.axis_size(axi...  44.6 us
    pallas_call x26, Pallas kernels, local(): pl.pallas_call(lambda *refs: kernel(*refs[skip:]), name=name, out_shape=[...  27.7 us
    pallas_call x1, Pallas kernels, all_grads(): pl.pallas_call(functools.partial(grads_body, layers, scale, [len(parts[0]...  11.8 us
    pallas_call x1, Pallas kernels, load(): pl.pallas_call(lambda *refs: load_kernel(count, *refs[skip:]), name='load...  7.72 us
  transfers between devices with their start and end apart: 45, of which 24 were waited for; matrix products, arithmetic and copies ran while one was open for 0% of the time, Pallas kernels for 14%

profile of v2, /device:TPU:0, one launch (start us, length us, event | category | flops | bytes accessed | tf_op | source)
XLA Modules:
  0.0 167.6 jit_solution(7006140057692357911)
XLA Ops:
  2.1 3.0 %collective-permute-start.6 = (bf16[48,2304]{1,0:T(8,128)(2,1)S(1)}, bf16[48,2304]{1,0:T(8,128)(2,1)S(1)}, u32[]{:S(2)}, u32[]{:S(2)}) collective-permute-start(bf16[48,2304]{1,0:T(8,128)(2,1)S(1)} %pad_maximum_fusion), channel_id=1, source_target_pairs={{0,4},{2,6},{4,0},{6,2},{8,12},{10,14},{12,8},{14,10},{16,20},{18,... | collective-permute-start | bytes 663560 | tf_op jit(solution)/shard_map/ppermute | solution.py:19
  6.7 2.6 %collective-permute-start.1 = (bf16[24,2304]{1,0:T(8,128)(2,1)S(1)}, bf16[24,2304]{1,0:T(8,128)(2,1)S(1)}, u32[]{:S(2)}, u32[]{:S(2)}) collective-permute-start(bf16[24,2304]{1,0:T(8,128)(2,1)S(1)} %bitcast.17), channel_id=1, source_target_pairs={{0,16},{2,18},{4,20},{6,22},{8,24},{10,26},{12,28},{14,30},{16,0},... | collective-permute-start | bytes 331784 | tf_op jit(solution)/shard_map/ppermute | solution.py:19
  9.5 7.7 %load.1 = (bf16[2,2304,1024]{2,1,0:T(8,128)(2,1)S(1)}, bf16[3,1024,2304]{2,1,0:T(8,128)(2,1)S(1)}) custom-call(bf16[2,2304,1024]{2,1,0:T(8,128)(2,1)} %refs_0_.1, bf16[3,1024,2304]{2,1,0:T(8,128)(2,1)} %refs_1_.1), custom_call_target="tpu_custom_call" | custom-call | tf_op jit(solution)/shard_map/load/pallas_call | solution.py:107
  19.7 1.9 %collective-permute-start.4 = (bf16[24,2304]{1,0:T(8,128)(2,1)S(1)}, bf16[24,2304]{1,0:T(8,128)(2,1)S(1)}, u32[]{:S(2)}, u32[]{:S(2)}) collective-permute-start(bf16[24,2304]{1,0:T(8,128)(2,1)S(1)} %get-tuple-element.48), channel_id=1, source_target_pairs={{0,16},{2,18},{4,20},{6,22},{8,24},{10,26},{12,28},{14,30},{16,0},... | collective-permute-start | bytes 331784 | tf_op jit(solution)/shard_map/ppermute | solution.py:19
  23.7 6.1 %collective-permute-done.4.refs_1_ = bf16[24,2304]{1,0:T(8,128)(2,1)S(1)} collective-permute-done((bf16[24,2304]{1,0:T(8,128)(2,1)S(1)}, bf16[24,2304]{1,0:T(8,128)(2,1)S(1)}, u32[]{:S(2)}, u32[]{:S(2)}) %collective-permute-start.4) | collective-permute-done | bytes 110624 | tf_op jit(solution)/shard_map/ppermute | solution.py:19
  30.6 1.8 %collective-permute-done.8.refs_1_.refs_13_ = bf16[192,2304]{1,0:T(8,128)(2,1)S(1)} collective-permute-done((bf16[192,2304]{1,0:T(8,128)(2,1)S(1)}, bf16[192,2304]{1,0:T(8,128)(2,1)S(1)}, u32[]{:S(2)}, u32[]{:S(2)}) %collective-permute-start.8) | collective-permute-done | bytes 884768 | tf_op jit(solution)/shard_map/ppermute | solution.py:19
  32.4 2.0 %encode.4 = (f32[384,1024]{1,0:T(8,128)S(1)}, bf16[384,1024]{1,0:T(8,128)(2,1)S(1)}) custom-call(bf16[192,2304]{1,0:T(8,128)(2,1)S(1)} %join.13.refs_0_.refs_12_, bf16[192,2304]{1,0:T(8,128)(2,1)S(1)} %collective-permute-done.8.refs_1_.refs_13_, bf16[2,2304,1024]{2,1,0:T(8,128)(2,1)S(1)} %get-tuple-element.50.refs_2_.refs_3_, ...), custom_call_target="tpu_custom_call" | custom-call | tf_op jit(solution)/shard_map/encode/pallas_call | solution.py:57
  34.4 2.0 %decode.2 = (bf16[192,2304]{1,0:T(8,128)(2,1)S(1)}, bf16[192,2304]{1,0:T(8,128)(2,1)S(1)}) custom-call(bf16[384,1024]{1,0:T(8,128)(2,1)S(1)} %get-tuple-element.51.refs_0_.refs_1_, bf16[3,1024,2304]{2,1,0:T(8,128)(2,1)S(1)} %get-tuple-element.47.refs_0_.refs_1_.refs_3_.refs_4_.refs_6_.refs_7_.refs_8_), custom_call_target="tpu_custom_call" | custom-call | tf_op jit(solution)/shard_map/decode/pallas_call | solution.py:57
  36.7 3.6 %collective-permute-done.18.refs_3_ = bf16[72,2304]{1,0:T(8,128)(2,1)S(1)} collective-permute-done((bf16[72,2304]{1,0:T(8,128)(2,1)S(1)}, bf16[72,2304]{1,0:T(8,128)(2,1)S(1)}, u32[]{:S(2)}, u32[]{:S(2)}) %collective-permute-start.18) | collective-permute-done | bytes 331808 | tf_op jit(solution)/shard_map/ppermute | solution.py:19
  40.6 2.2 %collective-permute-done.19.refs_2_.refs_17_ = bf16[192,2304]{1,0:T(8,128)(2,1)S(1)} collective-permute-done((bf16[192,2304]{1,0:T(8,128)(2,1)S(1)}, bf16[192,2304]{1,0:T(8,128)(2,1)S(1)}, u32[]{:S(2)}, u32[]{:S(2)}) %collective-permute-start.19) | collective-permute-done | bytes 884768 | tf_op jit(solution)/shard_map/ppermute | solution.py:19
  42.8 2.0 %encode.5 = (f32[384,1024]{1,0:T(8,128)S(1)}, bf16[384,1024]{1,0:T(8,128)(2,1)S(1)}) custom-call(bf16[72,2304]{1,0:T(8,128)(2,1)S(1)} %get-tuple-element.56.refs_0_, bf16[192,2304]{1,0:T(8,128)(2,1)S(1)} %join.15.refs_1_.refs_16_, bf16[192,2304]{1,0:T(8,128)(2,1)S(1)} %collective-permute-done.19.refs_2_.refs_17_, ...), custom_call_target="tpu_custom_call" | custom-call | tf_op jit(solution)/shard_map/encode/pallas_call | solution.py:57
  44.9 3.9 %decode.3 = (bf16[192,2304]{1,0:T(8,128)(2,1)S(1)}, bf16[192,2304]{1,0:T(8,128)(2,1)S(1)}) custom-call(bf16[72,2304]{1,0:T(8,128)(2,1)S(1)} %get-tuple-element.56.refs_0_, bf16[384,1024]{1,0:T(8,128)(2,1)S(1)} %get-tuple-element.51.refs_0_.refs_1_, bf16[384,1024]{1,0:T(8,128)(2,1)S(1)} %get-tuple-element.60.refs_2_, ...), custom_call_target="tpu_custom_call" | custom-call | tf_op jit(solution)/shard_map/decode/pallas_call | solution.py:57
  51.0 8.6 %collective-permute-done.11.refs_1_ = bf16[72,2304]{1,0:T(8,128)(2,1)S(1)} collective-permute-done((bf16[72,2304]{1,0:T(8,128)(2,1)S(1)}, bf16[72,2304]{1,0:T(8,128)(2,1)S(1)}, u32[]{:S(2)}, u32[]{:S(2)}) %collective-permute-start.11) | collective-permute-done | bytes 331808 | tf_op jit(solution)/shard_map/ppermute | solution.py:19
  63.4 2.0 %collective-permute-start.13 = (bf16[24,2304]{1,0:T(8,128)(2,1)S(1)}, bf16[24,2304]{1,0:T(8,128)(2,1)S(1)}, u32[]{:S(2)}, u32[]{:S(2)}) collective-permute-start(bf16[24,2304]{1,0:T(8,128)(2,1)S(1)} %get-tuple-element.58), channel_id=1, source_target_pairs={{0,16},{2,18},{4,20},{6,22},{8,24},{10,26},{12,28},{14,30},{16,0},... | collective-permute-start | bytes 331784 | tf_op jit(solution)/shard_map/ppermute | solution.py:19
  67.2 6.0 %collective-permute-done.13.refs_3_ = bf16[24,2304]{1,0:T(8,128)(2,1)S(1)} collective-permute-done((bf16[24,2304]{1,0:T(8,128)(2,1)S(1)}, bf16[24,2304]{1,0:T(8,128)(2,1)S(1)}, u32[]{:S(2)}, u32[]{:S(2)}) %collective-permute-start.13) | collective-permute-done | bytes 110624 | tf_op jit(solution)/shard_map/ppermute | solution.py:19
  76.3 3.0 %collective-permute-done.15.refs_0_.refs_1_.refs_4_ = bf16[24,2304]{1,0:T(8,128)(2,1)S(1)} collective-permute-done((bf16[24,2304]{1,0:T(8,128)(2,1)S(1)}, bf16[24,2304]{1,0:T(8,128)(2,1)S(1)}, u32[]{:S(2)}, u32[]{:S(2)}) %collective-permute-start.15) | collective-permute-done | bytes 110624 | tf_op jit(solution)/shard_map/ppermute | solution.py:19
  79.3 1.9 %collective-permute-start.17 = (bf16[24,2304]{1,0:T(8,128)(2,1)S(1)}, bf16[24,2304]{1,0:T(8,128)(2,1)S(1)}, u32[]{:S(2)}, u32[]{:S(2)}) collective-permute-start(bf16[24,2304]{1,0:T(8,128)(2,1)S(1)} %error.2.refs_0_), channel_id=1, source_target_pairs={{0,24},{2,26},{4,28},{6,30},{8,16},{10,18},{12,20},{14,22},{16,8},... | collective-permute-start | bytes 331784 | tf_op jit(solution)/shard_map/ppermute | solution.py:19
  81.8 2.7 %collective-permute-done.16.refs_1_.refs_2_.refs_5_ = bf16[24,2304]{1,0:T(8,128)(2,1)S(1)} collective-permute-done((bf16[24,2304]{1,0:T(8,128)(2,1)S(1)}, bf16[24,2304]{1,0:T(8,128)(2,1)S(1)}, u32[]{:S(2)}, u32[]{:S(2)}) %collective-permute-start.16) | collective-permute-done | bytes 110624 | tf_op jit(solution)/shard_map/ppermute | solution.py:19
  85.9 2.8 %collective-permute-start.24 = (bf16[24,2304]{1,0:T(8,128)(2,1)S(1)}, bf16[24,2304]{1,0:T(8,128)(2,1)S(1)}, u32[]{:S(2)}, u32[]{:S(2)}) collective-permute-start(bf16[24,2304]{1,0:T(8,128)(2,1)S(1)} %get-tuple-element.67), channel_id=1, source_target_pairs={{0,16},{2,18},{4,20},{6,22},{8,24},{10,26},{12,28},{14,30},{16,0},... | collective-permute-start | bytes 331784 | tf_op jit(solution)/shard_map/ppermute | solution.py:19
  90.4 6.6 %collective-permute-done.24.refs_6_ = bf16[24,2304]{1,0:T(8,128)(2,1)S(1)} collective-permute-done((bf16[24,2304]{1,0:T(8,128)(2,1)S(1)}, bf16[24,2304]{1,0:T(8,128)(2,1)S(1)}, u32[]{:S(2)}, u32[]{:S(2)}) %collective-permute-start.24) | collective-permute-done | bytes 110624 | tf_op jit(solution)/shard_map/ppermute | solution.py:19
  97.3 3.4 %collective-permute-done.28.refs_2_ = bf16[192,2304]{1,0:T(8,128)(2,1)S(1)} collective-permute-done((bf16[192,2304]{1,0:T(8,128)(2,1)S(1)}, bf16[192,2304]{1,0:T(8,128)(2,1)S(1)}, u32[]{:S(2)}, u32[]{:S(2)}) %collective-permute-start.28) | collective-permute-done | bytes 884768 | tf_op jit(solution)/shard_map/ppermute | solution.py:19
  101.2 2.6 %collective-permute-start.35 = (bf16[24,2304]{1,0:T(8,128)(2,1)S(1)}, bf16[24,2304]{1,0:T(8,128)(2,1)S(1)}, u32[]{:S(2)}, u32[]{:S(2)}) collective-permute-start(bf16[24,2304]{1,0:T(8,128)(2,1)S(1)} %error.3.refs_1_.refs_0_), channel_id=1, source_target_pairs={{0,16},{2,18},{4,20},{6,22},{8,24},{10,26},{12,28},{14,30},{16,0},... | collective-permute-start | bytes 331784 | tf_op jit(solution)/shard_map/ppermute | solution.py:19
  105.3 3.3 %collective-permute-done.34.refs_1_.refs_4_ = bf16[24,2304]{1,0:T(8,128)(2,1)S(1)} collective-permute-done((bf16[24,2304]{1,0:T(8,128)(2,1)S(1)}, bf16[24,2304]{1,0:T(8,128)(2,1)S(1)}, u32[]{:S(2)}, u32[]{:S(2)}) %collective-permute-start.34) | collective-permute-done | bytes 110624 | tf_op jit(solution)/shard_map/ppermute | solution.py:19
  110.7 1.9 %collective-permute-done.36.refs_3_.refs_6_ = bf16[24,2304]{1,0:T(8,128)(2,1)S(1)} collective-permute-done((bf16[24,2304]{1,0:T(8,128)(2,1)S(1)}, bf16[24,2304]{1,0:T(8,128)(2,1)S(1)}, u32[]{:S(2)}, u32[]{:S(2)}) %collective-permute-start.36) | collective-permute-done | bytes 110624 | tf_op jit(solution)/shard_map/ppermute | solution.py:19
  116.8 2.2 %encode.6 = (f32[384,1024]{1,0:T(8,128)S(1)}, bf16[384,1024]{1,0:T(8,128)(2,1)S(1)}) custom-call(bf16[192,2304]{1,0:T(8,128)(2,1)S(1)} %join.16.refs_0_.refs_14_, bf16[192,2304]{1,0:T(8,128)(2,1)S(1)} %collective-permute-done.27.refs_1_.refs_15_, bf16[2,2304,1024]{2,1,0:T(8,128)(2,1)S(1)} %get-tuple-element.50.refs_2_.refs_3_, ...), custom_call_target="tpu_custom_call" | custom-call | tf_op jit(solution)/shard_map/encode/pallas_call | solution.py:57
  119.0 2.0 %encode.7 = (f32[384,1024]{1,0:T(8,128)S(1)}, bf16[384,1024]{1,0:T(8,128)(2,1)S(1)}) custom-call(bf16[384,1024]{1,0:T(8,128)(2,1)S(1)} %get-tuple-element.69.refs_0_.refs_1_, bf16[192,2304]{1,0:T(8,128)(2,1)S(1)} %join.17.refs_1_.refs_18_, bf16[192,2304]{1,0:T(8,128)(2,1)S(1)} %collective-permute-done.29.refs_2_.refs_19_, ...), custom_call_target="tpu_custom_call" | custom-call | tf_op jit(solution)/shard_map/encode/pallas_call | solution.py:57
  121.0 3.9 %collective-permute-done.32.refs_4_.refs_6_ = bf16[72,2304]{1,0:T(8,128)(2,1)S(1)} collective-permute-done((bf16[72,2304]{1,0:T(8,128)(2,1)S(1)}, bf16[72,2304]{1,0:T(8,128)(2,1)S(1)}, u32[]{:S(2)}, u32[]{:S(2)}) %collective-permute-start.32) | collective-permute-done | bytes 331808 | tf_op jit(solution)/shard_map/ppermute | solution.py:19
  125.1 7.6 %collective-permute-done.38.refs_3_.refs_5_ = bf16[24,2304]{1,0:T(8,128)(2,1)S(1)} collective-permute-done((bf16[24,2304]{1,0:T(8,128)(2,1)S(1)}, bf16[24,2304]{1,0:T(8,128)(2,1)S(1)}, u32[]{:S(2)}, u32[]{:S(2)}) %collective-permute-start.38) | collective-permute-done | bytes 110624 | tf_op jit(solution)/shard_map/ppermute | solution.py:19
  136.0 5.7 %back.2 = (bf16[384,1024]{1,0:T(8,128)(2,1)S(1)}, bf16[384,1024]{1,0:T(8,128)(2,1)S(1)}, f32[2,1,1024]{2,1,0:T(1,128)S(1)}) custom-call(bf16[192,2304]{1,0:T(8,128)(2,1)S(1)} %get-tuple-element.73.refs_0_.refs_4_, bf16[192,2304]{1,0:T(8,128)(2,1)S(1)} %collective-permute-done.33.refs_1_.refs_5_, bf16[192,2304]{1,0:T(8,128)(2,1)S(1)} %get-tuple-element.76.refs_2_.refs_8_, ...), custom_call_target="tpu_custom_call" | custom-call | tf_op jit(solution)/shard_map/back/pallas_call | solution.py:57
  141.7 4.4 %collective-permute-done.41.refs_2_ = bf16[96,2304]{1,0:T(8,128)(2,1)S(1)} collective-permute-done((bf16[96,2304]{1,0:T(8,128)(2,1)S(1)}, bf16[96,2304]{1,0:T(8,128)(2,1)S(1)}, u32[]{:S(2)}, u32[]{:S(2)}) %collective-permute-start.41) | collective-permute-done | bytes 442400 | tf_op jit(solution)/shard_map/ppermute | solution.py:19
  150.0 5.7 %back.3 = (bf16[384,1024]{1,0:T(8,128)(2,1)S(1)}, bf16[384,1024]{1,0:T(8,128)(2,1)S(1)}, f32[2,1,1024]{2,1,0:T(1,128)S(1)}) custom-call(bf16[192,2304]{1,0:T(8,128)(2,1)S(1)} %join.22.refs_0_.refs_6_, bf16[192,2304]{1,0:T(8,128)(2,1)S(1)} %collective-permute-done.42.refs_1_.refs_7_, bf16[192,2304]{1,0:T(8,128)(2,1)S(1)} %join.23.refs_2_.refs_10_, ...), custom_call_target="tpu_custom_call" | custom-call | tf_op jit(solution)/shard_map/back/pallas_call | solution.py:57
  155.7 11.8 %grads.1 = (bf16[3,512,2304]{2,1,0:T(8,128)(2,1)}, bf16[2,1152,1024]{2,1,0:T(8,128)(2,1)}, f32[2,512]{1,0:T(2,128)}) custom-call(bf16[384,1024]{1,0:T(8,128)(2,1)S(1)} %get-tuple-element.51.refs_0_.refs_1_, bf16[384,1024]{1,0:T(8,128)(2,1)S(1)} %get-tuple-element.69.refs_0_.refs_1_, bf16[384,1024]{1,0:T(8,128)(2,1)S(1)} %get-tuple-element.60.refs_2_, ...), custom_call_target="tpu_custom_call" | custom-call | tf_op jit(solution)/shard_map/grads/pallas_call | solution.py:383
  (99 shorter events, 39.5 us)
Async XLA Ops:
  2.1 20.7 %collective-permute-start.6 = (bf16[48,2304]{1,0:T(8,128)(2,1)S(1)}, bf16[48,2304]{1,0:T(8,128)(2,1)S(1)}, u32[]{:S(2)}, u32[]{:S(2)}) collective-permute-start(bf16[48,2304]{1,0:T(8,128)(2,1)S(1)} %pad_maximum_fusion), channel_id=1, source_target_pairs={{0,4},{2,6},{4,0},{6,2},{8,12},{10,14},{12,8},{14,10},{16,20},{18,... | collective-permute-start | bytes 663560 | tf_op jit(solution)/shard_map/ppermute | solution.py:19
  5.1 12.1 %collective-permute-start = (bf16[24,2304]{1,0:T(8,128)(2,1)S(1)}, bf16[24,2304]{1,0:T(8,128)(2,1)S(1)}, u32[]{:S(2)}, u32[]{:S(2)}) collective-permute-start(bf16[24,2304]{1,0:T(8,128)(2,1)S(1)} %bitcast.16), channel_id=1, source_target_pairs={{0,8},{2,10},{4,12},{6,14},{8,0},{10,2},{12,4},{14,6},{16,24},{18,... | collective-permute-start | bytes 331784 | tf_op jit(solution)/shard_map/ppermute | solution.py:19
  6.7 11.1 %collective-permute-start.1 = (bf16[24,2304]{1,0:T(8,128)(2,1)S(1)}, bf16[24,2304]{1,0:T(8,128)(2,1)S(1)}, u32[]{:S(2)}, u32[]{:S(2)}) collective-permute-start(bf16[24,2304]{1,0:T(8,128)(2,1)S(1)} %bitcast.17), channel_id=1, source_target_pairs={{0,16},{2,18},{4,20},{6,22},{8,24},{10,26},{12,28},{14,30},{16,0},... | collective-permute-start | bytes 331784 | tf_op jit(solution)/shard_map/ppermute | solution.py:19
  9.3 8.5 %collective-permute-start.2 = (bf16[24,2304]{1,0:T(8,128)(2,1)S(1)}, bf16[24,2304]{1,0:T(8,128)(2,1)S(1)}, u32[]{:S(2)}, u32[]{:S(2)}) collective-permute-start(bf16[24,2304]{1,0:T(8,128)(2,1)S(1)} %bitcast.18), channel_id=1, source_target_pairs={{0,24},{2,26},{4,28},{6,30},{8,16},{10,18},{12,20},{14,22},{16,8},... | collective-permute-start | bytes 331784 | tf_op jit(solution)/shard_map/ppermute | solution.py:19
  19.7 10.1 %collective-permute-start.4 = (bf16[24,2304]{1,0:T(8,128)(2,1)S(1)}, bf16[24,2304]{1,0:T(8,128)(2,1)S(1)}, u32[]{:S(2)}, u32[]{:S(2)}) collective-permute-start(bf16[24,2304]{1,0:T(8,128)(2,1)S(1)} %get-tuple-element.48), channel_id=1, source_target_pairs={{0,16},{2,18},{4,20},{6,22},{8,24},{10,26},{12,28},{14,30},{16,0},... | collective-permute-start | bytes 331784 | tf_op jit(solution)/shard_map/ppermute | solution.py:19
  21.6 8.2 %collective-permute-start.5 = (bf16[24,2304]{1,0:T(8,128)(2,1)S(1)}, bf16[24,2304]{1,0:T(8,128)(2,1)S(1)}, u32[]{:S(2)}, u32[]{:S(2)}) collective-permute-start(bf16[24,2304]{1,0:T(8,128)(2,1)S(1)} %get-tuple-element.48), channel_id=1, source_target_pairs={{0,24},{2,26},{4,28},{6,30},{8,16},{10,18},{12,20},{14,22},{16,8},... | collective-permute-start | bytes 331784 | tf_op jit(solution)/shard_map/ppermute | solution.py:19
  22.3 7.5 %collective-permute-start.7 = (bf16[72,2304]{1,0:T(8,128)(2,1)S(1)}, bf16[72,2304]{1,0:T(8,128)(2,1)S(1)}, u32[]{:S(2)}, u32[]{:S(2)}) collective-permute-start(bf16[72,2304]{1,0:T(8,128)(2,1)S(1)} %get-tuple-element.49.refs_4_), channel_id=1, source_target_pairs={{0,4},{2,6},{4,0},{6,2},{8,12},{10,14},{12,8},{14,10},{16,20},{18,... | collective-permute-start | bytes 995336 | tf_op jit(solution)/shard_map/ppermute | solution.py:19
  30.0 10.3 %collective-permute-start.18 = (bf16[72,2304]{1,0:T(8,128)(2,1)S(1)}, bf16[72,2304]{1,0:T(8,128)(2,1)S(1)}, u32[]{:S(2)}, u32[]{:S(2)}) collective-permute-start(bf16[72,2304]{1,0:T(8,128)(2,1)S(1)} %join.14.refs_1_), channel_id=1, source_target_pairs={{0,4},{2,6},{4,0},{6,2},{8,12},{10,14},{12,8},{14,10},{16,20},{18,... | collective-permute-start | bytes 995336 | tf_op jit(solution)/shard_map/ppermute | solution.py:19
  48.8 14.7 %collective-permute-start.20 = (bf16[192,2304]{1,0:T(8,128)(2,1)S(1)}, bf16[192,2304]{1,0:T(8,128)(2,1)S(1)}, u32[]{:S(2)}, u32[]{:S(2)}) collective-permute-start(bf16[192,2304]{1,0:T(8,128)(2,1)S(1)} %get-tuple-element.62), channel_id=1, source_target_pairs={{0,2},{2,0},{4,6},{6,4},{8,10},{10,8},{12,14},{14,12},{16,18},{18,... | collective-permute-start | bytes 2654216 | tf_op jit(solution)/shard_map/ppermute | solution.py:19
  49.0 10.6 %collective-permute-start.11 = (bf16[72,2304]{1,0:T(8,128)(2,1)S(1)}, bf16[72,2304]{1,0:T(8,128)(2,1)S(1)}, u32[]{:S(2)}, u32[]{:S(2)}) collective-permute-start(bf16[72,2304]{1,0:T(8,128)(2,1)S(1)} %get-tuple-element.56.refs_0_), channel_id=1, source_target_pairs={{0,4},{2,6},{4,0},{6,2},{8,12},{10,14},{12,8},{14,10},{16,20},{18,... | collective-permute-start | bytes 995336 | tf_op jit(solution)/shard_map/ppermute | solution.py:19
  49.4 16.2 %collective-permute-start.10 = (bf16[24,2304]{1,0:T(8,128)(2,1)S(1)}, bf16[24,2304]{1,0:T(8,128)(2,1)S(1)}, u32[]{:S(2)}, u32[]{:S(2)}) collective-permute-start(bf16[24,2304]{1,0:T(8,128)(2,1)S(1)} %get-tuple-element.55), channel_id=1, source_target_pairs={{0,4},{2,6},{4,0},{6,2},{8,12},{10,14},{12,8},{14,10},{16,20},{18,... | collective-permute-start | bytes 331784 | tf_op jit(solution)/shard_map/ppermute | solution.py:19
  61.4 35.7 %collective-permute-start.26 = (bf16[192,2304]{1,0:T(8,128)(2,1)S(1)}, bf16[192,2304]{1,0:T(8,128)(2,1)S(1)}, u32[]{:S(2)}, u32[]{:S(2)}) collective-permute-start(bf16[192,2304]{1,0:T(8,128)(2,1)S(1)} %join.13.refs_0_.refs_12_), channel_id=1, source_target_pairs={{0,1},{1,0},{2,3},{3,2},{4,5},{5,4},{6,7},{7,6},{8,9},{9,8},{10,11... | collective-permute-start | bytes 2654216 | tf_op jit(solution)/shard_map/ppermute | solution.py:19
  62.9 37.7 %collective-permute-start.28 = (bf16[192,2304]{1,0:T(8,128)(2,1)S(1)}, bf16[192,2304]{1,0:T(8,128)(2,1)S(1)}, u32[]{:S(2)}, u32[]{:S(2)}) collective-permute-start(bf16[192,2304]{1,0:T(8,128)(2,1)S(1)} %join.15.refs_1_.refs_16_), channel_id=1, source_target_pairs={{0,1},{1,0},{2,3},{3,2},{4,5},{5,4},{6,7},{7,6},{8,9},{9,8},{10,11... | collective-permute-start | bytes 2654216 | tf_op jit(solution)/shard_map/ppermute | solution.py:19
  63.4 9.7 %collective-permute-start.13 = (bf16[24,2304]{1,0:T(8,128)(2,1)S(1)}, bf16[24,2304]{1,0:T(8,128)(2,1)S(1)}, u32[]{:S(2)}, u32[]{:S(2)}) collective-permute-start(bf16[24,2304]{1,0:T(8,128)(2,1)S(1)} %get-tuple-element.58), channel_id=1, source_target_pairs={{0,16},{2,18},{4,20},{6,22},{8,24},{10,26},{12,28},{14,30},{16,0},... | collective-permute-start | bytes 331784 | tf_op jit(solution)/shard_map/ppermute | solution.py:19
  65.7 7.5 %collective-permute-start.14 = (bf16[24,2304]{1,0:T(8,128)(2,1)S(1)}, bf16[24,2304]{1,0:T(8,128)(2,1)S(1)}, u32[]{:S(2)}, u32[]{:S(2)}) collective-permute-start(bf16[24,2304]{1,0:T(8,128)(2,1)S(1)} %get-tuple-element.59), channel_id=1, source_target_pairs={{0,24},{2,26},{4,28},{6,30},{8,16},{10,18},{12,20},{14,22},{16,8},... | collective-permute-start | bytes 331784 | tf_op jit(solution)/shard_map/ppermute | solution.py:19
  66.4 14.8 %collective-permute-start.22 = (bf16[72,2304]{1,0:T(8,128)(2,1)S(1)}, bf16[72,2304]{1,0:T(8,128)(2,1)S(1)}, u32[]{:S(2)}, u32[]{:S(2)}) collective-permute-start(bf16[72,2304]{1,0:T(8,128)(2,1)S(1)} %get-tuple-element.65), channel_id=1, source_target_pairs={{0,4},{2,6},{4,0},{6,2},{8,12},{10,14},{12,8},{14,10},{16,20},{18,... | collective-permute-start | bytes 995336 | tf_op jit(solution)/shard_map/ppermute | solution.py:19
  75.1 9.4 %collective-permute-start.16 = (bf16[24,2304]{1,0:T(8,128)(2,1)S(1)}, bf16[24,2304]{1,0:T(8,128)(2,1)S(1)}, u32[]{:S(2)}, u32[]{:S(2)}) collective-permute-start(bf16[24,2304]{1,0:T(8,128)(2,1)S(1)} %error.2.refs_0_), channel_id=1, source_target_pairs={{0,16},{2,18},{4,20},{6,22},{8,24},{10,26},{12,28},{14,30},{16,0},... | collective-permute-start | bytes 331784 | tf_op jit(solution)/shard_map/ppermute | solution.py:19
  85.9 11.1 %collective-permute-start.24 = (bf16[24,2304]{1,0:T(8,128)(2,1)S(1)}, bf16[24,2304]{1,0:T(8,128)(2,1)S(1)}, u32[]{:S(2)}, u32[]{:S(2)}) collective-permute-start(bf16[24,2304]{1,0:T(8,128)(2,1)S(1)} %get-tuple-element.67), channel_id=1, source_target_pairs={{0,16},{2,18},{4,20},{6,22},{8,24},{10,26},{12,28},{14,30},{16,0},... | collective-permute-start | bytes 331784 | tf_op jit(solution)/shard_map/ppermute | solution.py:19
  88.7 8.3 %collective-permute-start.25 = (bf16[24,2304]{1,0:T(8,128)(2,1)S(1)}, bf16[24,2304]{1,0:T(8,128)(2,1)S(1)}, u32[]{:S(2)}, u32[]{:S(2)}) collective-permute-start(bf16[24,2304]{1,0:T(8,128)(2,1)S(1)} %get-tuple-element.68), channel_id=1, source_target_pairs={{0,24},{2,26},{4,28},{6,30},{8,16},{10,18},{12,20},{14,22},{16,8},... | collective-permute-start | bytes 331784 | tf_op jit(solution)/shard_map/ppermute | solution.py:19
  97.2 17.6 %collective-permute-start.27 = (bf16[192,2304]{1,0:T(8,128)(2,1)S(1)}, bf16[192,2304]{1,0:T(8,128)(2,1)S(1)}, u32[]{:S(2)}, u32[]{:S(2)}) collective-permute-start(bf16[192,2304]{1,0:T(8,128)(2,1)S(1)} %join.16.refs_0_.refs_14_), channel_id=1, source_target_pairs={{0,2},{2,0},{4,6},{6,4},{8,10},{10,8},{12,14},{14,12},{16,18},{18,... | collective-permute-start | bytes 2654216 | tf_op jit(solution)/shard_map/ppermute | solution.py:19
  100.7 15.5 %collective-permute-start.29 = (bf16[192,2304]{1,0:T(8,128)(2,1)S(1)}, bf16[192,2304]{1,0:T(8,128)(2,1)S(1)}, u32[]{:S(2)}, u32[]{:S(2)}) collective-permute-start(bf16[192,2304]{1,0:T(8,128)(2,1)S(1)} %join.17.refs_1_.refs_18_), channel_id=1, source_target_pairs={{0,2},{2,0},{4,6},{6,4},{8,10},{10,8},{12,14},{14,12},{16,18},{18,... | collective-permute-start | bytes 2654216 | tf_op jit(solution)/shard_map/ppermute | solution.py:19
  100.8 7.8 %collective-permute-start.34 = (bf16[24,2304]{1,0:T(8,128)(2,1)S(1)}, bf16[24,2304]{1,0:T(8,128)(2,1)S(1)}, u32[]{:S(2)}, u32[]{:S(2)}) collective-permute-start(bf16[24,2304]{1,0:T(8,128)(2,1)S(1)} %error.3.refs_1_.refs_0_), channel_id=1, source_target_pairs={{0,8},{2,10},{4,12},{6,14},{8,0},{10,2},{12,4},{14,6},{16,24},{18,... | collective-permute-start | bytes 331784 | tf_op jit(solution)/shard_map/ppermute | solution.py:19
  101.2 7.9 %collective-permute-start.35 = (bf16[24,2304]{1,0:T(8,128)(2,1)S(1)}, bf16[24,2304]{1,0:T(8,128)(2,1)S(1)}, u32[]{:S(2)}, u32[]{:S(2)}) collective-permute-start(bf16[24,2304]{1,0:T(8,128)(2,1)S(1)} %error.3.refs_1_.refs_0_), channel_id=1, source_target_pairs={{0,16},{2,18},{4,20},{6,22},{8,24},{10,26},{12,28},{14,30},{16,0},... | collective-permute-start | bytes 331784 | tf_op jit(solution)/shard_map/ppermute | solution.py:19
  103.8 8.8 %collective-permute-start.36 = (bf16[24,2304]{1,0:T(8,128)(2,1)S(1)}, bf16[24,2304]{1,0:T(8,128)(2,1)S(1)}, u32[]{:S(2)}, u32[]{:S(2)}) collective-permute-start(bf16[24,2304]{1,0:T(8,128)(2,1)S(1)} %error.3.refs_1_.refs_0_), channel_id=1, source_target_pairs={{0,24},{2,26},{4,28},{6,30},{8,16},{10,18},{12,20},{14,22},{16,8},... | collective-permute-start | bytes 331784 | tf_op jit(solution)/shard_map/ppermute | solution.py:19
  109.1 15.9 %collective-permute-start.30 = (bf16[96,2304]{1,0:T(8,128)(2,1)S(1)}, bf16[96,2304]{1,0:T(8,128)(2,1)S(1)}, u32[]{:S(2)}, u32[]{:S(2)}) collective-permute-start(bf16[96,2304]{1,0:T(8,128)(2,1)S(1)} %get-tuple-element.71.refs_2_), channel_id=1, source_target_pairs={{0,1},{1,0},{2,3},{3,2},{4,5},{5,4},{6,7},{7,6},{8,9},{9,8},{10,11... | collective-permute-start | bytes 1327112 | tf_op jit(solution)/shard_map/ppermute | solution.py:19
  112.6 20.1 %collective-permute-start.37 = (bf16[96,2304]{1,0:T(8,128)(2,1)S(1)}, bf16[96,2304]{1,0:T(8,128)(2,1)S(1)}, u32[]{:S(2)}, u32[]{:S(2)}) collective-permute-start(bf16[96,2304]{1,0:T(8,128)(2,1)S(1)} %get-tuple-element.74.refs_2_), channel_id=1, source_target_pairs={{0,1},{1,0},{2,3},{3,2},{4,5},{5,4},{6,7},{7,6},{8,9},{9,8},{10,11... | collective-permute-start | bytes 1327112 | tf_op jit(solution)/shard_map/ppermute | solution.py:19
  114.2 10.7 %collective-permute-start.32 = (bf16[72,2304]{1,0:T(8,128)(2,1)S(1)}, bf16[72,2304]{1,0:T(8,128)(2,1)S(1)}, u32[]{:S(2)}, u32[]{:S(2)}) collective-permute-start(bf16[72,2304]{1,0:T(8,128)(2,1)S(1)} %get-tuple-element.72), channel_id=1, source_target_pairs={{0,4},{2,6},{4,0},{6,2},{8,12},{10,14},{12,8},{14,10},{16,20},{18,... | collective-permute-start | bytes 995336 | tf_op jit(solution)/shard_map/ppermute | solution.py:19
  114.7 18.0 %collective-permute-start.39 = (bf16[72,2304]{1,0:T(8,128)(2,1)S(1)}, bf16[72,2304]{1,0:T(8,128)(2,1)S(1)}, u32[]{:S(2)}, u32[]{:S(2)}) collective-permute-start(bf16[72,2304]{1,0:T(8,128)(2,1)S(1)} %get-tuple-element.75), channel_id=1, source_target_pairs={{0,4},{2,6},{4,0},{6,2},{8,12},{10,14},{12,8},{14,10},{16,20},{18,... | collective-permute-start | bytes 995336 | tf_op jit(solution)/shard_map/ppermute | solution.py:19
  116.2 16.5 %collective-permute-start.38 = (bf16[24,2304]{1,0:T(8,128)(2,1)S(1)}, bf16[24,2304]{1,0:T(8,128)(2,1)S(1)}, u32[]{:S(2)}, u32[]{:S(2)}) collective-permute-start(bf16[24,2304]{1,0:T(8,128)(2,1)S(1)} %error.3.refs_1_.refs_0_), channel_id=1, source_target_pairs={{0,4},{2,6},{4,0},{6,2},{8,12},{10,14},{12,8},{14,10},{16,20},{18,... | collective-permute-start | bytes 331784 | tf_op jit(solution)/shard_map/ppermute | solution.py:19
  125.0 9.6 %collective-permute-start.33 = (bf16[192,2304]{1,0:T(8,128)(2,1)S(1)}, bf16[192,2304]{1,0:T(8,128)(2,1)S(1)}, u32[]{:S(2)}, u32[]{:S(2)}) collective-permute-start(bf16[192,2304]{1,0:T(8,128)(2,1)S(1)} %get-tuple-element.73.refs_0_.refs_4_), channel_id=1, source_target_pairs={{0,2},{2,0},{4,6},{6,4},{8,10},{10,8},{12,14},{14,12},{16,18},{18,... | collective-permute-start | bytes 2654216 | tf_op jit(solution)/shard_map/ppermute | solution.py:19
  133.6 12.6 %collective-permute-start.41 = (bf16[96,2304]{1,0:T(8,128)(2,1)S(1)}, bf16[96,2304]{1,0:T(8,128)(2,1)S(1)}, u32[]{:S(2)}, u32[]{:S(2)}) collective-permute-start(bf16[96,2304]{1,0:T(8,128)(2,1)S(1)} %get-tuple-element.80), channel_id=1, source_target_pairs={{0,1},{1,0},{2,3},{3,2},{4,5},{5,4},{6,7},{7,6},{8,9},{9,8},{10,11... | collective-permute-start | bytes 1327112 | tf_op jit(solution)/shard_map/ppermute | solution.py:19
  134.1 12.3 %collective-permute-start.43 = (bf16[96,2304]{1,0:T(8,128)(2,1)S(1)}, bf16[96,2304]{1,0:T(8,128)(2,1)S(1)}, u32[]{:S(2)}, u32[]{:S(2)}) collective-permute-start(bf16[96,2304]{1,0:T(8,128)(2,1)S(1)} %collective-permute-done.37.refs_0_.refs_1_), channel_id=1, source_target_pairs={{0,4},{2,6},{4,0},{6,2},{8,12},{10,14},{12,8},{14,10},{16,20},{18,... | collective-permute-start | bytes 1327112 | tf_op jit(solution)/shard_map/ppermute | solution.py:19
  (15 other events, 96.4 us)

commit v3 on v2

v3 whole, which is shorter than its diff:
```python
import functools
import math

import jax
import jax.numpy as jnp
from jax import lax
from jax.experimental import pallas as pl
from jax.experimental.pallas import tpu as pltpu
from jax.sharding import PartitionSpec as P

MIB = 1 << 20


def pair_slot(source, target, layers):
    return sum((layers - k for k in range(source))) + (target - source)


def swap(value, axis, bits):
    return lax.ppermute(value, axis, [(i, i ^ bits) for i in range(lax.axis_size(axis))])


def cat(parts):
    return parts[0] if len(parts) == 1 else jnp.concatenate(parts, axis=0)


def dot(a, b, dims):
    return lax.dot_general(a, b, (dims, ((), ())), preferred_element_type=jnp.float32)


def piece(size, most):
    for c in range(most - most % 128, 0, -128):
        if size % c == 0:
            return c
    return size


def share(parts, own, me):
    if own % 128:
        return [(lax.dynamic_slice_in_dim(p, me[0] * own, own, axis=1), (p.shape[0], own), lambda j, me: (0, 0)) for p in parts]
    return [(p, (p.shape[0], own), lambda j, me: (0, me[0])) for p in parts]


def view(ref, block, index):
    at = []
    for size, most, i in zip(block, ref.shape, index):
        start = i * size
        at.append(slice(None) if size == most else pl.ds(start if isinstance(start, int) else pl.multiple_of(start, size), size))
    return ref.at[tuple(at)]


def inside(count):
    return [pl.BlockSpec(memory_space=pltpu.VMEM)] * count


def local(kernel, name, arrays, outs, after=(), flops=0):
    skip = len(after)
    return pl.pallas_call(
        lambda *refs: kernel(*refs[skip:]),
        name=name,
        out_shape=[pltpu.VMEM(s, d) for s, d in outs],
        in_specs=[pl.BlockSpec(memory_space=pl.ANY)] * skip
        + inside(len(arrays)),
        out_specs=inside(len(outs)),
        compiler_params=pltpu.CompilerParams(vmem_limit_bytes=4 * MIB),
        cost_estimate=pl.CostEstimate(flops=flops, bytes_accessed=0, transcendentals=0),
    )(*after, *[pltpu.with_memory_space_constraint(a, pltpu.VMEM) for a in arrays])


def steps_body(kernel, steps, ins, outs, *refs):
    for j in range(steps):
        kernel(*[view(r, b, m(j)) for r, (b, m) in zip(refs, ins + outs)])


def call(kernel, name, steps, ins, outs, flops, scalars=(), resident=False, after=()):
    if resident:
        body = functools.partial(steps_body, kernel, steps, [i[1:] for i in ins], [o[2:] for o in outs])
        return local(body, name, [i[0] for i in ins], [o[:2] for o in outs], after, flops)
    moved = sum(math.prod(a.shape) * a.dtype.itemsize for a, _, _ in ins)
    moved += sum(math.prod(s) * jnp.dtype(d).itemsize for s, d, _, _ in outs)
    return pl.pallas_call(
        kernel,
        name=name,
        out_shape=[jax.ShapeDtypeStruct(s, d) for s, d, _, _ in outs],
        grid_spec=pltpu.PrefetchScalarGridSpec(
            num_scalar_prefetch=len(scalars),
            grid=(steps,),
            in_specs=[pl.BlockSpec(b, m) for _, b, m in ins],
            out_specs=[pl.BlockSpec(b, m) for _, _, b, m in outs],
        ),
        compiler_params=pltpu.CompilerParams(vmem_limit_bytes=32 * MIB),
        cost_estimate=pl.CostEstimate(flops=flops, bytes_accessed=moved, transcendentals=0),
    )(*scalars, *[i[0] for i in ins])


def load_kernel(count, *refs):
    sources, places, sems = refs[:count], refs[count:2 * count], refs[2 * count]
    copies = [pltpu.make_async_copy(sources[i], places[i], sems.at[i]) for i in range(count)]
    for copy in copies:
        copy.start()
    for copy in copies:
        copy.wait()


def load(arrays, after=()):
    count, skip = len(arrays), len(after)
    return pl.pallas_call(
        lambda *refs: load_kernel(count, *refs[skip:]),
        name="load",
        out_shape=[pltpu.VMEM(a.shape, a.dtype) for a in arrays],
        in_specs=[pl.BlockSpec(memory_space=pl.ANY)] * skip + [pl.BlockSpec(memory_space=pltpu.HBM)] * count,
        out_specs=inside(count),
        scratch_shapes=[pltpu.SemaphoreType.DMA((count,))],
        compiler_params=pltpu.CompilerParams(vmem_limit_bytes=MIB),
        cost_estimate=pl.CostEstimate(flops=0, bytes_accessed=0, transcendentals=0),
    )(*after, *[pltpu.with_memory_space_constraint(a, pltpu.HBM) for a in arrays])


def wide(ref):
    return ref[...].astype(jnp.float32)


def join_kernel(groups, *refs):
    ins, outs = refs[:sum(len(g) for g in groups)], refs[sum(len(g) for g in groups):]
    for group, out in zip(groups, outs):
        values = [wide(r)[start:start + count] for r, (start, count) in zip(ins, group)]
        out[...] = cat(values).astype(out.dtype)
        ins = ins[len(group):]


def join(lists, after=()):
    lists = [[p if isinstance(p, tuple) else (p, 0, p.shape[0]) for p in parts] for parts in lists]
    outs = [((sum(c for _, _, c in parts), parts[0][0].shape[1]), parts[0][0].dtype) for parts in lists]
    kernel = functools.partial(join_kernel, [[p[1:] for p in parts] for parts in lists])
    return local(kernel, "join", [p[0] for parts in lists for p in parts], outs, after)


def pair_kernel(keep, *refs):
    got, (low, high) = refs[:-2], refs[-2:]
    part = wide(keep) + cat([wide(g) for g in got])
    half = part.shape[0] // 2
    low[...] = part[:half]
    high[...] = part[half:].astype(high.dtype)


def line_kernel(n, low, got, *outs):
    part = low[...] + wide(got)
    for k, out in enumerate(outs):
        out[...] = part[(k + 1) * n:(k + 2) * n].astype(out.dtype)


def open_kernel(n, count, low, got, *refs):
    line_kernel(n, low, got, *refs[-2 - count:-2])
    pair_kernel(*refs[:-2 - count], *refs[-2:])


def error_kernel(n, low, got, *refs):
    refs, target, out = refs[:-2], refs[-2], refs[-1]
    value = low[:n] + wide(got)[:n]
    for r in refs:
        value = value + wide(r)[:n]
    out[...] = (value - wide(target)).astype(out.dtype)


def turn_kernel(n, count, low, got, *refs):
    ends, (target, next_low, next_got), outs = refs[:count], refs[count:count + 3], refs[count + 3:]
    error_kernel(n, low, got, *ends, target, outs[-1])
    part = next_low[...] + wide(next_got)
    for k, out in enumerate(outs[:-1]):
        out[...] = cat([part[(k + 1) * n:(k + 2) * n], wide(outs[-1])]).astype(out.dtype)


def encode_kernel(parts, *refs):
    x = cat([r[...] for r in refs[:parts]])
    w, b, pre, code = refs[parts:]
    value = jnp.maximum(dot(x, w[0], ((1,), (0,))) + b[0], 0.0)
    pre[...] = value
    code[...] = (0.5 * value * value).astype(code.dtype)


def encode(source, parts, weight, bias, resident, after=()):
    _, width, feats = weight.shape
    m = sum(p.shape[0] for p in parts)
    c = piece(feats, 256)
    ins = [(p, p.shape, lambda j: (0, 0)) for p in parts]
    ins.append((weight, (1, width, c), lambda j: (source, 0, j)))
    ins.append((bias, (1, 1, c), lambda j: (source, 0, j)))
    outs = [((m, feats), d, (m, c), lambda j: (0, j)) for d in (jnp.float32, jnp.bfloat16)]
    return call(
        functools.partial(encode_kernel, len(parts)), "encode", feats // c, ins, outs, 2 * m * width * feats, (), resident, after
    )


def decode_kernel(sources, early, last, *refs):
    total = refs[2 * sources][...] if early else None
    for s in range(sources):
        term = dot(refs[s][...], refs[sources + s][0], ((1,), (0,)))
        total = term if total is None else total + term
    if not last:
        refs[-1][...] = total
        return
    keep, *gives = refs[2 * sources + early:]
    half = keep.shape[0]
    keep[...] = total[:half].astype(keep.dtype)
    size = half // len(gives)
    for k, give in enumerate(gives):
        give[...] = total[half + k * size:half + (k + 1) * size].astype(give.dtype)


def decode(target, sources, codes, weight, layers, early, last, resident, after=(), pieces=1):
    _, feats, width = weight.shape
    m = codes[0].shape[0]
    c = piece(width, 768)
    ins = [(codes[s], codes[s].shape, lambda j: (0, 0)) for s in sources]
    for s in sources:
        slot = pair_slot(s, target, layers)
        ins.append((weight, (1, feats, c), lambda j, slot=slot: (slot, 0, j)))
    ins += [(e, (m, c), lambda j: (0, j)) for e in early]
    outs = [((r, width), jnp.bfloat16, (r, c), lambda j: (0, j)) for r in [m // 2] + [m // 2 // pieces] * pieces]
    if not last:
        outs = [((m, width), jnp.float32, (m, c), lambda j: (0, j))]
    return call(
        functools.partial(decode_kernel, len(sources), len(early), last),
        "decode",
        width // c,
        ins,
        outs,
        2 * m * width * feats * len(sources),
        (),
        resident,
        after,
    )


def back_kernel(layers, counts, known, *refs):
    errors = []
    for count in counts:
        errors.append(cat([r[...] for r in refs[:count]]))
        refs = refs[count:]
    pre, refs = refs[:layers], refs[layers:]
    pairs = layers * (layers + 1) // 2
    weight, refs = refs[:pairs], refs[pairs:]
    early, refs = refs[:known], refs[known:]
    out, total = refs[:layers], refs[layers]
    for s in range(layers):
        value = early[s][...] if s < known else None
        for t in range(max(s, layers - 1 if s < known else 0), layers):
            term = dot(errors[t], weight[pair_slot(s, t, layers)][0], ((1,), (1,)))
            value = term if value is None else value + term
        value = (value * pre[s][...]).astype(out[s].dtype)
        out[s][...] = value
        total[s] = jnp.sum(value.astype(jnp.float32), axis=0, keepdims=True)


def back(errors, pre, weight, layers, resident, early=(), after=()):
    pairs, feats, width = weight.shape
    m = pre[0].shape[0]
    c = piece(feats, 256)
    ins = [(e, e.shape, lambda j: (0, 0)) for t in range(layers) for e in errors[t]]
    ins += [(p, (m, c), lambda j: (0, j)) for p in pre]
    ins += [(weight, (1, c, width), lambda j, k=k: (k, j, 0)) for k in range(pairs)]
    ins += [(e, (m, c), lambda j: (0, j)) for e in early]
    outs = [((m, feats), jnp.bfloat16, (m, c), lambda j: (0, j))] * layers
    outs.append(((layers, 1, feats), jnp.float32, (layers, 1, c), lambda j: (0, 0, j)))
    got = call(
        functools.partial(back_kernel, layers, [len(e) for e in errors], len(early)),
        "back",
        feats // c,
        ins,
        outs,
        2 * m * width * feats * (pairs - len(early)),
        (),
        resident,
        after,
    )
    return got[:layers], got[layers]


def first_kernel(parts, *refs):
    error = cat([r[...] for r in refs[:parts]])
    weight, out = refs[parts:]
    out[...] = dot(error, weight[0], ((1,), (1,)))


def first(errors, weight, after=()):
    _, feats, width = weight.shape
    m = sum(e.shape[0] for e in errors)
    c = piece(feats, 256)
    ins = [(e, e.shape, lambda j: (0, 0)) for e in errors]
    ins.append((weight, (1, c, width), lambda j: (0, j, 0)))
    outs = [((m, feats), jnp.float32, (m, c), lambda j: (0, j))]
    body = functools.partial(first_kernel, len(errors))
    return call(body, "first", feats // c, ins, outs, 2 * m * width * feats, (), True, after)[0]


def dec_kernel(layers, scale, counts, me, *refs):
    a, b = counts
    codes = [cat([r[...] for r in refs[s * a:(s + 1) * a]]) for s in range(layers)]
    refs = refs[layers * a:]
    errors = [cat([r[...] for r in refs[t * b:(t + 1) * b]]) for t in range(layers)]
    out = refs[layers * b]
    for s in range(layers):
        for t in range(s, layers):
            value = dot(codes[s], errors[t], ((0,), (0,))) * scale
            out[pair_slot(s, t, layers)] = value.astype(out.dtype)


def dec_grads(codes, errors, me, own, scale, layers):
    width = errors[0][0].shape[1]
    pairs = layers * (layers + 1) // 2
    m = sum(p.shape[0] for p in codes[0])
    c = piece(width, 768)
    ins = [i for s in range(layers) for i in share(codes[s], own, me)]
    ins += [(p, (p.shape[0], c), lambda j, me: (0, j)) for t in range(layers) for p in errors[t]]
    outs = [((pairs, own, width), jnp.bfloat16, (pairs, own, c), lambda j, me: (0, 0, j))]
    return call(
        functools.partial(dec_kernel, layers, scale, (len(codes[0]), len(errors[0]))),
        "dec_grads",
        width // c,
        ins,
        outs,
        2 * m * width * own * pairs,
        (me,),
    )[0]


def enc_kernel(layers, scale, counts, me, *refs):
    a, b = counts
    inputs = [cat([r[...] for r in refs[s * a:(s + 1) * a]]) for s in range(layers)]
    refs = refs[layers * a:]
    grads = [cat([r[...] for r in refs[s * b:(s + 1) * b]]) for s in range(layers)]
    out = refs[layers * b]
    for s in range(layers):
        out[s] = (dot(inputs[s], grads[s], ((0,), (0,))) * scale).astype(out.dtype)


def enc_grads(inputs, grads, me, own, scale, layers):
    feats = grads[0][0].shape[1]
    m = sum(p.shape[0] for p in inputs[0])
    c = piece(feats, 256)
    ins = [i for s in range(layers) for i in share(inputs[s], own, me)]
    ins += [(p, (p.shape[0], c), lambda j, me: (0, j)) for s in range(layers) for p in grads[s]]
    outs = [((layers, own, feats), jnp.bfloat16, (layers, own, c), lambda j, me: (0, 0, j))]
    return call(
        functools.partial(enc_kernel, layers, scale, (len(inputs[0]), len(grads[0]))),
        "enc_grads",
        feats // c,
        ins,
        outs,
        2 * m * own * feats * layers,
        (me,),
    )[0]


def grads_body(layers, scale, counts, own, *refs):
    lists = []
    for count in counts:
        lists.append([refs[s * count:(s + 1) * count] for s in range(layers)])
        refs = refs[layers * count:]
    codes, errors, inputs, grads = lists
    sums, refs = refs[:-7], refs[-7:]
    dec_out, enc_out, bias_out, dec_held, enc_held, dec_sems, enc_sems = refs
    copies = []
    me = lax.axis_index("tok")

    def mine(size):
        return pl.ds(pl.multiple_of(me * size, 128), size)

    def leave(held, out, sems, slot, left, right):
        width = right.shape[1]
        size = piece(width, 768)
        for j in range(width // size):
            value = dot(left, right[:, j * size:(j + 1) * size], ((0,), (0,)))
            at = (slot, slice(None), slice(j * size, (j + 1) * size))
            held[at] = (value * scale).astype(held.dtype)
            copy = pltpu.make_async_copy(held.at[at], out.at[at], sems.at[slot, j])
            copy.start()
            copies.append(copy)

    def columns(parts, size):
        if parts[0].shape[1] == size:
            return cat([p[...] for p in parts])
        return cat([p[:, mine(size)] for p in parts])

    for s in range(layers):
        left = columns(codes[s], own[0])
        for t in range(s, layers):
            right = cat([e[...] for e in errors[t]])
            leave(dec_held, dec_out, dec_sems, pair_slot(s, t, layers), left, right)
    for s in range(layers):
        leave(enc_held, enc_out, enc_sems, s, columns(inputs[s], own[1]), cat([g[...] for g in grads[s]]))
        total = sums[0][s, :, mine(own[0])]
        for more in sums[1:]:
            total = total + more[s, :, mine(own[0])]
        bias_out[pl.ds(s, 1)] = total * scale
    for copy in copies:
        copy.wait()


def all_grads(codes, errors, inputs, grads, sums, own, scale, layers):
    lists = (codes, errors, inputs, grads)
    dec = (layers * (layers + 1) // 2, own[0], errors[0][0].shape[1])
    enc = (layers, own[1], grads[0][0].shape[1])
    arrays = [pltpu.with_memory_space_constraint(p, pltpu.VMEM) for parts in lists for s in parts for p in s]
    arrays += [pltpu.with_memory_space_constraint(p, pltpu.VMEM) for p in sums]
    return pl.pallas_call(
        functools.partial(grads_body, layers, scale, [len(parts[0]) for parts in lists], own),
        name="grads",
        out_shape=[
            jax.ShapeDtypeStruct(dec, jnp.bfloat16),
            jax.ShapeDtypeStruct(enc, jnp.bfloat16),
            jax.ShapeDtypeStruct((layers, own[0]), jnp.float32),
        ],
        in_specs=inside(len(arrays)),
        out_specs=[pl.BlockSpec(memory_space=pltpu.HBM)] * 2 + inside(1),
        scratch_shapes=[
            pltpu.VMEM(dec, jnp.bfloat16),
            pltpu.VMEM(enc, jnp.bfloat16),
            pltpu.SemaphoreType.DMA((dec[0], dec[2] // piece(dec[2], 768))),
            pltpu.SemaphoreType.DMA((enc[0], enc[2] // piece(enc[2], 768))),
        ],
        compiler_params=pltpu.CompilerParams(vmem_limit_bytes=2 * (math.prod(dec) + math.prod(enc)) + 8 * MIB),
        cost_estimate=pl.CostEstimate(flops=0, bytes_accessed=0, transcendentals=0),
    )(*arrays)


def plain(acts_in, targets, enc_weight, bias, dec_weight, scale):
    layers, width, feats = enc_weight.shape
    feat, tok = lax.axis_size("feat"), lax.axis_size("tok")

    def gather(value):
        return lax.all_gather(value, "feat", axis=0, tiled=True)

    inputs, pre, codes, errors, grads, sums = [], [], [], [], [], []
    for g in range(tok):
        acts = swap(acts_in, "tok", g) if g else acts_in
        inputs.append([])
        pre.append([])
        codes.append([])
        for s in range(layers):
            inputs[g].append([gather(acts[:, s, :])])
            p, c = encode(s, inputs[g][s], enc_weight, bias, False)
            pre[g].append(p)
            codes[g].append(c)
    own = []
    for t in range(layers):
        halves = decode(t, range(t + 1), codes[0], dec_weight, layers, (), True, False)
        part = lax.psum_scatter(cat(halves), "feat", scatter_dimension=0, tiled=True)
        own.append((part.astype(jnp.float32) - targets[:, t, :].astype(jnp.float32)).astype(jnp.bfloat16))
    for g in range(tok):
        errors.append([[gather(swap(e, "tok", g) if g else e)] for e in own])
        d, total = back(errors[g], pre[g], dec_weight, layers, False)
        grads.append(d)
        sums.append(total)
    me = lax.axis_index("tok")
    index = me.reshape(1).astype(jnp.int32)

    def every(parts):
        return [[parts[g][s] for g in range(tok)] for s in range(layers)]

    def flat(parts):
        return [[parts[g][s][0] for g in range(tok)] for s in range(layers)]

    rows = feats // tok
    dec_out = dec_grads(every(codes), flat(errors), index, rows, scale, layers)
    enc_out = enc_grads(flat(inputs), every(grads), index, width // tok, scale, layers)
    total = sum(sums[1:], sums[0]).reshape(layers, feats) * scale
    return enc_out, lax.dynamic_slice_in_dim(total, me * rows, rows, axis=1), dec_out


def staged(acts_in, targets, enc_weight, bias, dec_weight, scale):
    layers, width, feats = enc_weight.shape
    n = acts_in.shape[0]
    quart = n * (lax.axis_size("feat") // 4)
    hop = quart // 2
    line = [4 * k for k in range(1, lax.axis_size("feat") // 4)]
    small = ((n, width), jnp.bfloat16)
    lows = [((quart, width), jnp.float32), ((quart, width), jnp.bfloat16)]

    def along(values):
        return [swap(v, "feat", bits) for v, bits in zip(values, line)]

    def across(value):
        return swap(value, "feat", 2)

    def core(value):
        return swap(value, "feat", 1)

    def away(value):
        return swap(value, "tok", 1)

    def encoded(s, parts, after=()):
        return encode(s, parts, enc_held, bias, True, after)

    def pair(keep, got, after):
        return local(pair_kernel, "pair", [keep, *got], lows, after)

    def error(t, low, got, ends, after):
        arrays = [low, got, *ends, targets[:, t, :]]
        return local(functools.partial(error_kernel, n), "error", arrays, [small], after)[0]

    acts = [acts_in[:, s, :] for s in range(layers)]
    ends = quart - n
    z_a0 = along([acts[0]] * len(line))
    enc_held = load([enc_weight])[0]
    done = [*z_a0, enc_held]
    line0, send, a1 = join([z_a0, [*z_a0, *acts], [acts[1]]], done)
    y_s, x_s = away(send), across(send)
    z_a1 = along([a1] * len(line))
    dec_held = load([dec_weight], [line0])[0]
    done = [*z_a1, x_s, y_s, dec_held]
    far0, far1 = [(x_s, ends, n), (x_s, 0, ends)], [(x_s, quart, n)]
    line1, col0 = join([z_a1, [acts[0], line0, *far0]], done)
    y_l1, x_l1 = away(line1), across(line1)
    in0 = [col0, core(col0)]
    pre0, code0 = encoded(0, in0)
    keep0, *give0 = decode(0, [0], [code0], dec_held, layers, (), True, True, (), 4)
    early = decode(1, [0], [code0], dec_held, layers, (), False, True, (keep0,))
    got0 = [core(g) for g in give0]
    done = [x_l1, y_l1, *got0, *early]
    low0, high0 = pair(keep0, got0, done)
    far1.append(x_l1)
    col1, fars = join([[a1, line1, *far1], far0 + far1], done)
    x_h0 = across(high0)
    in1 = [col1, core(col1)]
    pre1, code1 = encoded(1, in1)
    keep1, *give1 = decode(1, [1], [code0, code1], dec_held, layers, early, True, True, (), 4)
    got1 = [core(g) for g in give1]
    done = [x_h0, *got1]
    body = functools.partial(open_kernel, n, len(line))
    *ends0, low1, high1 = local(body, "open", [low0, x_h0, keep1, *got1], [small] * len(line) + lows, done)
    z_r0 = along(ends0)
    x_h1 = across(high1)
    done = [*z_r0, x_h1]
    arrays = [low0, x_h0, *z_r0, targets[:, 0, :], low1, x_h1]
    shapes = [((2 * n, width), jnp.bfloat16)] * len(line) + [small]
    *turned, e0 = local(functools.partial(turn_kernel, n, len(line)), "turn", arrays, shapes, done)
    y_f, y_e0, x_e0 = away(fars), away(e0), across(e0)
    z_t = along(turned)
    done = [*z_t, x_e0, y_e0, y_f]
    e1 = error(1, low1, x_h1, z_t, done)
    lines = [(z, n, n) for z in z_t]
    near0, both = join([[e0, *lines], [*lines, e1]], done)
    there0 = [(y_s, ends, n), (y_s, 0, ends), (y_f, 0, quart)]
    there0, there1 = join([there0, [(y_s, quart, n), y_l1, (y_f, quart, quart)]], done)
    y_b, x_b = away(both), across(both)
    z_e1 = along([e1] * len(line))
    there_in0, there_in1 = [there0, core(there0)], [there1, core(there1)]
    there_pre0, there_code0 = encoded(0, there_in0)
    there_pre1, there_code1 = encoded(1, there_in1)
    done = [*z_e1, x_b, y_b, there_code0, there_code1]
    near_y0 = [y_e0, (y_b, 0, ends)]
    half_y0 = [y_e0, (y_b, 0, hop - n)]
    near1, whole0, near_y0, go_x, go_y = join(
        [
            [e1, *z_e1],
            [near0, x_e0, (x_b, 0, ends)],
            near_y0,
            [*z_e1, *half_y0],
            [*z_e1, (x_b, hop - n, quart - hop)],
        ],
        done,
    )
    y_g, x_g = away(go_y), across(go_x)
    err0 = [whole0, core(whole0)]
    first_own = first(err0, dec_held)
    done = [x_g, y_g, first_own]
    whole1, one1, two1, near_y1, far_y0 = join(
        [
            [near1, (x_b, ends, n), (x_g, 0, ends)],
            [(y_b, ends, n), (y_g, 0, hop - n)],
            [(x_g, hop - n, quart - hop)],
            [(y_b, ends, n), (y_g, 0, ends)],
            [(x_g, ends, hop), (y_g, ends, quart - hop)],
        ],
        done,
    )
    y_t1, x_o1 = away(two1), across(one1)
    err1 = [whole1, core(whole1)]
    there_err0 = [near_y0, far_y0, core(near_y0), core(far_y0)]
    core_n1 = core(near_y1)
    grad_own, sum_own = back([err0, err1], [pre0, pre1], dec_held, layers, True, [first_own])
    first_there = first(there_err0, dec_held, [grad_own[0]])
    done = [x_o1, y_t1, core_n1, first_there]
    far_y1 = join([[x_o1, y_t1]], done)[0]
    there_err1 = [near_y1, far_y1, core_n1, core(far_y1)]
    there_errs, there_pres = [there_err0, there_err1], [there_pre0, there_pre1]
    grad_there, sum_there = back(there_errs, there_pres, dec_held, layers, True, [first_there])
    dec_out, enc_out, bias_out = all_grads(
        [[code0, there_code0], [code1, there_code1]],
        [err0 + there_err0, err1 + there_err1],
        [in0 + there_in0, in1 + there_in1],
        [[grad_own[s], grad_there[s]] for s in range(layers)],
        [sum_own, sum_there],
        (feats // lax.axis_size("tok"), width // lax.axis_size("tok")),
        scale,
        layers,
    )
    return enc_out, bias_out, dec_out


def shards(acts_in, targets, enc_weight, enc_bias, dec_weight):
    layers, width, feats = enc_weight.shape
    n = acts_in.shape[0]
    feat, tok = lax.axis_size("feat"), lax.axis_size("tok")
    scale = 1.0 / math.sqrt(n * feat * tok)
    bias = enc_bias.reshape(layers, 1, feats)
    held = 2 * (math.prod(enc_weight.shape) + math.prod(dec_weight.shape))
    held += 4 * layers * n * feat * tok * (width + 2 * feats)
    fits = held <= 54 * MIB and n % 8 == 0 and (feats // tok) % 128 == 0 and (width // tok) % 128 == 0
    run = staged if fits and layers == 2 and tok == 2 and feat >= 8 else plain
    return run(acts_in, targets, enc_weight, bias, dec_weight, scale)


def solution(mesh):
    return jax.shard_map(
        shards,
        mesh=mesh,
        in_specs=(
            P(("tok", "feat"), None, None),
            P(("tok", "feat"), None, None),
            P(None, None, "feat"),
            P(None, "feat"),
            P(None, "feat", None),
        ),
        out_specs=(
            P(None, "tok", "feat"),
            P(None, ("feat", "tok")),
            P(None, ("feat", "tok"), None),
        ),
        check_vma=False,
    )
```

time: 168 us -> 151 us (0.90)
  waiting for transfers between devices: 72.8 us -> 54.1 us
    ppermute x45 -> x48, waiting for transfers between devices: 72.8 us -> 54.1 us  [swap(): lax.ppermute(value, axis, [(i, i ^ bits) for i in range(lax.axis_size(axi...]
    pallas_call x1 -> x2, Pallas kernels: 7.72 us -> 8.72 us  [load(): pl.pallas_call(lambda *refs: load_kernel(count, *refs[skip:]), name='load...]
    ppermute x45 -> x48, starting transfers between devices: 44.6 us -> 45.4 us  [swap(): lax.ppermute(value, axis, [(i, i ^ bits) for i in range(lax.axis_size(axi...]
    pallas_call x26 -> x23, Pallas kernels: 27.7 us -> 28 us  [local(): pl.pallas_call(lambda *refs: kernel(*refs[skip:]), name=name, out_shape=[...]
  transfers between devices with their start and end apart: 45 -> 48, of which waited for: 24 -> 20; matrix products, arithmetic and copies ran while one was open for 0% -> 0% of each run, Pallas kernels for 14% -> 21%
where the time goes in v3:
time: 151 us
  waiting for transfers between devices  54.1 us (36%)
  Pallas kernels  48.2 us (32%)
  starting transfers between devices  45.4 us (30%)
  local copies, waits for them, and re-layouts  1.81 us (1%)
    ppermute x48, waiting for transfers between devices, swap(): lax.ppermute(value, axis, [(i, i ^ bits) for i in range(lax.axis_size(axi...  54.1 us
    ppermute x48, starting transfers between devices, swap(): lax.ppermute(value, axis, [(i, i ^ bits) for i in range(lax.axis_size(axi...  45.4 us
    pallas_call x23, Pallas kernels, local(): pl.pallas_call(lambda *refs: kernel(*refs[skip:]), name=name, out_shape=[...  28 us
    pallas_call x1, Pallas kernels, all_grads(): pl.pallas_call(functools.partial(grads_body, layers, scale, [len(parts[0]...  11.5 us
    pallas_call x2, Pallas kernels, load(): pl.pallas_call(lambda *refs: load_kernel(count, *refs[skip:]), name='load...  8.72 us
  transfers between devices with their start and end apart: 48, of which 20 were waited for; matrix products, arithmetic and copies ran while one was open for 0% of the time, Pallas kernels for 21%

profile of v3, /device:TPU:0, one launch (start us, length us, event | category | flops | bytes accessed | tf_op | source)
XLA Modules:
  0.0 150.7 jit_solution(13623614491871506696)
XLA Ops:
  2.1 5.1 %collective-permute-start.2 = (bf16[24,2304]{1,0:T(8,128)(2,1)S(1)}, bf16[24,2304]{1,0:T(8,128)(2,1)S(1)}, u32[]{:S(2)}, u32[]{:S(2)}) collective-permute-start(bf16[24,2304]{1,0:T(8,128)(2,1)S(1)} %bitcast.14), channel_id=1, source_target_pairs={{0,24},{2,26},{4,28},{6,30},{8,16},{10,18},{12,20},{14,22},{16,8},... | collective-permute-start | bytes 331784 | tf_op jit(solution)/shard_map/ppermute | solution.py:19
  7.9 3.7 %load.2.refs_3_.refs_2_ = bf16[2,2304,1024]{2,1,0:T(8,128)(2,1)S(1)} custom-call(bf16[2,2304,1024]{2,1,0:T(8,128)(2,1)} %refs_0_.1), custom_call_target="tpu_custom_call" | custom-call | tf_op jit(solution)/shard_map/load/pallas_call | solution.py:106
  11.6 4.9 %collective-permute-done.1.refs_1_.refs_5_.refs_8_ = bf16[24,2304]{1,0:T(8,128)(2,1)S(1)} collective-permute-done((bf16[24,2304]{1,0:T(8,128)(2,1)S(1)}, bf16[24,2304]{1,0:T(8,128)(2,1)S(1)}, u32[]{:S(2)}, u32[]{:S(2)}) %collective-permute-start.1) | collective-permute-done | bytes 110624 | tf_op jit(solution)/shard_map/ppermute | solution.py:19
  19.7 2.5 %collective-permute-start.5 = (bf16[24,2304]{1,0:T(8,128)(2,1)S(1)}, bf16[24,2304]{1,0:T(8,128)(2,1)S(1)}, u32[]{:S(2)}, u32[]{:S(2)}) collective-permute-start(bf16[24,2304]{1,0:T(8,128)(2,1)S(1)} %get-tuple-element.62.refs_7_), channel_id=1, source_target_pairs={{0,24},{2,26},{4,28},{6,30},{8,16},{10,18},{12,20},{14,22},{16,8},... | collective-permute-start | bytes 331784 | tf_op jit(solution)/shard_map/ppermute | solution.py:19
  22.1 1.9 %collective-permute-start.3 = (bf16[24,2304]{1,0:T(8,128)(2,1)S(1)}, bf16[24,2304]{1,0:T(8,128)(2,1)S(1)}, u32[]{:S(2)}, u32[]{:S(2)}) collective-permute-start(bf16[24,2304]{1,0:T(8,128)(2,1)S(1)} %get-tuple-element.62.refs_7_), channel_id=1, source_target_pairs={{0,8},{2,10},{4,12},{6,14},{8,0},{10,2},{12,4},{14,6},{16,24},{18,... | collective-permute-start | bytes 331784 | tf_op jit(solution)/shard_map/ppermute | solution.py:19
  24.1 5.0 %load.3.refs_5_.refs_1_.refs_2_.refs_6_.refs_7_.refs_8_.refs_10_.refs_11_.refs_12_ = bf16[3,1024,2304]{2,1,0:T(8,128)(2,1)S(1)} custom-call(bf16[72,2304]{1,0:T(8,128)(2,1)S(1)} %get-tuple-element.64.refs_0_.refs_10_, bf16[3,1024,2304]{2,1,0:T(8,128)(2,1)} %refs_1_.1), custom_call_target="tpu_custom_call" | custom-call | tf_op jit(solution)/shard_map/load/pallas_call | solution.py:106
  29.1 1.8 %collective-permute-done.4.refs_1_.refs_7_ = bf16[24,2304]{1,0:T(8,128)(2,1)S(1)} collective-permute-done((bf16[24,2304]{1,0:T(8,128)(2,1)S(1)}, bf16[24,2304]{1,0:T(8,128)(2,1)S(1)}, u32[]{:S(2)}, u32[]{:S(2)}) %collective-permute-start.4) | collective-permute-done | bytes 110624 | tf_op jit(solution)/shard_map/ppermute | solution.py:19
  34.1 2.1 %encode.4 = (f32[384,1024]{1,0:T(8,128)S(1)}, bf16[384,1024]{1,0:T(8,128)(2,1)S(1)}) custom-call(bf16[192,2304]{1,0:T(8,128)(2,1)S(1)} %get-tuple-element.65.refs_0_.refs_16_, bf16[192,2304]{1,0:T(8,128)(2,1)S(1)} %collective-permute-done.8.refs_1_.refs_17_, bf16[2,2304,1024]{2,1,0:T(8,128)(2,1)S(1)} %load.2.refs_3_.refs_2_, f32[2,1,1024]{2,1,0:T(1,128)S(1)} %reshape.9.refs_3_), custom_call_target="tpu_custom_call" | custom-call | flops 1811939328 | tf_op jit(solution)/shard_map/encode/pallas_call | solution.py:57
  36.1 2.0 %decode.3 = (bf16[192,2304]{1,0:T(8,128)(2,1)S(1)}, bf16[48,2304]{1,0:T(8,128)(2,1)S(1)}, bf16[48,2304]{1,0:T(8,128)(2,1)S(1)}, bf16[48,2304]{1,0:T(8,128)(2,1)S(1)}, bf16[48,2304]{1,0:T(8,128)(2,1)S(1)}) custom-call(bf16[384,1024]{1,0:T(8,128)(2,1)S(1)} %get-tuple-element.66.refs_0_.refs_1_, ...), custom_call_target="tpu_custom_call" | custom-call | flops 1811939328 | tf_op jit(solution)/shard_map/decode/pallas_call | solution.py:57
  38.9 3.0 %collective-permute-done.10.refs_1_.refs_10_ = bf16[72,2304]{1,0:T(8,128)(2,1)S(1)} collective-permute-done((bf16[72,2304]{1,0:T(8,128)(2,1)S(1)}, bf16[72,2304]{1,0:T(8,128)(2,1)S(1)}, u32[]{:S(2)}, u32[]{:S(2)}) %collective-permute-start.10) | collective-permute-done | bytes 331808 | tf_op jit(solution)/shard_map/ppermute | solution.py:19
  41.9 2.0 %decode.4.refs_6_.refs_2_ = f32[384,2304]{1,0:T(8,128)S(1)} custom-call(bf16[192,2304]{1,0:T(8,128)(2,1)S(1)} %get-tuple-element.72.refs_0_.refs_7_, bf16[384,1024]{1,0:T(8,128)(2,1)S(1)} %get-tuple-element.66.refs_0_.refs_1_, bf16[3,1024,2304]{2,1,0:T(8,128)(2,1)S(1)} %load.3.refs_5_.refs_1_.refs_2_.refs_6_.refs_7_.refs_8_.refs_10_.refs_11_.refs_12_), custom_call_target="tpu_custom_call" | custom-call | flops 1811939328 | tf_op jit(solution)/shard_map/decode/pallas_call | solution.py:57
  46.8 2.1 %encode.5 = (f32[384,1024]{1,0:T(8,128)S(1)}, bf16[384,1024]{1,0:T(8,128)(2,1)S(1)}) custom-call(bf16[192,2304]{1,0:T(8,128)(2,1)S(1)} %get-tuple-element.74.refs_0_.refs_20_, bf16[192,2304]{1,0:T(8,128)(2,1)S(1)} %collective-permute-done.16.refs_1_.refs_21_, bf16[2,2304,1024]{2,1,0:T(8,128)(2,1)S(1)} %load.2.refs_3_.refs_2_, f32[2,1,1024]{2,1,0:T(1,128)S(1)} %reshape.9.refs_3_), custom_call_target="tpu_custom_call" | custom-call | flops 1811939328 | tf_op jit(solution)/shard_map/encode/pallas_call | solution.py:57
  48.8 2.1 %decode.5 = (bf16[192,2304]{1,0:T(8,128)(2,1)S(1)}, bf16[48,2304]{1,0:T(8,128)(2,1)S(1)}, bf16[48,2304]{1,0:T(8,128)(2,1)S(1)}, bf16[48,2304]{1,0:T(8,128)(2,1)S(1)}, bf16[48,2304]{1,0:T(8,128)(2,1)S(1)}) custom-call(bf16[384,1024]{1,0:T(8,128)(2,1)S(1)} %get-tuple-element.75.refs_0_.refs_2_, ...), custom_call_target="tpu_custom_call" | custom-call | flops 1811939328 | tf_op jit(solution)/shard_map/decode/pallas_call | solution.py:57
  52.0 5.0 %collective-permute-done.15.refs_0_.refs_6_.refs_5_ = bf16[96,2304]{1,0:T(8,128)(2,1)S(1)} collective-permute-done((bf16[96,2304]{1,0:T(8,128)(2,1)S(1)}, bf16[96,2304]{1,0:T(8,128)(2,1)S(1)}, u32[]{:S(2)}, u32[]{:S(2)}) %collective-permute-start.15) | collective-permute-done | bytes 442400 | tf_op jit(solution)/shard_map/ppermute | solution.py:19
  58.1 2.7 %collective-permute-start.22 = (bf16[24,2304]{1,0:T(8,128)(2,1)S(1)}, bf16[24,2304]{1,0:T(8,128)(2,1)S(1)}, u32[]{:S(2)}, u32[]{:S(2)}) collective-permute-start(bf16[24,2304]{1,0:T(8,128)(2,1)S(1)} %get-tuple-element.83), channel_id=1, source_target_pairs={{0,16},{2,18},{4,20},{6,22},{8,24},{10,26},{12,28},{14,30},{16,0},... | collective-permute-start | bytes 331784 | tf_op jit(solution)/shard_map/ppermute | solution.py:19
  64.2 4.6 %collective-permute-done.22.refs_1_.refs_7_ = bf16[24,2304]{1,0:T(8,128)(2,1)S(1)} collective-permute-done((bf16[24,2304]{1,0:T(8,128)(2,1)S(1)}, bf16[24,2304]{1,0:T(8,128)(2,1)S(1)}, u32[]{:S(2)}, u32[]{:S(2)}) %collective-permute-start.22) | collective-permute-done | bytes 110624 | tf_op jit(solution)/shard_map/ppermute | solution.py:19
  68.8 3.7 %collective-permute-done.24.refs_3_.refs_11_.refs_7_ = bf16[96,2304]{1,0:T(8,128)(2,1)S(1)} collective-permute-done((bf16[96,2304]{1,0:T(8,128)(2,1)S(1)}, bf16[96,2304]{1,0:T(8,128)(2,1)S(1)}, u32[]{:S(2)}, u32[]{:S(2)}) %collective-permute-start.24) | collective-permute-done | bytes 442400 | tf_op jit(solution)/shard_map/ppermute | solution.py:19
  72.8 2.8 %collective-permute-start.26 = (bf16[48,2304]{1,0:T(8,128)(2,1)S(1)}, bf16[48,2304]{1,0:T(8,128)(2,1)S(1)}, u32[]{:S(2)}, u32[]{:S(2)}) collective-permute-start(bf16[48,2304]{1,0:T(8,128)(2,1)S(1)} %get-tuple-element.88), channel_id=1, source_target_pairs={{0,16},{2,18},{4,20},{6,22},{8,24},{10,26},{12,28},{14,30},{16,0},... | collective-permute-start | bytes 663560 | tf_op jit(solution)/shard_map/ppermute | solution.py:19
  81.9 1.8 %collective-permute-done.28.refs_3_.refs_12_ = bf16[24,2304]{1,0:T(8,128)(2,1)S(1)} collective-permute-done((bf16[24,2304]{1,0:T(8,128)(2,1)S(1)}, bf16[24,2304]{1,0:T(8,128)(2,1)S(1)}, u32[]{:S(2)}, u32[]{:S(2)}) %collective-permute-start.28) | collective-permute-done | bytes 110624 | tf_op jit(solution)/shard_map/ppermute | solution.py:19
  83.7 6.3 %collective-permute-done.26.refs_1_.refs_9_.refs_8_.refs_11_ = bf16[48,2304]{1,0:T(8,128)(2,1)S(1)} collective-permute-done((bf16[48,2304]{1,0:T(8,128)(2,1)S(1)}, bf16[48,2304]{1,0:T(8,128)(2,1)S(1)}, u32[]{:S(2)}, u32[]{:S(2)}) %collective-permute-start.26) | collective-permute-done | bytes 221216 | tf_op jit(solution)/shard_map/ppermute | solution.py:19
  94.2 1.9 %collective-permute-start.35 = (bf16[24,2304]{1,0:T(8,128)(2,1)S(1)}, bf16[24,2304]{1,0:T(8,128)(2,1)S(1)}, u32[]{:S(2)}, u32[]{:S(2)}) collective-permute-start(bf16[24,2304]{1,0:T(8,128)(2,1)S(1)} %error.1.refs_13_.refs_7_), channel_id=1, source_target_pairs={{0,24},{2,26},{4,28},{6,30},{8,16},{10,18},{12,20},{14,22},{16,8},... | collective-permute-start | bytes 331784 | tf_op jit(solution)/shard_map/ppermute | solution.py:19
  96.1 2.5 %collective-permute-start.34 = (bf16[24,2304]{1,0:T(8,128)(2,1)S(1)}, bf16[24,2304]{1,0:T(8,128)(2,1)S(1)}, u32[]{:S(2)}, u32[]{:S(2)}) collective-permute-start(bf16[24,2304]{1,0:T(8,128)(2,1)S(1)} %error.1.refs_13_.refs_7_), channel_id=1, source_target_pairs={{0,16},{2,18},{4,20},{6,22},{8,24},{10,26},{12,28},{14,30},{16,0},... | collective-permute-start | bytes 331784 | tf_op jit(solution)/shard_map/ppermute | solution.py:19
  98.7 2.1 %encode.7 = (f32[384,1024]{1,0:T(8,128)S(1)}, bf16[384,1024]{1,0:T(8,128)(2,1)S(1)}) custom-call(bf16[192,2304]{1,0:T(8,128)(2,1)S(1)} %get-tuple-element.94.refs_0_.refs_22_, bf16[192,2304]{1,0:T(8,128)(2,1)S(1)} %collective-permute-done.32.refs_1_.refs_23_, bf16[2,2304,1024]{2,1,0:T(8,128)(2,1)S(1)} %load.2.refs_3_.refs_2_, f32[2,1,1024]{2,1,0:T(1,128)S(1)} %reshape.9.refs_3_), custom_call_target="tpu_custom_call" | custom-call | flops 1811939328 | tf_op jit(solution)/shard_map/encode/pallas_call | solution.py:57
  100.8 2.1 %encode.6 = (f32[384,1024]{1,0:T(8,128)S(1)}, bf16[384,1024]{1,0:T(8,128)(2,1)S(1)}) custom-call(bf16[192,2304]{1,0:T(8,128)(2,1)S(1)} %get-tuple-element.92.refs_0_.refs_18_, bf16[192,2304]{1,0:T(8,128)(2,1)S(1)} %collective-permute-done.31.refs_1_.refs_19_, bf16[2,2304,1024]{2,1,0:T(8,128)(2,1)S(1)} %load.2.refs_3_.refs_2_, f32[2,1,1024]{2,1,0:T(1,128)S(1)} %reshape.9.refs_3_), custom_call_target="tpu_custom_call" | custom-call | flops 1811939328 | tf_op jit(solution)/shard_map/encode/pallas_call | solution.py:57
  102.9 4.8 %collective-permute-done.34.refs_1_.refs_9_.refs_17_.refs_22_ = bf16[24,2304]{1,0:T(8,128)(2,1)S(1)} collective-permute-done((bf16[24,2304]{1,0:T(8,128)(2,1)S(1)}, bf16[24,2304]{1,0:T(8,128)(2,1)S(1)}, u32[]{:S(2)}, u32[]{:S(2)}) %collective-permute-start.34) | collective-permute-done | bytes 110624 | tf_op jit(solution)/shard_map/ppermute | solution.py:19
  110.6 2.0 %first.2.refs_2_.refs_9_ = f32[384,1024]{1,0:T(8,128)S(1)} custom-call(bf16[192,2304]{1,0:T(8,128)(2,1)S(1)} %get-tuple-element.98.refs_0_.refs_4_, bf16[192,2304]{1,0:T(8,128)(2,1)S(1)} %collective-permute-done.38.refs_1_.refs_5_, bf16[3,1024,2304]{2,1,0:T(8,128)(2,1)S(1)} %load.3.refs_5_.refs_1_.refs_2_.refs_6_.refs_7_.refs_8_.refs_10_.refs_11_.refs_12_), custom_call_target="tpu_custom_call" | custom-call | flops 1811939328 | tf_op jit(solution)/shard_map/first/pallas_call | solution.py:57
  112.6 10.5 %collective-permute-done.39.refs_0_.refs_5_.refs_8_.refs_11_ = bf16[120,2304]{1,0:T(8,128)(2,1)S(1)} collective-permute-done((bf16[120,2304]{1,0:T(8,128)(2,1)S(1)}, bf16[120,2304]{1,0:T(8,128)(2,1)S(1)}, u32[]{:S(2)}, u32[]{:S(2)}) %collective-permute-start.39) | collective-permute-done | bytes 552992 | tf_op jit(solution)/shard_map/ppermute | solution.py:19
  126.2 4.0 %back.2 = (bf16[384,1024]{1,0:T(8,128)(2,1)S(1)}, bf16[384,1024]{1,0:T(8,128)(2,1)S(1)}, f32[2,1,1024]{2,1,0:T(1,128)S(1)}) custom-call(bf16[192,2304]{1,0:T(8,128)(2,1)S(1)} %get-tuple-element.98.refs_0_.refs_4_, bf16[192,2304]{1,0:T(8,128)(2,1)S(1)} %collective-permute-done.38.refs_1_.refs_5_, bf16[192,2304]{1,0:T(8,128)(2,1)S(1)} %get-tuple-element.104.refs_2_.refs_10_, ...), custom_call_target="tpu_custom_call" | custom-call | flops 3623878656 | tf_op jit(solution)/shard_map/back/pallas_call | solution.py:57
  130.2 2.0 %first.3.refs_3_.refs_13_ = f32[384,1024]{1,0:T(8,128)S(1)} custom-call(bf16[384,1024]{1,0:T(8,128)(2,1)S(1)} %get-tuple-element.110.refs_0_.refs_24_, bf16[96,2304]{1,0:T(8,128)(2,1)S(1)} %get-tuple-element.99.refs_1_.refs_0_.refs_6_, bf16[96,2304]{1,0:T(8,128)(2,1)S(1)} %get-tuple-element.103.refs_2_.refs_1_.refs_7_, ...), custom_call_target="tpu_custom_call" | custom-call | flops 1811939328 | tf_op jit(solution)/shard_map/first/pallas_call | solution.py:57
  133.3 1.8 %collective-permute-done.47.refs_7_.refs_15_ = bf16[96,2304]{1,0:T(8,128)(2,1)S(1)} collective-permute-done((bf16[96,2304]{1,0:T(8,128)(2,1)S(1)}, bf16[96,2304]{1,0:T(8,128)(2,1)S(1)}, u32[]{:S(2)}, u32[]{:S(2)}) %collective-permute-start.47) | collective-permute-done | bytes 442400 | tf_op jit(solution)/shard_map/ppermute | solution.py:19
  135.1 3.9 %back.3 = (bf16[384,1024]{1,0:T(8,128)(2,1)S(1)}, bf16[384,1024]{1,0:T(8,128)(2,1)S(1)}, f32[2,1,1024]{2,1,0:T(1,128)S(1)}) custom-call(bf16[96,2304]{1,0:T(8,128)(2,1)S(1)} %get-tuple-element.99.refs_1_.refs_0_.refs_6_, bf16[96,2304]{1,0:T(8,128)(2,1)S(1)} %get-tuple-element.103.refs_2_.refs_1_.refs_7_, ...), custom_call_target="tpu_custom_call" | custom-call | flops 3623878656 | tf_op jit(solution)/shard_map/back/pallas_call | solution.py:57
  139.0 11.5 %grads.1 = (bf16[3,512,2304]{2,1,0:T(8,128)(2,1)}, bf16[2,1152,1024]{2,1,0:T(8,128)(2,1)}, f32[2,512]{1,0:T(2,128)}) custom-call(bf16[384,1024]{1,0:T(8,128)(2,1)S(1)} %get-tuple-element.66.refs_0_.refs_1_, bf16[384,1024]{1,0:T(8,128)(2,1)S(1)} %get-tuple-element.93.refs_5_.refs_1_, bf16[384,1024]{1,0:T(8,128)(2,1)S(1)} %get-tuple-element.75.refs_0_.refs_2_, ...), custom_call_target="tpu_custom_call" | custom-call | tf_op jit(solution)/shard_map/grads/pallas_call | solution.py:405
  (101 shorter events, 35.0 us)
Async XLA Ops:
  2.1 9.5 %collective-permute-start.2 = (bf16[24,2304]{1,0:T(8,128)(2,1)S(1)}, bf16[24,2304]{1,0:T(8,128)(2,1)S(1)}, u32[]{:S(2)}, u32[]{:S(2)}) collective-permute-start(bf16[24,2304]{1,0:T(8,128)(2,1)S(1)} %bitcast.14), channel_id=1, source_target_pairs={{0,24},{2,26},{4,28},{6,30},{8,16},{10,18},{12,20},{14,22},{16,8},... | collective-permute-start | bytes 331784 | tf_op jit(solution)/shard_map/ppermute | solution.py:19
  7.2 9.3 %collective-permute-start.1 = (bf16[24,2304]{1,0:T(8,128)(2,1)S(1)}, bf16[24,2304]{1,0:T(8,128)(2,1)S(1)}, u32[]{:S(2)}, u32[]{:S(2)}) collective-permute-start(bf16[24,2304]{1,0:T(8,128)(2,1)S(1)} %bitcast.15), channel_id=1, source_target_pairs={{0,16},{2,18},{4,20},{6,22},{8,24},{10,26},{12,28},{14,30},{16,0},... | collective-permute-start | bytes 331784 | tf_op jit(solution)/shard_map/ppermute | solution.py:19
  7.2 9.3 %collective-permute-start = (bf16[24,2304]{1,0:T(8,128)(2,1)S(1)}, bf16[24,2304]{1,0:T(8,128)(2,1)S(1)}, u32[]{:S(2)}, u32[]{:S(2)}) collective-permute-start(bf16[24,2304]{1,0:T(8,128)(2,1)S(1)} %bitcast.16), channel_id=1, source_target_pairs={{0,8},{2,10},{4,12},{6,14},{8,0},{10,2},{12,4},{14,6},{16,24},{18,... | collective-permute-start | bytes 331784 | tf_op jit(solution)/shard_map/ppermute | solution.py:19
  16.6 14.4 %collective-permute-start.7 = (bf16[120,2304]{1,0:T(8,128)(2,1)S(1)}, bf16[120,2304]{1,0:T(8,128)(2,1)S(1)}, u32[]{:S(2)}, u32[]{:S(2)}) collective-permute-start(bf16[120,2304]{1,0:T(8,128)(2,1)S(1)} %get-tuple-element.63), channel_id=1, source_target_pairs={{0,1},{1,0},{2,3},{3,2},{4,5},{5,4},{6,7},{7,6},{8,9},{9,8},{10,11... | collective-permute-start | bytes 1658888 | tf_op jit(solution)/shard_map/ppermute | solution.py:19
  18.2 13.3 %collective-permute-start.6 = (bf16[120,2304]{1,0:T(8,128)(2,1)S(1)}, bf16[120,2304]{1,0:T(8,128)(2,1)S(1)}, u32[]{:S(2)}, u32[]{:S(2)}) collective-permute-start(bf16[120,2304]{1,0:T(8,128)(2,1)S(1)} %get-tuple-element.63), channel_id=1, source_target_pairs={{0,4},{2,6},{4,0},{6,2},{8,12},{10,14},{12,8},{14,10},{16,20},{18,... | collective-permute-start | bytes 1658888 | tf_op jit(solution)/shard_map/ppermute | solution.py:19
  19.7 9.4 %collective-permute-start.5 = (bf16[24,2304]{1,0:T(8,128)(2,1)S(1)}, bf16[24,2304]{1,0:T(8,128)(2,1)S(1)}, u32[]{:S(2)}, u32[]{:S(2)}) collective-permute-start(bf16[24,2304]{1,0:T(8,128)(2,1)S(1)} %get-tuple-element.62.refs_7_), channel_id=1, source_target_pairs={{0,24},{2,26},{4,28},{6,30},{8,16},{10,18},{12,20},{14,22},{16,8},... | collective-permute-start | bytes 331784 | tf_op jit(solution)/shard_map/ppermute | solution.py:19
  22.1 8.8 %collective-permute-start.4 = (bf16[24,2304]{1,0:T(8,128)(2,1)S(1)}, bf16[24,2304]{1,0:T(8,128)(2,1)S(1)}, u32[]{:S(2)}, u32[]{:S(2)}) collective-permute-start(bf16[24,2304]{1,0:T(8,128)(2,1)S(1)} %get-tuple-element.62.refs_7_), channel_id=1, source_target_pairs={{0,16},{2,18},{4,20},{6,22},{8,24},{10,26},{12,28},{14,30},{16,0},... | collective-permute-start | bytes 331784 | tf_op jit(solution)/shard_map/ppermute | solution.py:19
  22.1 8.8 %collective-permute-start.3 = (bf16[24,2304]{1,0:T(8,128)(2,1)S(1)}, bf16[24,2304]{1,0:T(8,128)(2,1)S(1)}, u32[]{:S(2)}, u32[]{:S(2)}) collective-permute-start(bf16[24,2304]{1,0:T(8,128)(2,1)S(1)} %get-tuple-element.62.refs_7_), channel_id=1, source_target_pairs={{0,8},{2,10},{4,12},{6,14},{8,0},{10,2},{12,4},{14,6},{16,24},{18,... | collective-permute-start | bytes 331784 | tf_op jit(solution)/shard_map/ppermute | solution.py:19
  31.7 10.3 %collective-permute-start.10 = (bf16[72,2304]{1,0:T(8,128)(2,1)S(1)}, bf16[72,2304]{1,0:T(8,128)(2,1)S(1)}, u32[]{:S(2)}, u32[]{:S(2)}) collective-permute-start(bf16[72,2304]{1,0:T(8,128)(2,1)S(1)} %get-tuple-element.67.refs_8_), channel_id=1, source_target_pairs={{0,1},{1,0},{2,3},{3,2},{4,5},{5,4},{6,7},{7,6},{8,9},{9,8},{10,11... | collective-permute-start | bytes 995336 | tf_op jit(solution)/shard_map/ppermute | solution.py:19
  32.2 11.7 %collective-permute-start.9 = (bf16[72,2304]{1,0:T(8,128)(2,1)S(1)}, bf16[72,2304]{1,0:T(8,128)(2,1)S(1)}, u32[]{:S(2)}, u32[]{:S(2)}) collective-permute-start(bf16[72,2304]{1,0:T(8,128)(2,1)S(1)} %get-tuple-element.67.refs_8_), channel_id=1, source_target_pairs={{0,4},{2,6},{4,0},{6,2},{8,12},{10,14},{12,8},{14,10},{16,20},{18,... | collective-permute-start | bytes 995336 | tf_op jit(solution)/shard_map/ppermute | solution.py:19
  44.9 12.2 %collective-permute-start.15 = (bf16[96,2304]{1,0:T(8,128)(2,1)S(1)}, bf16[96,2304]{1,0:T(8,128)(2,1)S(1)}, u32[]{:S(2)}, u32[]{:S(2)}) collective-permute-start(bf16[96,2304]{1,0:T(8,128)(2,1)S(1)} %get-tuple-element.73), channel_id=1, source_target_pairs={{0,4},{2,6},{4,0},{6,2},{8,12},{10,14},{12,8},{14,10},{16,20},{18,... | collective-permute-start | bytes 1327112 | tf_op jit(solution)/shard_map/ppermute | solution.py:19
  51.0 6.6 %collective-permute-start.17 = (bf16[48,2304]{1,0:T(8,128)(2,1)S(1)}, bf16[48,2304]{1,0:T(8,128)(2,1)S(1)}, u32[]{:S(2)}, u32[]{:S(2)}) collective-permute-start(bf16[48,2304]{1,0:T(8,128)(2,1)S(1)} %get-tuple-element.76), channel_id=1, source_target_pairs={{0,2},{2,0},{4,6},{6,4},{8,10},{10,8},{12,14},{14,12},{16,18},{18,... | collective-permute-start | bytes 663560 | tf_op jit(solution)/shard_map/ppermute | solution.py:19
  57.1 21.9 %collective-permute-start.30 = (bf16[192,2304]{1,0:T(8,128)(2,1)S(1)}, bf16[192,2304]{1,0:T(8,128)(2,1)S(1)}, u32[]{:S(2)}, u32[]{:S(2)}) collective-permute-start(bf16[192,2304]{1,0:T(8,128)(2,1)S(1)} %get-tuple-element.91), channel_id=1, source_target_pairs={{0,1},{1,0},{2,3},{3,2},{4,5},{5,4},{6,7},{7,6},{8,9},{9,8},{10,11... | collective-permute-start | bytes 2654216 | tf_op jit(solution)/shard_map/ppermute | solution.py:19
  57.9 6.3 %collective-permute-start.21 = (bf16[24,2304]{1,0:T(8,128)(2,1)S(1)}, bf16[24,2304]{1,0:T(8,128)(2,1)S(1)}, u32[]{:S(2)}, u32[]{:S(2)}) collective-permute-start(bf16[24,2304]{1,0:T(8,128)(2,1)S(1)} %get-tuple-element.82), channel_id=1, source_target_pairs={{0,8},{2,10},{4,12},{6,14},{8,0},{10,2},{12,4},{14,6},{16,24},{18,... | collective-permute-start | bytes 331784 | tf_op jit(solution)/shard_map/ppermute | solution.py:19
  58.1 10.7 %collective-permute-start.22 = (bf16[24,2304]{1,0:T(8,128)(2,1)S(1)}, bf16[24,2304]{1,0:T(8,128)(2,1)S(1)}, u32[]{:S(2)}, u32[]{:S(2)}) collective-permute-start(bf16[24,2304]{1,0:T(8,128)(2,1)S(1)} %get-tuple-element.83), channel_id=1, source_target_pairs={{0,16},{2,18},{4,20},{6,22},{8,24},{10,26},{12,28},{14,30},{16,0},... | collective-permute-start | bytes 331784 | tf_op jit(solution)/shard_map/ppermute | solution.py:19
  60.8 8.0 %collective-permute-start.23 = (bf16[24,2304]{1,0:T(8,128)(2,1)S(1)}, bf16[24,2304]{1,0:T(8,128)(2,1)S(1)}, u32[]{:S(2)}, u32[]{:S(2)}) collective-permute-start(bf16[24,2304]{1,0:T(8,128)(2,1)S(1)} %get-tuple-element.84), channel_id=1, source_target_pairs={{0,24},{2,26},{4,28},{6,30},{8,16},{10,18},{12,20},{14,22},{16,8},... | collective-permute-start | bytes 331784 | tf_op jit(solution)/shard_map/ppermute | solution.py:19
  62.3 10.1 %collective-permute-start.24 = (bf16[96,2304]{1,0:T(8,128)(2,1)S(1)}, bf16[96,2304]{1,0:T(8,128)(2,1)S(1)}, u32[]{:S(2)}, u32[]{:S(2)}) collective-permute-start(bf16[96,2304]{1,0:T(8,128)(2,1)S(1)} %get-tuple-element.85), channel_id=1, source_target_pairs={{0,4},{2,6},{4,0},{6,2},{8,12},{10,14},{12,8},{14,10},{16,20},{18,... | collective-permute-start | bytes 1327112 | tf_op jit(solution)/shard_map/ppermute | solution.py:19
  72.7 11.0 %collective-permute-start.25 = (bf16[48,2304]{1,0:T(8,128)(2,1)S(1)}, bf16[48,2304]{1,0:T(8,128)(2,1)S(1)}, u32[]{:S(2)}, u32[]{:S(2)}) collective-permute-start(bf16[48,2304]{1,0:T(8,128)(2,1)S(1)} %get-tuple-element.87), channel_id=1, source_target_pairs={{0,8},{2,10},{4,12},{6,14},{8,0},{10,2},{12,4},{14,6},{16,24},{18,... | collective-permute-start | bytes 663560 | tf_op jit(solution)/shard_map/ppermute | solution.py:19
  72.8 17.3 %collective-permute-start.26 = (bf16[48,2304]{1,0:T(8,128)(2,1)S(1)}, bf16[48,2304]{1,0:T(8,128)(2,1)S(1)}, u32[]{:S(2)}, u32[]{:S(2)}) collective-permute-start(bf16[48,2304]{1,0:T(8,128)(2,1)S(1)} %get-tuple-element.88), channel_id=1, source_target_pairs={{0,16},{2,18},{4,20},{6,22},{8,24},{10,26},{12,28},{14,30},{16,0},... | collective-permute-start | bytes 663560 | tf_op jit(solution)/shard_map/ppermute | solution.py:19
  75.6 14.4 %collective-permute-start.27 = (bf16[48,2304]{1,0:T(8,128)(2,1)S(1)}, bf16[48,2304]{1,0:T(8,128)(2,1)S(1)}, u32[]{:S(2)}, u32[]{:S(2)}) collective-permute-start(bf16[48,2304]{1,0:T(8,128)(2,1)S(1)} %get-tuple-element.89), channel_id=1, source_target_pairs={{0,24},{2,26},{4,28},{6,30},{8,16},{10,18},{12,20},{14,22},{16,8},... | collective-permute-start | bytes 663560 | tf_op jit(solution)/shard_map/ppermute | solution.py:19
  90.3 10.5 %collective-permute-start.31 = (bf16[192,2304]{1,0:T(8,128)(2,1)S(1)}, bf16[192,2304]{1,0:T(8,128)(2,1)S(1)}, u32[]{:S(2)}, u32[]{:S(2)}) collective-permute-start(bf16[192,2304]{1,0:T(8,128)(2,1)S(1)} %get-tuple-element.92.refs_0_.refs_18_), channel_id=1, source_target_pairs={{0,2},{2,0},{4,6},{6,4},{8,10},{10,8},{12,14},{14,12},{16,18},{18,... | collective-permute-start | bytes 2654216 | tf_op jit(solution)/shard_map/ppermute | solution.py:19
  91.0 17.0 %collective-permute-start.37 = (bf16[96,2304]{1,0:T(8,128)(2,1)S(1)}, bf16[96,2304]{1,0:T(8,128)(2,1)S(1)}, u32[]{:S(2)}, u32[]{:S(2)}) collective-permute-start(bf16[96,2304]{1,0:T(8,128)(2,1)S(1)} %get-tuple-element.96), channel_id=1, source_target_pairs={{0,1},{1,0},{2,3},{3,2},{4,5},{5,4},{6,7},{7,6},{8,9},{9,8},{10,11... | collective-permute-start | bytes 1327112 | tf_op jit(solution)/shard_map/ppermute | solution.py:19
  92.7 15.2 %collective-permute-start.36 = (bf16[96,2304]{1,0:T(8,128)(2,1)S(1)}, bf16[96,2304]{1,0:T(8,128)(2,1)S(1)}, u32[]{:S(2)}, u32[]{:S(2)}) collective-permute-start(bf16[96,2304]{1,0:T(8,128)(2,1)S(1)} %get-tuple-element.96), channel_id=1, source_target_pairs={{0,4},{2,6},{4,0},{6,2},{8,12},{10,14},{12,8},{14,10},{16,20},{18,... | collective-permute-start | bytes 1327112 | tf_op jit(solution)/shard_map/ppermute | solution.py:19
  94.2 8.7 %collective-permute-start.35 = (bf16[24,2304]{1,0:T(8,128)(2,1)S(1)}, bf16[24,2304]{1,0:T(8,128)(2,1)S(1)}, u32[]{:S(2)}, u32[]{:S(2)}) collective-permute-start(bf16[24,2304]{1,0:T(8,128)(2,1)S(1)} %error.1.refs_13_.refs_7_), channel_id=1, source_target_pairs={{0,24},{2,26},{4,28},{6,30},{8,16},{10,18},{12,20},{14,22},{16,8},... | collective-permute-start | bytes 331784 | tf_op jit(solution)/shard_map/ppermute | solution.py:19
  96.1 11.6 %collective-permute-start.34 = (bf16[24,2304]{1,0:T(8,128)(2,1)S(1)}, bf16[24,2304]{1,0:T(8,128)(2,1)S(1)}, u32[]{:S(2)}, u32[]{:S(2)}) collective-permute-start(bf16[24,2304]{1,0:T(8,128)(2,1)S(1)} %error.1.refs_13_.refs_7_), channel_id=1, source_target_pairs={{0,16},{2,18},{4,20},{6,22},{8,24},{10,26},{12,28},{14,30},{16,0},... | collective-permute-start | bytes 331784 | tf_op jit(solution)/shard_map/ppermute | solution.py:19
  100.7 7.2 %collective-permute-start.33 = (bf16[24,2304]{1,0:T(8,128)(2,1)S(1)}, bf16[24,2304]{1,0:T(8,128)(2,1)S(1)}, u32[]{:S(2)}, u32[]{:S(2)}) collective-permute-start(bf16[24,2304]{1,0:T(8,128)(2,1)S(1)} %error.1.refs_13_.refs_7_), channel_id=1, source_target_pairs={{0,8},{2,10},{4,12},{6,14},{8,0},{10,2},{12,4},{14,6},{16,24},{18,... | collective-permute-start | bytes 331784 | tf_op jit(solution)/shard_map/ppermute | solution.py:19
  108.2 15.0 %collective-permute-start.39 = (bf16[120,2304]{1,0:T(8,128)(2,1)S(1)}, bf16[120,2304]{1,0:T(8,128)(2,1)S(1)}, u32[]{:S(2)}, u32[]{:S(2)}) collective-permute-start(bf16[120,2304]{1,0:T(8,128)(2,1)S(1)} %get-tuple-element.100), channel_id=1, source_target_pairs={{0,4},{2,6},{4,0},{6,2},{8,12},{10,14},{12,8},{14,10},{16,20},{18,... | collective-permute-start | bytes 1658888 | tf_op jit(solution)/shard_map/ppermute | solution.py:19
  108.8 14.6 %collective-permute-start.40 = (bf16[120,2304]{1,0:T(8,128)(2,1)S(1)}, bf16[120,2304]{1,0:T(8,128)(2,1)S(1)}, u32[]{:S(2)}, u32[]{:S(2)}) collective-permute-start(bf16[120,2304]{1,0:T(8,128)(2,1)S(1)} %get-tuple-element.101), channel_id=1, source_target_pairs={{0,1},{1,0},{2,3},{3,2},{4,5},{5,4},{6,7},{7,6},{8,9},{9,8},{10,11... | collective-permute-start | bytes 1658888 | tf_op jit(solution)/shard_map/ppermute | solution.py:19
  123.6 6.6 %collective-permute-start.41 = (bf16[96,2304]{1,0:T(8,128)(2,1)S(1)}, bf16[96,2304]{1,0:T(8,128)(2,1)S(1)}, u32[]{:S(2)}, u32[]{:S(2)}) collective-permute-start(bf16[96,2304]{1,0:T(8,128)(2,1)S(1)} %get-tuple-element.99.refs_1_.refs_0_.refs_6_), channel_id=1, source_target_pairs={{0,2},{2,0},{4,6},{6,4},{8,10},{10,8},{12,14},{14,12},{16,18},{18,... | collective-permute-start | bytes 1327112 | tf_op jit(solution)/shard_map/ppermute | solution.py:19
  124.2 8.0 %collective-permute-start.44 = (bf16[48,2304]{1,0:T(8,128)(2,1)S(1)}, bf16[48,2304]{1,0:T(8,128)(2,1)S(1)}, u32[]{:S(2)}, u32[]{:S(2)}) collective-permute-start(bf16[48,2304]{1,0:T(8,128)(2,1)S(1)} %get-tuple-element.106), channel_id=1, source_target_pairs={{0,4},{2,6},{4,0},{6,2},{8,12},{10,14},{12,8},{14,10},{16,20},{18,... | collective-permute-start | bytes 663560 | tf_op jit(solution)/shard_map/ppermute | solution.py:19
  125.7 7.5 %collective-permute-start.45 = (bf16[48,2304]{1,0:T(8,128)(2,1)S(1)}, bf16[48,2304]{1,0:T(8,128)(2,1)S(1)}, u32[]{:S(2)}, u32[]{:S(2)}) collective-permute-start(bf16[48,2304]{1,0:T(8,128)(2,1)S(1)} %get-tuple-element.107), channel_id=1, source_target_pairs={{0,1},{1,0},{2,3},{3,2},{4,5},{5,4},{6,7},{7,6},{8,9},{9,8},{10,11... | collective-permute-start | bytes 663560 | tf_op jit(solution)/shard_map/ppermute | solution.py:19
  126.2 7.0 %collective-permute-start.46 = (bf16[96,2304]{1,0:T(8,128)(2,1)S(1)}, bf16[96,2304]{1,0:T(8,128)(2,1)S(1)}, u32[]{:S(2)}, u32[]{:S(2)}) collective-permute-start(bf16[96,2304]{1,0:T(8,128)(2,1)S(1)} %get-tuple-element.105.refs_4_.refs_12_), channel_id=1, source_target_pairs={{0,2},{2,0},{4,6},{6,4},{8,10},{10,8},{12,14},{14,12},{16,18},{18,... | collective-permute-start | bytes 1327112 | tf_op jit(solution)/shard_map/ppermute | solution.py:19
  (18 other events, 85.8 us)

commit v4 on v3

--- a/solution.py
+++ b/solution.py
@@ -127,11 +127,11 @@
         ins = ins[len(group):]
 
 
-def join(lists, after=()):
+def join(lists, after=(), flops=0):
     lists = [[p if isinstance(p, tuple) else (p, 0, p.shape[0]) for p in parts] for parts in lists]
     outs = [((sum(c for _, _, c in parts), parts[0][0].shape[1]), parts[0][0].dtype) for parts in lists]
     kernel = functools.partial(join_kernel, [[p[1:] for p in parts] for parts in lists])
-    return local(kernel, "join", [p[0] for parts in lists for p in parts], outs, after)
+    return local(kernel, "join", [p[0] for parts in lists for p in parts], outs, after, flops)
 
 
 def pair_kernel(keep, *refs):
@@ -231,12 +231,19 @@
     )
 
 
-def back_kernel(layers, counts, known, *refs):
+def some(part):
+    return part if isinstance(part, tuple) else (part, 0, part.shape[0])
+
+
+def back_kernel(layers, counts, parts, known, *refs):
     errors = []
     for count in counts:
         errors.append(cat([r[...] for r in refs[:count]]))
         refs = refs[count:]
-    pre, refs = refs[:layers], refs[layers:]
+    pre = []
+    for _ in range(layers):
+        pre.append(cat([r[...] for r in refs[:parts]]))
+        refs = refs[parts:]
     pairs = layers * (layers + 1) // 2
     weight, refs = refs[:pairs], refs[pairs:]
     early, refs = refs[:known], refs[known:]
@@ -246,23 +253,24 @@
         for t in range(max(s, layers - 1 if s < known else 0), layers):
             term = dot(errors[t], weight[pair_slot(s, t, layers)][0], ((1,), (1,)))
             value = term if value is None else value + term
-        value = (value * pre[s][...]).astype(out[s].dtype)
+        value = (value * pre[s]).astype(out[s].dtype)
         out[s][...] = value
         total[s] = jnp.sum(value.astype(jnp.float32), axis=0, keepdims=True)
 
 
 def back(errors, pre, weight, layers, resident, early=(), after=()):
     pairs, feats, width = weight.shape
-    m = pre[0].shape[0]
+    errors, pre = ([[some(p) for p in parts] for parts in lists] for lists in (errors, pre))
+    m = sum(count for _, _, count in pre[0])
     c = piece(feats, 256)
-    ins = [(e, e.shape, lambda j: (0, 0)) for t in range(layers) for e in errors[t]]
-    ins += [(p, (m, c), lambda j: (0, j)) for p in pre]
+    ins = [(e, (r, width), lambda j, i=i // r: (i, 0)) for parts in errors for e, i, r in parts]
+    ins += [(p, (r, c), lambda j, i=i // r: (i, j)) for parts in pre for p, i, r in parts]
     ins += [(weight, (1, c, width), lambda j, k=k: (k, j, 0)) for k in range(pairs)]
     ins += [(e, (m, c), lambda j: (0, j)) for e in early]
     outs = [((m, feats), jnp.bfloat16, (m, c), lambda j: (0, j))] * layers
     outs.append(((layers, 1, feats), jnp.float32, (layers, 1, c), lambda j: (0, 0, j)))
     got = call(
-        functools.partial(back_kernel, layers, [len(e) for e in errors], len(early)),
+        functools.partial(back_kernel, layers, [len(e) for e in errors], len(pre[0]), len(early)),
         "back",
         feats // c,
         ins,
@@ -351,43 +359,69 @@
     )[0]
 
 
-def grads_body(layers, scale, counts, own, *refs):
+def mine(size):
+    return pl.ds(pl.multiple_of(lax.axis_index("tok") * size, 128), size)
+
+
+def gathered(parts, size):
+    at = slice(None) if parts[0][0].shape[1] == size else mine(size)
+    return cat([p[start:start + count, at] for p, (start, count) in parts])
+
+
+def ahead_kernel(rows, own, *refs):
+    *ins, out = refs
+    count = len(rows[0])
+    left = gathered(list(zip(ins[:count], rows[0])), own)
+    right = gathered(list(zip(ins[count:], rows[1])), out.shape[1])
+    size = piece(right.shape[1], 768)
+    for j in range(right.shape[1] // size):
+        at = slice(j * size, (j + 1) * size)
+        out[:, at] = dot(left, right[:, at], ((0,), (0,)))
+
+
+def ahead(codes, errors, own):
+    lists = [[some(p) for p in parts] for parts in (codes, errors)]
+    rows = [[p[1:] for p in parts] for parts in lists]
+    arrays = [p[0] for parts in lists for p in parts]
+    out = ((own, arrays[-1].shape[1]), jnp.float32)
+    flops = 2 * math.prod(out[0]) * sum(r[1] for r in rows[0])
+    return local(functools.partial(ahead_kernel, rows, own), "ahead", arrays, [out], (), flops)[0]
+
+
+def grads_body(layers, scale, rows, own, late, *refs):
     lists = []
-    for count in counts:
-        lists.append([refs[s * count:(s + 1) * count] for s in range(layers)])
-        refs = refs[layers * count:]
+    for parts in rows:
+        lists.append([])
+        for bounds in parts:
+            lists[-1].append(list(zip(refs, bounds)))
+            refs = refs[len(bounds):]
     codes, errors, inputs, grads = lists
-    sums, refs = refs[:-7], refs[-7:]
+    early, sums, refs = refs[0], refs[1:-7], refs[-7:]
     dec_out, enc_out, bias_out, dec_held, enc_held, dec_sems, enc_sems = refs
     copies = []
-    me = lax.axis_index("tok")
-
-    def mine(size):
-        return pl.ds(pl.multiple_of(me * size, 128), size)
-
-    def leave(held, out, sems, slot, left, right):
+    def leave(held, out, sems, slot, left, right, before=None):
         width = right.shape[1]
         size = piece(width, 768)
         for j in range(width // size):
             value = dot(left, right[:, j * size:(j + 1) * size], ((0,), (0,)))
+            if before is not None:
+                value = value + before[:, j * size:(j + 1) * size]
             at = (slot, slice(None), slice(j * size, (j + 1) * size))
             held[at] = (value * scale).astype(held.dtype)
             copy = pltpu.make_async_copy(held.at[at], out.at[at], sems.at[slot, j])
             copy.start()
             copies.append(copy)
 
-    def columns(parts, size):
-        if parts[0].shape[1] == size:
-            return cat([p[...] for p in parts])
-        return cat([p[:, mine(size)] for p in parts])
-
     for s in range(layers):
-        left = columns(codes[s], own[0])
+        left = gathered(codes[s], own[0])
         for t in range(s, layers):
-            right = cat([e[...] for e in errors[t]])
-            leave(dec_held, dec_out, dec_sems, pair_slot(s, t, layers), left, right)
+            slot, before, first = pair_slot(s, t, layers), None, left
+            right = errors[t]
+            if slot == 0:
+                before, first, right = early, gathered(codes[s][-late:], own[0]), right[-late:]
+            leave(dec_held, dec_out, dec_sems, slot, first, gathered(right, dec_out.shape[2]), before)
     for s in range(layers):
-        leave(enc_held, enc_out, enc_sems, s, columns(inputs[s], own[1]), cat([g[...] for g in grads[s]]))
+        leave(enc_held, enc_out, enc_sems, s, gathered(inputs[s], own[1]), gathered(grads[s], enc_out.shape[2]))
         total = sums[0][s, :, mine(own[0])]
         for more in sums[1:]:
             total = total + more[s, :, mine(own[0])]
@@ -396,14 +430,15 @@
         copy.wait()
 
 
-def all_grads(codes, errors, inputs, grads, sums, own, scale, layers):
-    lists = (codes, errors, inputs, grads)
-    dec = (layers * (layers + 1) // 2, own[0], errors[0][0].shape[1])
-    enc = (layers, own[1], grads[0][0].shape[1])
-    arrays = [pltpu.with_memory_space_constraint(p, pltpu.VMEM) for parts in lists for s in parts for p in s]
-    arrays += [pltpu.with_memory_space_constraint(p, pltpu.VMEM) for p in sums]
+def all_grads(codes, errors, inputs, grads, early, late, sums, own, scale, layers):
+    lists = [[[some(p) for p in parts] for parts in each] for each in (codes, errors, inputs, grads)]
+    rows = [[[p[1:] for p in parts] for parts in each] for each in lists]
+    dec = (layers * (layers + 1) // 2, own[0], lists[1][0][0][0].shape[1])
+    enc = (layers, own[1], lists[3][0][0][0].shape[1])
+    arrays = [p[0] for each in lists for parts in each for p in parts] + [early, *sums]
+    arrays = [pltpu.with_memory_space_constraint(a, pltpu.VMEM) for a in arrays]
     return pl.pallas_call(
-        functools.partial(grads_body, layers, scale, [len(parts[0]) for parts in lists], own),
+        functools.partial(grads_body, layers, scale, rows, own, late),
         name="grads",
         out_shape=[
             jax.ShapeDtypeStruct(dec, jnp.bfloat16),
@@ -448,7 +483,7 @@
         own.append((part.astype(jnp.float32) - targets[:, t, :].astype(jnp.float32)).astype(jnp.bfloat16))
     for g in range(tok):
         errors.append([[gather(swap(e, "tok", g) if g else e)] for e in own])
-        d, total = back(errors[g], pre[g], dec_weight, layers, False)
+        d, total = back(errors[g], [[p] for p in pre[g]], dec_weight, layers, False)
         grads.append(d)
         sums.append(total)
     me = lax.axis_index("tok")
@@ -497,6 +532,15 @@
     def error(t, low, got, ends, after):
         arrays = [low, got, *ends, targets[:, t, :]]
         return local(functools.partial(error_kernel, n), "error", arrays, [small], after)[0]
+
+    def nears(parts):
+        return [(p, 0, quart) for p in parts]
+
+    def fars(parts):
+        return [(p, quart, quart) for p in parts]
+
+    def halves(value):
+        return [(value, k * quart, quart) for k in (0, 2)], [(value, k * quart, quart) for k in (1, 3)]
 
     acts = [acts_in[:, s, :] for s in range(layers)]
     ends = quart - n
@@ -510,31 +554,32 @@
     done = [*z_a1, x_s, y_s, dec_held]
     far0, far1 = [(x_s, ends, n), (x_s, 0, ends)], [(x_s, quart, n)]
     line1, col0 = join([z_a1, [acts[0], line0, *far0]], done)
-    y_l1, x_l1 = away(line1), across(line1)
+    x_l1 = across(line1)
     in0 = [col0, core(col0)]
     pre0, code0 = encoded(0, in0)
-    keep0, *give0 = decode(0, [0], [code0], dec_held, layers, (), True, True, (), 4)
-    early = decode(1, [0], [code0], dec_held, layers, (), False, True, (keep0,))
+    keep0, *give0 = decode(0, [0], [code0], dec_held, layers, (), True, True, (), 3)
     got0 = [core(g) for g in give0]
-    done = [x_l1, y_l1, *got0, *early]
+    done = [x_l1, *got0]
     low0, high0 = pair(keep0, got0, done)
     far1.append(x_l1)
-    col1, fars = join([[a1, line1, *far1], far0 + far1], done)
-    x_h0 = across(high0)
+    col1, far_both = join([[a1, line1, *far1], far0 + far1], done)
+    y_l1, x_h0 = away(line1), across(high0)
     in1 = [col1, core(col1)]
-    pre1, code1 = encoded(1, in1)
-    keep1, *give1 = decode(1, [1], [code0, code1], dec_held, layers, early, True, True, (), 4)
+    early = decode(1, [0], [code0], dec_held, layers, (), False, True, (low0, col1))
+    pre1, code1 = encoded(1, in1, early)
+    keep1, *give1 = decode(1, [1], [code0, code1], dec_held, layers, early, True, True, (), 3)
     got1 = [core(g) for g in give1]
-    done = [x_h0, *got1]
+    done = [x_h0, y_l1, *got1]
     body = functools.partial(open_kernel, n, len(line))
     *ends0, low1, high1 = local(body, "open", [low0, x_h0, keep1, *got1], [small] * len(line) + lows, done)
     z_r0 = along(ends0)
     x_h1 = across(high1)
     done = [*z_r0, x_h1]
-    arrays = [low0, x_h0, *z_r0, targets[:, 0, :], low1, x_h1]
+    target = join([[targets[:, 0, :]]], [low1], 2 * quart * width * feats)[0]
+    arrays = [low0, x_h0, *z_r0, target, low1, x_h1]
     shapes = [((2 * n, width), jnp.bfloat16)] * len(line) + [small]
     *turned, e0 = local(functools.partial(turn_kernel, n, len(line)), "turn", arrays, shapes, done)
-    y_f, y_e0, x_e0 = away(fars), away(e0), across(e0)
+    y_f, y_e0, x_e0 = away(far_both), away(e0), across(e0)
     z_t = along(turned)
     done = [*z_t, x_e0, y_e0, y_f]
     e1 = error(1, low1, x_h1, z_t, done)
@@ -548,50 +593,50 @@
     there_pre0, there_code0 = encoded(0, there_in0)
     there_pre1, there_code1 = encoded(1, there_in1)
     done = [*z_e1, x_b, y_b, there_code0, there_code1]
-    near_y0 = [y_e0, (y_b, 0, ends)]
-    half_y0 = [y_e0, (y_b, 0, hop - n)]
-    near1, whole0, near_y0, go_x, go_y = join(
+    near1, whole0, near_y0, send = join(
+        [[e1, *z_e1], [near0, x_e0, (x_b, 0, ends)], [y_e0, (y_b, 0, ends)], z_e1], done
+    )
+    y_g, x_g = away(send), across(send)
+    err0 = [whole0, core(whole0)]
+    near_err0 = [near_y0, core(near_y0)]
+    first_own = first(err0, dec_held)
+    first_near = first(near_err0, dec_held)
+    share = (feats // lax.axis_size("tok"), width // lax.axis_size("tok"))
+    early = ahead([code0] + halves(there_code0)[0], err0 + near_err0, share[0])
+    done = [x_g, y_g, first_own, first_near, early]
+    whole1, near_y1, go_x, go_y = join(
         [
-            [e1, *z_e1],
-            [near0, x_e0, (x_b, 0, ends)],
-            near_y0,
-            [*z_e1, *half_y0],
-            [*z_e1, (x_b, hop - n, quart - hop)],
+            [near1, (x_b, ends, n), x_g],
+            [(y_b, ends, n), y_g],
+            [(near_y0, 0, hop), (y_b, ends, n), (y_g, 0, hop - n)],
+            [(x_b, hop - n, quart - hop), (x_g, hop - n, quart - hop)],
         ],
         done,
     )
-    y_g, x_g = away(go_y), across(go_x)
-    err0 = [whole0, core(whole0)]
-    first_own = first(err0, dec_held)
-    done = [x_g, y_g, first_own]
-    whole1, one1, two1, near_y1, far_y0 = join(
-        [
-            [near1, (x_b, ends, n), (x_g, 0, ends)],
-            [(y_b, ends, n), (y_g, 0, hop - n)],
-            [(x_g, hop - n, quart - hop)],
-            [(y_b, ends, n), (y_g, 0, ends)],
-            [(x_g, ends, hop), (y_g, ends, quart - hop)],
-        ],
-        done,
-    )
-    y_t1, x_o1 = away(two1), across(one1)
+    y_t, x_o = away(go_y), across(go_x)
     err1 = [whole1, core(whole1)]
-    there_err0 = [near_y0, far_y0, core(near_y0), core(far_y0)]
-    core_n1 = core(near_y1)
-    grad_own, sum_own = back([err0, err1], [pre0, pre1], dec_held, layers, True, [first_own])
-    first_there = first(there_err0, dec_held, [grad_own[0]])
-    done = [x_o1, y_t1, core_n1, first_there]
-    far_y1 = join([[x_o1, y_t1]], done)[0]
-    there_err1 = [near_y1, far_y1, core_n1, core(far_y1)]
-    there_errs, there_pres = [there_err0, there_err1], [there_pre0, there_pre1]
-    grad_there, sum_there = back(there_errs, there_pres, dec_held, layers, True, [first_there])
+    near_err1 = [near_y1, core(near_y1)]
+
+    near_pre, far_pre = zip(halves(there_pre0), halves(there_pre1))
+    grad_own, sum_own = back([err0, err1], [[pre0], [pre1]], dec_held, layers, True, [first_own])
+    grad_near, sum_near = back([near_err0, near_err1], near_pre, dec_held, layers, True, [first_near])
+    done = [x_o, y_t, grad_own[0], grad_near[0]]
+    left = quart - hop
+    far = join([[(x_o, 0, hop), (y_t, 0, left), (x_o, hop, hop), (y_t, left, left)]], done)[0]
+    far = [far, core(far)]
+    far_errs = [nears(far), fars(far)]
+    grad_far, sum_far = back(far_errs, far_pre, dec_held, layers, True)
+    codes = [sum(halves(c), []) for c in (there_code0, there_code1)]
+    seen = [nears(p) + fars(p) for p in (there_in0, there_in1)]
     dec_out, enc_out, bias_out = all_grads(
-        [[code0, there_code0], [code1, there_code1]],
-        [err0 + there_err0, err1 + there_err1],
-        [in0 + there_in0, in1 + there_in1],
-        [[grad_own[s], grad_there[s]] for s in range(layers)],
-        [sum_own, sum_there],
-        (feats // lax.axis_size("tok"), width // lax.axis_size("tok")),
+        [[code0] + codes[0], [code1] + codes[1]],
+        [err0 + near_err0 + far_errs[0], err1 + near_err1 + far_errs[1]],
+        [in0 + seen[0], in1 + seen[1]],
+        [[grad_own[s], grad_near[s], grad_far[s]] for s in range(layers)],
+        early,
+        2,
+        [sum_own, sum_near, sum_far],
+        share,
         scale,
         layers,
     )

time: 151 us -> 148 us (0.980)
  Pallas kernels: 48.2 us -> 52.4 us
  starting transfers between devices: 45.4 us -> 41.5 us
  waiting for transfers between devices: 54.1 us -> 50.6 us
    pallas_call x23 -> x26, Pallas kernels: 28 us -> 33.6 us  [local(): pl.pallas_call(lambda *refs: kernel(*refs[skip:]), name=name, out_shape=[...]
    ppermute x48 -> x45, starting transfers between devices: 45.4 us -> 41.5 us  [swap(): lax.ppermute(value, axis, [(i, i ^ bits) for i in range(lax.axis_size(axi...]
    ppermute x48 -> x45, waiting for transfers between devices: 54.1 us -> 50.6 us  [swap(): lax.ppermute(value, axis, [(i, i ^ bits) for i in range(lax.axis_size(axi...]
  transfers between devices with their start and end apart: 48 -> 45, of which waited for: 20 -> 22; matrix products, arithmetic and copies ran while one was open for 0% -> 0% of each run, Pallas kernels for 21% -> 25%
where the time goes in v4:
time: 148 us
  Pallas kernels  52.4 us (35%)
  waiting for transfers between devices  50.6 us (34%)
  starting transfers between devices  41.5 us (28%)
  local copies, waits for them, and re-layouts  1.82 us (1%)
    ppermute x45, waiting for transfers between devices, swap(): lax.ppermute(value, axis, [(i, i ^ bits) for i in range(lax.axis_size(axi...  50.6 us
    ppermute x45, starting transfers between devices, swap(): lax.ppermute(value, axis, [(i, i ^ bits) for i in range(lax.axis_size(axi...  41.5 us
    pallas_call x26, Pallas kernels, local(): pl.pallas_call(lambda *refs: kernel(*refs[skip:]), name=name, out_shape=[...  33.6 us
    pallas_call x1, Pallas kernels, all_grads(): pl.pallas_call(functools.partial(grads_body, layers, scale, rows, own, la...  10 us
    pallas_call x2, Pallas kernels, load(): pl.pallas_call(lambda *refs: load_kernel(count, *refs[skip:]), name='load...  8.72 us
  transfers between devices with their start and end apart: 45, of which 22 were waited for; matrix products, arithmetic and copies ran while one was open for 0% of the time, Pallas kernels for 25%

profile of v4, /device:TPU:0, one launch (start us, length us, event | category | flops | bytes accessed | tf_op | source)
XLA Modules:
  0.0 147.6 jit_solution(7522797648152450901)
XLA Ops:
  2.1 3.1 %collective-permute-start = (bf16[24,2304]{1,0:T(8,128)(2,1)S(1)}, bf16[24,2304]{1,0:T(8,128)(2,1)S(1)}, u32[]{:S(2)}, u32[]{:S(2)}) collective-permute-start(bf16[24,2304]{1,0:T(8,128)(2,1)S(1)} %bitcast.14), channel_id=1, source_target_pairs={{0,8},{2,10},{4,12},{6,14},{8,0},{10,2},{12,4},{14,6},{16,24},{18,... | collective-permute-start | bytes 331784 | tf_op jit(solution)/shard_map/ppermute | solution.py:19
  5.2 2.6 %collective-permute-start.1 = (bf16[24,2304]{1,0:T(8,128)(2,1)S(1)}, bf16[24,2304]{1,0:T(8,128)(2,1)S(1)}, u32[]{:S(2)}, u32[]{:S(2)}) collective-permute-start(bf16[24,2304]{1,0:T(8,128)(2,1)S(1)} %bitcast.15), channel_id=1, source_target_pairs={{0,16},{2,18},{4,20},{6,22},{8,24},{10,26},{12,28},{14,30},{16,0},... | collective-permute-start | bytes 331784 | tf_op jit(solution)/shard_map/ppermute | solution.py:19
  7.8 3.7 %load.2.refs_3_.refs_2_ = bf16[2,2304,1024]{2,1,0:T(8,128)(2,1)S(1)} custom-call(bf16[2,2304,1024]{2,1,0:T(8,128)(2,1)} %refs_0_.1), custom_call_target="tpu_custom_call" | custom-call | tf_op jit(solution)/shard_map/load/pallas_call | solution.py:106
  11.5 5.0 %collective-permute-done.1.refs_1_.refs_5_.refs_8_ = bf16[24,2304]{1,0:T(8,128)(2,1)S(1)} collective-permute-done((bf16[24,2304]{1,0:T(8,128)(2,1)S(1)}, bf16[24,2304]{1,0:T(8,128)(2,1)S(1)}, u32[]{:S(2)}, u32[]{:S(2)}) %collective-permute-start.1) | collective-permute-done | bytes 110624 | tf_op jit(solution)/shard_map/ppermute | solution.py:19
  24.1 5.0 %load.3.refs_5_.refs_1_.refs_3_.refs_2_.refs_6_.refs_7_.refs_8_.refs_9_.refs_10_ = bf16[3,1024,2304]{2,1,0:T(8,128)(2,1)S(1)} custom-call(bf16[72,2304]{1,0:T(8,128)(2,1)S(1)} %get-tuple-element.63.refs_0_.refs_10_, bf16[3,1024,2304]{2,1,0:T(8,128)(2,1)} %refs_1_.1), custom_call_target="tpu_custom_call" | custom-call | tf_op jit(solution)/shard_map/load/pallas_call | solution.py:106
  29.2 1.8 %collective-permute-done.4.refs_1_.refs_7_ = bf16[24,2304]{1,0:T(8,128)(2,1)S(1)} collective-permute-done((bf16[24,2304]{1,0:T(8,128)(2,1)S(1)}, bf16[24,2304]{1,0:T(8,128)(2,1)S(1)}, u32[]{:S(2)}, u32[]{:S(2)}) %collective-permute-start.4) | collective-permute-done | bytes 110624 | tf_op jit(solution)/shard_map/ppermute | solution.py:19
  33.6 2.1 %encode.4 = (f32[384,1024]{1,0:T(8,128)S(1)}, bf16[384,1024]{1,0:T(8,128)(2,1)S(1)}) custom-call(bf16[192,2304]{1,0:T(8,128)(2,1)S(1)} %get-tuple-element.64.refs_0_.refs_22_, bf16[192,2304]{1,0:T(8,128)(2,1)S(1)} %collective-permute-done.8.refs_1_.refs_23_, bf16[2,2304,1024]{2,1,0:T(8,128)(2,1)S(1)} %load.2.refs_3_.refs_2_, ...), custom_call_target="tpu_custom_call" | custom-call | flops 1811939328 | tf_op jit(solution)/shard_map/encode/pallas_call | solution.py:57
  35.7 2.0 %decode.3 = (bf16[192,2304]{1,0:T(8,128)(2,1)S(1)}, bf16[64,2304]{1,0:T(8,128)(2,1)S(1)}, bf16[64,2304]{1,0:T(8,128)(2,1)S(1)}, bf16[64,2304]{1,0:T(8,128)(2,1)S(1)}) custom-call(bf16[384,1024]{1,0:T(8,128)(2,1)S(1)} %get-tuple-element.65.refs_0_.refs_2_, bf16[3,1024,2304]{2,1,0:T(8,128)(2,1)S(1)} %load.3.refs_5_.refs_1_.refs_3_.refs_2_.refs_6_.refs_7_.refs_8_.refs_9_.refs_10_), custom_call_target="tpu_custom_call" | custom-call | flops 1811939328 | tf_op jit(solution)/shard_map/decode/pallas_call | solution.py:57
  38.4 3.0 %collective-permute-done.9.refs_0_.refs_7_.refs_11_ = bf16[72,2304]{1,0:T(8,128)(2,1)S(1)} collective-permute-done((bf16[72,2304]{1,0:T(8,128)(2,1)S(1)}, bf16[72,2304]{1,0:T(8,128)(2,1)S(1)}, u32[]{:S(2)}, u32[]{:S(2)}) %collective-permute-start.9) | collective-permute-done | bytes 331808 | tf_op jit(solution)/shard_map/ppermute | solution.py:19
  43.0 2.0 %decode.4.refs_0_.refs_2_ = f32[384,2304]{1,0:T(8,128)S(1)} custom-call(f32[96,2304]{1,0:T(8,128)S(1)} %get-tuple-element.72.refs_0_.refs_5_.refs_4_, bf16[192,2304]{1,0:T(8,128)(2,1)S(1)} %get-tuple-element.73.refs_1_.refs_28_, bf16[384,1024]{1,0:T(8,128)(2,1)S(1)} %get-tuple-element.65.refs_0_.refs_2_, ...), custom_call_target="tpu_custom_call" | custom-call | flops 1811939328 | tf_op jit(solution)/shard_map/decode/pallas_call | solution.py:57
  45.0 2.0 %encode.5 = (f32[384,1024]{1,0:T(8,128)S(1)}, bf16[384,1024]{1,0:T(8,128)(2,1)S(1)}) custom-call(f32[384,2304]{1,0:T(8,128)S(1)} %decode.4.refs_0_.refs_2_, bf16[192,2304]{1,0:T(8,128)(2,1)S(1)} %get-tuple-element.73.refs_1_.refs_28_, bf16[192,2304]{1,0:T(8,128)(2,1)S(1)} %collective-permute-done.15.refs_2_.refs_29_, ...), custom_call_target="tpu_custom_call" | custom-call | flops 1811939328 | tf_op jit(solution)/shard_map/encode/pallas_call | solution.py:57
  47.1 2.0 %decode.5 = (bf16[192,2304]{1,0:T(8,128)(2,1)S(1)}, bf16[64,2304]{1,0:T(8,128)(2,1)S(1)}, bf16[64,2304]{1,0:T(8,128)(2,1)S(1)}, bf16[64,2304]{1,0:T(8,128)(2,1)S(1)}) custom-call(bf16[384,1024]{1,0:T(8,128)(2,1)S(1)} %get-tuple-element.74.refs_0_.refs_5_, ...), custom_call_target="tpu_custom_call" | custom-call | flops 1811939328 | tf_op jit(solution)/shard_map/decode/pallas_call | solution.py:57
  49.8 2.1 %collective-permute-done.14.refs_1_.refs_10_ = bf16[72,2304]{1,0:T(8,128)(2,1)S(1)} collective-permute-done((bf16[72,2304]{1,0:T(8,128)(2,1)S(1)}, bf16[72,2304]{1,0:T(8,128)(2,1)S(1)}, u32[]{:S(2)}, u32[]{:S(2)}) %collective-permute-start.14) | collective-permute-done | bytes 331808 | tf_op jit(solution)/shard_map/ppermute | solution.py:19
  52.4 2.3 %collective-permute-done.13.refs_0_.refs_6_.refs_5_ = bf16[96,2304]{1,0:T(8,128)(2,1)S(1)} collective-permute-done((bf16[96,2304]{1,0:T(8,128)(2,1)S(1)}, bf16[96,2304]{1,0:T(8,128)(2,1)S(1)}, u32[]{:S(2)}, u32[]{:S(2)}) %collective-permute-start.13) | collective-permute-done | bytes 442400 | tf_op jit(solution)/shard_map/ppermute | solution.py:19
  55.0 2.8 %collective-permute-start.19 = (bf16[24,2304]{1,0:T(8,128)(2,1)S(1)}, bf16[24,2304]{1,0:T(8,128)(2,1)S(1)}, u32[]{:S(2)}, u32[]{:S(2)}) collective-permute-start(bf16[24,2304]{1,0:T(8,128)(2,1)S(1)} %get-tuple-element.79), channel_id=1, source_target_pairs={{0,8},{2,10},{4,12},{6,14},{8,0},{10,2},{12,4},{14,6},{16,24},{18,... | collective-permute-start | bytes 331784 | tf_op jit(solution)/shard_map/ppermute | solution.py:19
  61.6 7.0 %collective-permute-done.20.refs_1_.refs_7_ = bf16[24,2304]{1,0:T(8,128)(2,1)S(1)} collective-permute-done((bf16[24,2304]{1,0:T(8,128)(2,1)S(1)}, bf16[24,2304]{1,0:T(8,128)(2,1)S(1)}, u32[]{:S(2)}, u32[]{:S(2)}) %collective-permute-start.20) | collective-permute-done | bytes 110624 | tf_op jit(solution)/shard_map/ppermute | solution.py:19
  68.6 2.5 %collective-permute-done.22.refs_3_.refs_11_.refs_7_ = bf16[96,2304]{1,0:T(8,128)(2,1)S(1)} collective-permute-done((bf16[96,2304]{1,0:T(8,128)(2,1)S(1)}, bf16[96,2304]{1,0:T(8,128)(2,1)S(1)}, u32[]{:S(2)}, u32[]{:S(2)}) %collective-permute-start.22) | collective-permute-done | bytes 442400 | tf_op jit(solution)/shard_map/ppermute | solution.py:19
  72.1 2.3 %collective-permute-start.24 = (bf16[48,2304]{1,0:T(8,128)(2,1)S(1)}, bf16[48,2304]{1,0:T(8,128)(2,1)S(1)}, u32[]{:S(2)}, u32[]{:S(2)}) collective-permute-start(bf16[48,2304]{1,0:T(8,128)(2,1)S(1)} %get-tuple-element.85), channel_id=1, source_target_pairs={{0,16},{2,18},{4,20},{6,22},{8,24},{10,26},{12,28},{14,30},{16,0},... | collective-permute-start | bytes 663560 | tf_op jit(solution)/shard_map/ppermute | solution.py:19
  76.9 3.7 %collective-permute-done.26.refs_3_.refs_12_ = bf16[24,2304]{1,0:T(8,128)(2,1)S(1)} collective-permute-done((bf16[24,2304]{1,0:T(8,128)(2,1)S(1)}, bf16[24,2304]{1,0:T(8,128)(2,1)S(1)}, u32[]{:S(2)}, u32[]{:S(2)}) %collective-permute-start.26) | collective-permute-done | bytes 110624 | tf_op jit(solution)/shard_map/ppermute | solution.py:19
  81.2 8.4 %collective-permute-done.24.refs_1_.refs_9_.refs_8_.refs_11_ = bf16[48,2304]{1,0:T(8,128)(2,1)S(1)} collective-permute-done((bf16[48,2304]{1,0:T(8,128)(2,1)S(1)}, bf16[48,2304]{1,0:T(8,128)(2,1)S(1)}, u32[]{:S(2)}, u32[]{:S(2)}) %collective-permute-start.24) | collective-permute-done | bytes 221216 | tf_op jit(solution)/shard_map/ppermute | solution.py:19
  91.6 2.9 %collective-permute-start.31 = (bf16[24,2304]{1,0:T(8,128)(2,1)S(1)}, bf16[24,2304]{1,0:T(8,128)(2,1)S(1)}, u32[]{:S(2)}, u32[]{:S(2)}) collective-permute-start(bf16[24,2304]{1,0:T(8,128)(2,1)S(1)} %error.1.refs_13_.refs_7_), channel_id=1, source_target_pairs={{0,8},{2,10},{4,12},{6,14},{8,0},{10,2},{12,4},{14,6},{16,24},{18,... | collective-permute-start | bytes 331784 | tf_op jit(solution)/shard_map/ppermute | solution.py:19
  96.2 2.0 %encode.6 = (f32[384,1024]{1,0:T(8,128)S(1)}, bf16[384,1024]{1,0:T(8,128)(2,1)S(1)}) custom-call(bf16[192,2304]{1,0:T(8,128)(2,1)S(1)} %get-tuple-element.89.refs_0_.refs_24_.refs_26_, bf16[192,2304]{1,0:T(8,128)(2,1)S(1)} %collective-permute-done.29.refs_1_.refs_25_.refs_27_, bf16[2,2304,1024]{2,1,0:T(8,128)(2,1)S(1)} %load.2.refs_3_.refs_2_, ...), custom_call_target="tpu_custom_call" | custom-call | flops 1811939328 | tf_op jit(solution)/shard_map/encode/pallas_call | solution.py:57
  99.6 2.0 %encode.7 = (f32[384,1024]{1,0:T(8,128)S(1)}, bf16[384,1024]{1,0:T(8,128)(2,1)S(1)}) custom-call(bf16[192,2304]{1,0:T(8,128)(2,1)S(1)} %get-tuple-element.91.refs_0_.refs_30_.refs_32_, bf16[192,2304]{1,0:T(8,128)(2,1)S(1)} %collective-permute-done.30.refs_1_.refs_31_.refs_33_, bf16[2,2304,1024]{2,1,0:T(8,128)(2,1)S(1)} %load.2.refs_3_.refs_2_, ...), custom_call_target="tpu_custom_call" | custom-call | flops 1811939328 | tf_op jit(solution)/shard_map/encode/pallas_call | solution.py:57
  102.2 2.9 %collective-permute-done.33.refs_2_.refs_10_.refs_18_ = bf16[24,2304]{1,0:T(8,128)(2,1)S(1)} collective-permute-done((bf16[24,2304]{1,0:T(8,128)(2,1)S(1)}, bf16[24,2304]{1,0:T(8,128)(2,1)S(1)}, u32[]{:S(2)}, u32[]{:S(2)}) %collective-permute-start.33) | collective-permute-done | bytes 110624 | tf_op jit(solution)/shard_map/ppermute | solution.py:19
  110.0 2.1 %ahead.1.refs_4_.refs_40_ = f32[512,2304]{1,0:T(8,128)S(1)} custom-call(bf16[384,1024]{1,0:T(8,128)(2,1)S(1)} %get-tuple-element.65.refs_0_.refs_2_, bf16[384,1024]{1,0:T(8,128)(2,1)S(1)} %get-tuple-element.90.refs_5_.refs_1_.refs_2_.refs_3_.refs_4_, bf16[384,1024]{1,0:T(8,128)(2,1)S(1)} %get-tuple-element.90.refs_5_.refs_1_.refs_2_.refs_3_.refs_4_, ...), custom_call_target="tpu_custom_call" | custom-call | flops 1358954496 | tf_op jit(solution)/shard_map/ahead/pallas_call | solution.py:57
  112.1 2.0 %first.2.refs_2_.refs_9_ = f32[384,1024]{1,0:T(8,128)S(1)} custom-call(bf16[192,2304]{1,0:T(8,128)(2,1)S(1)} %get-tuple-element.95.refs_0_.refs_3_.refs_10_, bf16[192,2304]{1,0:T(8,128)(2,1)S(1)} %collective-permute-done.36.refs_1_.refs_4_.refs_11_, bf16[3,1024,2304]{2,1,0:T(8,128)(2,1)S(1)} %load.3.refs_5_.refs_1_.refs_3_.refs_2_.refs_6_.refs_7_.refs_8_.refs_9_.refs_10_), custom_call_target="tpu_custom_call" | custom-call | flops 1811939328 | tf_op jit(solution)/shard_map/first/pallas_call | solution.py:57
  119.5 3.2 %back.4 = (bf16[192,1024]{1,0:T(8,128)(2,1)S(1)}, bf16[192,1024]{1,0:T(8,128)(2,1)S(1)}, f32[2,1,1024]{2,1,0:T(1,128)S(1)}) custom-call(bf16[96,2304]{1,0:T(8,128)(2,1)S(1)} %get-tuple-element.96.refs_0_.refs_5_.refs_10_.refs_12_, bf16[96,2304]{1,0:T(8,128)(2,1)S(1)} %collective-permute-done.37.refs_1_.refs_6_.refs_13_, ...), custom_call_target="tpu_custom_call" | custom-call | flops 1811939328 | tf_op jit(solution)/shard_map/back/pallas_call | solution.py:57
  122.8 3.9 %back.3 = (bf16[384,1024]{1,0:T(8,128)(2,1)S(1)}, bf16[384,1024]{1,0:T(8,128)(2,1)S(1)}, f32[2,1,1024]{2,1,0:T(1,128)S(1)}) custom-call(bf16[192,2304]{1,0:T(8,128)(2,1)S(1)} %get-tuple-element.95.refs_0_.refs_3_.refs_10_, bf16[192,2304]{1,0:T(8,128)(2,1)S(1)} %collective-permute-done.36.refs_1_.refs_4_.refs_11_, ...), custom_call_target="tpu_custom_call" | custom-call | flops 3623878656 | tf_op jit(solution)/shard_map/back/pallas_call | solution.py:57
  126.7 2.4 %collective-permute-done.40.refs_0_.refs_4_.refs_6_ = bf16[96,2304]{1,0:T(8,128)(2,1)S(1)} collective-permute-done((bf16[96,2304]{1,0:T(8,128)(2,1)S(1)}, bf16[96,2304]{1,0:T(8,128)(2,1)S(1)}, u32[]{:S(2)}, u32[]{:S(2)}) %collective-permute-start.40) | collective-permute-done | bytes 442400 | tf_op jit(solution)/shard_map/ppermute | solution.py:19
  130.1 2.4 %collective-permute-done.44.refs_1_.refs_3_.refs_15_.refs_21_ = bf16[192,2304]{1,0:T(8,128)(2,1)S(1)} collective-permute-done((bf16[192,2304]{1,0:T(8,128)(2,1)S(1)}, bf16[192,2304]{1,0:T(8,128)(2,1)S(1)}, u32[]{:S(2)}, u32[]{:S(2)}) %collective-permute-start.44) | collective-permute-done | bytes 884768 | tf_op jit(solution)/shard_map/ppermute | solution.py:19
  132.5 4.9 %back.5 = (bf16[192,1024]{1,0:T(8,128)(2,1)S(1)}, bf16[192,1024]{1,0:T(8,128)(2,1)S(1)}, f32[2,1,1024]{2,1,0:T(1,128)S(1)}) custom-call(bf16[192,2304]{1,0:T(8,128)(2,1)S(1)} %join.17.refs_0_.refs_2_.refs_14_.refs_20_, bf16[192,2304]{1,0:T(8,128)(2,1)S(1)} %collective-permute-done.44.refs_1_.refs_3_.refs_15_.refs_21_, ...), custom_call_target="tpu_custom_call" | custom-call | flops 2717908992 | tf_op jit(solution)/shard_map/back/pallas_call | solution.py:57
  137.4 10.0 %grads.1 = (bf16[3,512,2304]{2,1,0:T(8,128)(2,1)}, bf16[2,1152,1024]{2,1,0:T(8,128)(2,1)}, f32[2,512]{1,0:T(2,128)}) custom-call(bf16[384,1024]{1,0:T(8,128)(2,1)S(1)} %get-tuple-element.65.refs_0_.refs_2_, bf16[384,1024]{1,0:T(8,128)(2,1)S(1)} %get-tuple-element.90.refs_5_.refs_1_.refs_2_.refs_3_.refs_4_, ...), custom_call_target="tpu_custom_call" | custom-call | tf_op jit(solution)/shard_map/grads/pallas_call | solution.py:440
  (98 shorter events, 39.9 us)
Async XLA Ops:
  2.1 9.4 %collective-permute-start = (bf16[24,2304]{1,0:T(8,128)(2,1)S(1)}, bf16[24,2304]{1,0:T(8,128)(2,1)S(1)}, u32[]{:S(2)}, u32[]{:S(2)}) collective-permute-start(bf16[24,2304]{1,0:T(8,128)(2,1)S(1)} %bitcast.14), channel_id=1, source_target_pairs={{0,8},{2,10},{4,12},{6,14},{8,0},{10,2},{12,4},{14,6},{16,24},{18,... | collective-permute-start | bytes 331784 | tf_op jit(solution)/shard_map/ppermute | solution.py:19
  5.2 11.3 %collective-permute-start.1 = (bf16[24,2304]{1,0:T(8,128)(2,1)S(1)}, bf16[24,2304]{1,0:T(8,128)(2,1)S(1)}, u32[]{:S(2)}, u32[]{:S(2)}) collective-permute-start(bf16[24,2304]{1,0:T(8,128)(2,1)S(1)} %bitcast.15), channel_id=1, source_target_pairs={{0,16},{2,18},{4,20},{6,22},{8,24},{10,26},{12,28},{14,30},{16,0},... | collective-permute-start | bytes 331784 | tf_op jit(solution)/shard_map/ppermute | solution.py:19
  7.8 8.8 %collective-permute-start.2 = (bf16[24,2304]{1,0:T(8,128)(2,1)S(1)}, bf16[24,2304]{1,0:T(8,128)(2,1)S(1)}, u32[]{:S(2)}, u32[]{:S(2)}) collective-permute-start(bf16[24,2304]{1,0:T(8,128)(2,1)S(1)} %bitcast.16), channel_id=1, source_target_pairs={{0,24},{2,26},{4,28},{6,30},{8,16},{10,18},{12,20},{14,22},{16,8},... | collective-permute-start | bytes 331784 | tf_op jit(solution)/shard_map/ppermute | solution.py:19
  16.6 14.4 %collective-permute-start.6 = (bf16[120,2304]{1,0:T(8,128)(2,1)S(1)}, bf16[120,2304]{1,0:T(8,128)(2,1)S(1)}, u32[]{:S(2)}, u32[]{:S(2)}) collective-permute-start(bf16[120,2304]{1,0:T(8,128)(2,1)S(1)} %get-tuple-element.62), channel_id=1, source_target_pairs={{0,4},{2,6},{4,0},{6,2},{8,12},{10,14},{12,8},{14,10},{16,20},{18,... | collective-permute-start | bytes 1658888 | tf_op jit(solution)/shard_map/ppermute | solution.py:19
  18.2 12.8 %collective-permute-start.7 = (bf16[120,2304]{1,0:T(8,128)(2,1)S(1)}, bf16[120,2304]{1,0:T(8,128)(2,1)S(1)}, u32[]{:S(2)}, u32[]{:S(2)}) collective-permute-start(bf16[120,2304]{1,0:T(8,128)(2,1)S(1)} %get-tuple-element.62), channel_id=1, source_target_pairs={{0,1},{1,0},{2,3},{3,2},{4,5},{5,4},{6,7},{7,6},{8,9},{9,8},{10,11... | collective-permute-start | bytes 1658888 | tf_op jit(solution)/shard_map/ppermute | solution.py:19
  19.7 9.4 %collective-permute-start.3 = (bf16[24,2304]{1,0:T(8,128)(2,1)S(1)}, bf16[24,2304]{1,0:T(8,128)(2,1)S(1)}, u32[]{:S(2)}, u32[]{:S(2)}) collective-permute-start(bf16[24,2304]{1,0:T(8,128)(2,1)S(1)} %get-tuple-element.61.refs_4_), channel_id=1, source_target_pairs={{0,8},{2,10},{4,12},{6,14},{8,0},{10,2},{12,4},{14,6},{16,24},{18,... | collective-permute-start | bytes 331784 | tf_op jit(solution)/shard_map/ppermute | solution.py:19
  21.5 9.5 %collective-permute-start.4 = (bf16[24,2304]{1,0:T(8,128)(2,1)S(1)}, bf16[24,2304]{1,0:T(8,128)(2,1)S(1)}, u32[]{:S(2)}, u32[]{:S(2)}) collective-permute-start(bf16[24,2304]{1,0:T(8,128)(2,1)S(1)} %get-tuple-element.61.refs_4_), channel_id=1, source_target_pairs={{0,16},{2,18},{4,20},{6,22},{8,24},{10,26},{12,28},{14,30},{16,0},... | collective-permute-start | bytes 331784 | tf_op jit(solution)/shard_map/ppermute | solution.py:19
  22.7 8.2 %collective-permute-start.5 = (bf16[24,2304]{1,0:T(8,128)(2,1)S(1)}, bf16[24,2304]{1,0:T(8,128)(2,1)S(1)}, u32[]{:S(2)}, u32[]{:S(2)}) collective-permute-start(bf16[24,2304]{1,0:T(8,128)(2,1)S(1)} %get-tuple-element.61.refs_4_), channel_id=1, source_target_pairs={{0,24},{2,26},{4,28},{6,30},{8,16},{10,18},{12,20},{14,22},{16,8},... | collective-permute-start | bytes 331784 | tf_op jit(solution)/shard_map/ppermute | solution.py:19
  31.2 10.3 %collective-permute-start.9 = (bf16[72,2304]{1,0:T(8,128)(2,1)S(1)}, bf16[72,2304]{1,0:T(8,128)(2,1)S(1)}, u32[]{:S(2)}, u32[]{:S(2)}) collective-permute-start(bf16[72,2304]{1,0:T(8,128)(2,1)S(1)} %get-tuple-element.66.refs_5_), channel_id=1, source_target_pairs={{0,4},{2,6},{4,0},{6,2},{8,12},{10,14},{12,8},{14,10},{16,20},{18,... | collective-permute-start | bytes 995336 | tf_op jit(solution)/shard_map/ppermute | solution.py:19
  41.7 10.2 %collective-permute-start.14 = (bf16[72,2304]{1,0:T(8,128)(2,1)S(1)}, bf16[72,2304]{1,0:T(8,128)(2,1)S(1)}, u32[]{:S(2)}, u32[]{:S(2)}) collective-permute-start(bf16[72,2304]{1,0:T(8,128)(2,1)S(1)} %get-tuple-element.66.refs_5_), channel_id=1, source_target_pairs={{0,1},{1,0},{2,3},{3,2},{4,5},{5,4},{6,7},{7,6},{8,9},{9,8},{10,11... | collective-permute-start | bytes 995336 | tf_op jit(solution)/shard_map/ppermute | solution.py:19
  42.4 12.3 %collective-permute-start.13 = (bf16[96,2304]{1,0:T(8,128)(2,1)S(1)}, bf16[96,2304]{1,0:T(8,128)(2,1)S(1)}, u32[]{:S(2)}, u32[]{:S(2)}) collective-permute-start(bf16[96,2304]{1,0:T(8,128)(2,1)S(1)} %get-tuple-element.71), channel_id=1, source_target_pairs={{0,4},{2,6},{4,0},{6,2},{8,12},{10,14},{12,8},{14,10},{16,20},{18,... | collective-permute-start | bytes 1327112 | tf_op jit(solution)/shard_map/ppermute | solution.py:19
  49.1 5.6 %collective-permute-start.16 = (bf16[64,2304]{1,0:T(8,128)(2,1)S(1)}, bf16[64,2304]{1,0:T(8,128)(2,1)S(1)}, u32[]{:S(2)}, u32[]{:S(2)}) collective-permute-start(bf16[64,2304]{1,0:T(8,128)(2,1)S(1)} %get-tuple-element.75), channel_id=1, source_target_pairs={{0,2},{2,0},{4,6},{6,4},{8,10},{10,8},{12,14},{14,12},{16,18},{18,... | collective-permute-start | bytes 884744 | tf_op jit(solution)/shard_map/ppermute | solution.py:19
  49.2 5.5 %collective-permute-start.17 = (bf16[64,2304]{1,0:T(8,128)(2,1)S(1)}, bf16[64,2304]{1,0:T(8,128)(2,1)S(1)}, u32[]{:S(2)}, u32[]{:S(2)}) collective-permute-start(bf16[64,2304]{1,0:T(8,128)(2,1)S(1)} %get-tuple-element.76), channel_id=1, source_target_pairs={{0,2},{2,0},{4,6},{6,4},{8,10},{10,8},{12,14},{14,12},{16,18},{18,... | collective-permute-start | bytes 884744 | tf_op jit(solution)/shard_map/ppermute | solution.py:19
  51.9 24.5 %collective-permute-start.28 = (bf16[192,2304]{1,0:T(8,128)(2,1)S(1)}, bf16[192,2304]{1,0:T(8,128)(2,1)S(1)}, u32[]{:S(2)}, u32[]{:S(2)}) collective-permute-start(bf16[192,2304]{1,0:T(8,128)(2,1)S(1)} %get-tuple-element.88), channel_id=1, source_target_pairs={{0,1},{1,0},{2,3},{3,2},{4,5},{5,4},{6,7},{7,6},{8,9},{9,8},{10,11... | collective-permute-start | bytes 2654216 | tf_op jit(solution)/shard_map/ppermute | solution.py:19
  55.0 6.6 %collective-permute-start.19 = (bf16[24,2304]{1,0:T(8,128)(2,1)S(1)}, bf16[24,2304]{1,0:T(8,128)(2,1)S(1)}, u32[]{:S(2)}, u32[]{:S(2)}) collective-permute-start(bf16[24,2304]{1,0:T(8,128)(2,1)S(1)} %get-tuple-element.79), channel_id=1, source_target_pairs={{0,8},{2,10},{4,12},{6,14},{8,0},{10,2},{12,4},{14,6},{16,24},{18,... | collective-permute-start | bytes 331784 | tf_op jit(solution)/shard_map/ppermute | solution.py:19
  57.7 10.9 %collective-permute-start.20 = (bf16[24,2304]{1,0:T(8,128)(2,1)S(1)}, bf16[24,2304]{1,0:T(8,128)(2,1)S(1)}, u32[]{:S(2)}, u32[]{:S(2)}) collective-permute-start(bf16[24,2304]{1,0:T(8,128)(2,1)S(1)} %get-tuple-element.80), channel_id=1, source_target_pairs={{0,16},{2,18},{4,20},{6,22},{8,24},{10,26},{12,28},{14,30},{16,0},... | collective-permute-start | bytes 331784 | tf_op jit(solution)/shard_map/ppermute | solution.py:19
  58.9 9.7 %collective-permute-start.21 = (bf16[24,2304]{1,0:T(8,128)(2,1)S(1)}, bf16[24,2304]{1,0:T(8,128)(2,1)S(1)}, u32[]{:S(2)}, u32[]{:S(2)}) collective-permute-start(bf16[24,2304]{1,0:T(8,128)(2,1)S(1)} %get-tuple-element.81), channel_id=1, source_target_pairs={{0,24},{2,26},{4,28},{6,30},{8,16},{10,18},{12,20},{14,22},{16,8},... | collective-permute-start | bytes 331784 | tf_op jit(solution)/shard_map/ppermute | solution.py:19
  60.3 10.8 %collective-permute-start.22 = (bf16[96,2304]{1,0:T(8,128)(2,1)S(1)}, bf16[96,2304]{1,0:T(8,128)(2,1)S(1)}, u32[]{:S(2)}, u32[]{:S(2)}) collective-permute-start(bf16[96,2304]{1,0:T(8,128)(2,1)S(1)} %get-tuple-element.82), channel_id=1, source_target_pairs={{0,4},{2,6},{4,0},{6,2},{8,12},{10,14},{12,8},{14,10},{16,20},{18,... | collective-permute-start | bytes 1327112 | tf_op jit(solution)/shard_map/ppermute | solution.py:19
  71.4 9.8 %collective-permute-start.23 = (bf16[48,2304]{1,0:T(8,128)(2,1)S(1)}, bf16[48,2304]{1,0:T(8,128)(2,1)S(1)}, u32[]{:S(2)}, u32[]{:S(2)}) collective-permute-start(bf16[48,2304]{1,0:T(8,128)(2,1)S(1)} %get-tuple-element.84), channel_id=1, source_target_pairs={{0,8},{2,10},{4,12},{6,14},{8,0},{10,2},{12,4},{14,6},{16,24},{18,... | collective-permute-start | bytes 663560 | tf_op jit(solution)/shard_map/ppermute | solution.py:19
  72.1 17.4 %collective-permute-start.24 = (bf16[48,2304]{1,0:T(8,128)(2,1)S(1)}, bf16[48,2304]{1,0:T(8,128)(2,1)S(1)}, u32[]{:S(2)}, u32[]{:S(2)}) collective-permute-start(bf16[48,2304]{1,0:T(8,128)(2,1)S(1)} %get-tuple-element.85), channel_id=1, source_target_pairs={{0,16},{2,18},{4,20},{6,22},{8,24},{10,26},{12,28},{14,30},{16,0},... | collective-permute-start | bytes 663560 | tf_op jit(solution)/shard_map/ppermute | solution.py:19
  74.5 15.1 %collective-permute-start.25 = (bf16[48,2304]{1,0:T(8,128)(2,1)S(1)}, bf16[48,2304]{1,0:T(8,128)(2,1)S(1)}, u32[]{:S(2)}, u32[]{:S(2)}) collective-permute-start(bf16[48,2304]{1,0:T(8,128)(2,1)S(1)} %get-tuple-element.86), channel_id=1, source_target_pairs={{0,24},{2,26},{4,28},{6,30},{8,16},{10,18},{12,20},{14,22},{16,8},... | collective-permute-start | bytes 663560 | tf_op jit(solution)/shard_map/ppermute | solution.py:19
  89.8 8.5 %collective-permute-start.30 = (bf16[192,2304]{1,0:T(8,128)(2,1)S(1)}, bf16[192,2304]{1,0:T(8,128)(2,1)S(1)}, u32[]{:S(2)}, u32[]{:S(2)}) collective-permute-start(bf16[192,2304]{1,0:T(8,128)(2,1)S(1)} %get-tuple-element.91.refs_0_.refs_30_.refs_32_), channel_id=1, source_target_pairs={{0,2},{2,0},{4,6},{6,4},{8,10},{10,8},{12,14},{14,12},{16,18},{18,... | collective-permute-start | bytes 2654216 | tf_op jit(solution)/shard_map/ppermute | solution.py:19
  90.4 14.6 %collective-permute-start.34 = (bf16[96,2304]{1,0:T(8,128)(2,1)S(1)}, bf16[96,2304]{1,0:T(8,128)(2,1)S(1)}, u32[]{:S(2)}, u32[]{:S(2)}) collective-permute-start(bf16[96,2304]{1,0:T(8,128)(2,1)S(1)} %get-tuple-element.93), channel_id=1, source_target_pairs={{0,4},{2,6},{4,0},{6,2},{8,12},{10,14},{12,8},{14,10},{16,20},{18,... | collective-permute-start | bytes 1327112 | tf_op jit(solution)/shard_map/ppermute | solution.py:19
  91.0 14.0 %collective-permute-start.35 = (bf16[96,2304]{1,0:T(8,128)(2,1)S(1)}, bf16[96,2304]{1,0:T(8,128)(2,1)S(1)}, u32[]{:S(2)}, u32[]{:S(2)}) collective-permute-start(bf16[96,2304]{1,0:T(8,128)(2,1)S(1)} %get-tuple-element.93), channel_id=1, source_target_pairs={{0,1},{1,0},{2,3},{3,2},{4,5},{5,4},{6,7},{7,6},{8,9},{9,8},{10,11... | collective-permute-start | bytes 1327112 | tf_op jit(solution)/shard_map/ppermute | solution.py:19
  91.6 10.0 %collective-permute-start.31 = (bf16[24,2304]{1,0:T(8,128)(2,1)S(1)}, bf16[24,2304]{1,0:T(8,128)(2,1)S(1)}, u32[]{:S(2)}, u32[]{:S(2)}) collective-permute-start(bf16[24,2304]{1,0:T(8,128)(2,1)S(1)} %error.1.refs_13_.refs_7_), channel_id=1, source_target_pairs={{0,8},{2,10},{4,12},{6,14},{8,0},{10,2},{12,4},{14,6},{16,24},{18,... | collective-permute-start | bytes 331784 | tf_op jit(solution)/shard_map/ppermute | solution.py:19
  94.5 7.6 %collective-permute-start.32 = (bf16[24,2304]{1,0:T(8,128)(2,1)S(1)}, bf16[24,2304]{1,0:T(8,128)(2,1)S(1)}, u32[]{:S(2)}, u32[]{:S(2)}) collective-permute-start(bf16[24,2304]{1,0:T(8,128)(2,1)S(1)} %error.1.refs_13_.refs_7_), channel_id=1, source_target_pairs={{0,16},{2,18},{4,20},{6,22},{8,24},{10,26},{12,28},{14,30},{16,0},... | collective-permute-start | bytes 331784 | tf_op jit(solution)/shard_map/ppermute | solution.py:19
  98.3 6.8 %collective-permute-start.33 = (bf16[24,2304]{1,0:T(8,128)(2,1)S(1)}, bf16[24,2304]{1,0:T(8,128)(2,1)S(1)}, u32[]{:S(2)}, u32[]{:S(2)}) collective-permute-start(bf16[24,2304]{1,0:T(8,128)(2,1)S(1)} %error.1.refs_13_.refs_7_), channel_id=1, source_target_pairs={{0,24},{2,26},{4,28},{6,30},{8,16},{10,18},{12,20},{14,22},{16,8},... | collective-permute-start | bytes 331784 | tf_op jit(solution)/shard_map/ppermute | solution.py:19
  105.8 9.8 %collective-permute-start.38 = (bf16[72,2304]{1,0:T(8,128)(2,1)S(1)}, bf16[72,2304]{1,0:T(8,128)(2,1)S(1)}, u32[]{:S(2)}, u32[]{:S(2)}) collective-permute-start(bf16[72,2304]{1,0:T(8,128)(2,1)S(1)} %get-tuple-element.97), channel_id=1, source_target_pairs={{0,4},{2,6},{4,0},{6,2},{8,12},{10,14},{12,8},{14,10},{16,20},{18,... | collective-permute-start | bytes 995336 | tf_op jit(solution)/shard_map/ppermute | solution.py:19
  106.8 9.5 %collective-permute-start.39 = (bf16[72,2304]{1,0:T(8,128)(2,1)S(1)}, bf16[72,2304]{1,0:T(8,128)(2,1)S(1)}, u32[]{:S(2)}, u32[]{:S(2)}) collective-permute-start(bf16[72,2304]{1,0:T(8,128)(2,1)S(1)} %get-tuple-element.97), channel_id=1, source_target_pairs={{0,1},{1,0},{2,3},{3,2},{4,5},{5,4},{6,7},{7,6},{8,9},{9,8},{10,11... | collective-permute-start | bytes 995336 | tf_op jit(solution)/shard_map/ppermute | solution.py:19
  116.4 6.4 %collective-permute-start.42 = (bf16[192,2304]{1,0:T(8,128)(2,1)S(1)}, bf16[192,2304]{1,0:T(8,128)(2,1)S(1)}, u32[]{:S(2)}, u32[]{:S(2)}) collective-permute-start(bf16[192,2304]{1,0:T(8,128)(2,1)S(1)} %get-tuple-element.101.refs_2_.refs_16_), channel_id=1, source_target_pairs={{0,2},{2,0},{4,6},{6,4},{8,10},{10,8},{12,14},{14,12},{16,18},{18,... | collective-permute-start | bytes 2654216 | tf_op jit(solution)/shard_map/ppermute | solution.py:19
  117.0 12.2 %collective-permute-start.40 = (bf16[96,2304]{1,0:T(8,128)(2,1)S(1)}, bf16[96,2304]{1,0:T(8,128)(2,1)S(1)}, u32[]{:S(2)}, u32[]{:S(2)}) collective-permute-start(bf16[96,2304]{1,0:T(8,128)(2,1)S(1)} %get-tuple-element.99), channel_id=1, source_target_pairs={{0,4},{2,6},{4,0},{6,2},{8,12},{10,14},{12,8},{14,10},{16,20},{18,... | collective-permute-start | bytes 1327112 | tf_op jit(solution)/shard_map/ppermute | solution.py:19
  118.0 11.9 %collective-permute-start.41 = (bf16[96,2304]{1,0:T(8,128)(2,1)S(1)}, bf16[96,2304]{1,0:T(8,128)(2,1)S(1)}, u32[]{:S(2)}, u32[]{:S(2)}) collective-permute-start(bf16[96,2304]{1,0:T(8,128)(2,1)S(1)} %get-tuple-element.100), channel_id=1, source_target_pairs={{0,1},{1,0},{2,3},{3,2},{4,5},{5,4},{6,7},{7,6},{8,9},{9,8},{10,11... | collective-permute-start | bytes 1327112 | tf_op jit(solution)/shard_map/ppermute | solution.py:19
  (15 other events, 63.0 us)

commit v5 on v4

--- a/solution.py
+++ b/solution.py
@@ -529,8 +529,8 @@
     def pair(keep, got, after):
         return local(pair_kernel, "pair", [keep, *got], lows, after)
 
-    def error(t, low, got, ends, after):
-        arrays = [low, got, *ends, targets[:, t, :]]
+    def error(low, got, ends, target, after):
+        arrays = [low, got, *ends, target]
         return local(functools.partial(error_kernel, n), "error", arrays, [small], after)[0]
 
     def nears(parts):
@@ -542,10 +542,11 @@
     def halves(value):
         return [(value, k * quart, quart) for k in (0, 2)], [(value, k * quart, quart) for k in (1, 3)]
 
-    acts = [acts_in[:, s, :] for s in range(layers)]
+    acts = [acts_in[:, 0, :]]
     ends = quart - n
     z_a0 = along([acts[0]] * len(line))
     enc_held = load([enc_weight])[0]
+    acts.append(lax.optimization_barrier((acts_in, enc_held))[0][:, 1, :])
     done = [*z_a0, enc_held]
     line0, send, a1 = join([z_a0, [*z_a0, *acts], [acts[1]]], done)
     y_s, x_s = away(send), across(send)
@@ -562,7 +563,7 @@
     done = [x_l1, *got0]
     low0, high0 = pair(keep0, got0, done)
     far1.append(x_l1)
-    col1, far_both = join([[a1, line1, *far1], far0 + far1], done)
+    col1, far_both = join([[a1, line1, *far1], far0 + far1], [*done, high0])
     y_l1, x_h0 = away(line1), across(high0)
     in1 = [col1, core(col1)]
     early = decode(1, [0], [code0], dec_held, layers, (), False, True, (low0, col1))
@@ -575,26 +576,27 @@
     z_r0 = along(ends0)
     x_h1 = across(high1)
     done = [*z_r0, x_h1]
-    target = join([[targets[:, 0, :]]], [low1], 2 * quart * width * feats)[0]
-    arrays = [low0, x_h0, *z_r0, target, low1, x_h1]
+    target0, target1 = join([[targets[:, 0, :]], [targets[:, 1, :]]], [low1], 2 * quart * width * feats)
+    arrays = [low0, x_h0, *z_r0, target0, low1, x_h1]
     shapes = [((2 * n, width), jnp.bfloat16)] * len(line) + [small]
     *turned, e0 = local(functools.partial(turn_kernel, n, len(line)), "turn", arrays, shapes, done)
     y_f, y_e0, x_e0 = away(far_both), away(e0), across(e0)
     z_t = along(turned)
     done = [*z_t, x_e0, y_e0, y_f]
-    e1 = error(1, low1, x_h1, z_t, done)
+    e1 = error(low1, x_h1, z_t, target1, done)
     lines = [(z, n, n) for z in z_t]
     near0, both = join([[e0, *lines], [*lines, e1]], done)
     there0 = [(y_s, ends, n), (y_s, 0, ends), (y_f, 0, quart)]
-    there0, there1 = join([there0, [(y_s, quart, n), y_l1, (y_f, quart, quart)]], done)
+    there0, there1 = join([there0, [(y_s, quart, n), y_l1, (y_f, quart, quart)]], [*done, both])
     y_b, x_b = away(both), across(both)
     z_e1 = along([e1] * len(line))
     there_in0, there_in1 = [there0, core(there0)], [there1, core(there1)]
     there_pre0, there_code0 = encoded(0, there_in0)
     there_pre1, there_code1 = encoded(1, there_in1)
     done = [*z_e1, x_b, y_b, there_code0, there_code1]
-    near1, whole0, near_y0, send = join(
-        [[e1, *z_e1], [near0, x_e0, (x_b, 0, ends)], [y_e0, (y_b, 0, ends)], z_e1], done
+    near1, send = join([[e1, *z_e1], z_e1], (), 32 * quart * width * feats)
+    whole0, near_y0 = join(
+        [[near0, x_e0, (x_b, 0, ends)], [y_e0, (y_b, 0, ends)]], [there_code0, there_code1]
     )
     y_g, x_g = away(send), across(send)
     err0 = [whole0, core(whole0)]
@@ -603,7 +605,7 @@
     first_near = first(near_err0, dec_held)
     share = (feats // lax.axis_size("tok"), width // lax.axis_size("tok"))
     early = ahead([code0] + halves(there_code0)[0], err0 + near_err0, share[0])
-    done = [x_g, y_g, first_own, first_near, early]
+    done = [x_g, y_g, first_own, first_near]
     whole1, near_y1, go_x, go_y = join(
         [
             [near1, (x_b, ends, n), x_g],
@@ -620,11 +622,10 @@
     near_pre, far_pre = zip(halves(there_pre0), halves(there_pre1))
     grad_own, sum_own = back([err0, err1], [[pre0], [pre1]], dec_held, layers, True, [first_own])
     grad_near, sum_near = back([near_err0, near_err1], near_pre, dec_held, layers, True, [first_near])
-    done = [x_o, y_t, grad_own[0], grad_near[0]]
+    done = [x_o, y_t, grad_own[0], grad_near[0], early]
     left = quart - hop
-    far = join([[(x_o, 0, hop), (y_t, 0, left), (x_o, hop, hop), (y_t, left, left)]], done)[0]
-    far = [far, core(far)]
-    far_errs = [nears(far), fars(far)]
+    far0, far1 = join([[(x_o, 0, hop), (y_t, 0, left)], [(x_o, hop, hop), (y_t, left, left)]], done)
+    far_errs = [[far0, core(far0)], [far1, core(far1)]]
     grad_far, sum_far = back(far_errs, far_pre, dec_held, layers, True)
     codes = [sum(halves(c), []) for c in (there_code0, there_code1)]
     seen = [nears(p) + fars(p) for p in (there_in0, there_in1)]

time: 148 us -> 146 us (0.986)
  waiting for transfers between devices: 50.6 us -> 47.4 us
  starting transfers between devices: 41.5 us -> 43.2 us
    ppermute x45 -> x46, waiting for transfers between devices: 50.6 us -> 47.4 us  [swap(): lax.ppermute(value, axis, [(i, i ^ bits) for i in range(lax.axis_size(axi...]
    ppermute x45 -> x46, starting transfers between devices: 41.5 us -> 43.2 us  [swap(): lax.ppermute(value, axis, [(i, i ^ bits) for i in range(lax.axis_size(axi...]
    pallas_call x26 -> x27, Pallas kernels: 33.6 us -> 33.8 us  [local(): pl.pallas_call(lambda *refs: kernel(*refs[skip:]), name=name, out_shape=[...]
  transfers between devices with their start and end apart: 45 -> 46, of which waited for: 22 -> 22; matrix products, arithmetic and copies ran while one was open for 0% -> 0% of each run, Pallas kernels for 25% -> 25%
where the time goes in v5:
time: 146 us
  Pallas kernels  52.6 us (36%)
  waiting for transfers between devices  47.4 us (32%)
  starting transfers between devices  43.2 us (30%)
    ppermute x46, waiting for transfers between devices, swap(): lax.ppermute(value, axis, [(i, i ^ bits) for i in range(lax.axis_size(axi...  47.4 us
    ppermute x46, starting transfers between devices, swap(): lax.ppermute(value, axis, [(i, i ^ bits) for i in range(lax.axis_size(axi...  43.2 us
    pallas_call x27, Pallas kernels, local(): pl.pallas_call(lambda *refs: kernel(*refs[skip:]), name=name, out_shape=[...  33.8 us
    pallas_call x1, Pallas kernels, all_grads(): pl.pallas_call(functools.partial(grads_body, layers, scale, rows, own, la...  10 us
    pallas_call x2, Pallas kernels, load(): pl.pallas_call(lambda *refs: load_kernel(count, *refs[skip:]), name='load...  8.72 us
  transfers between devices with their start and end apart: 46, of which 22 were waited for; matrix products, arithmetic and copies ran while one was open for 0% of the time, Pallas kernels for 25%

profile of v5, /device:TPU:0, one launch (start us, length us, event | category | flops | bytes accessed | tf_op | source)
XLA Modules:
  0.0 145.7 jit_solution(15283052558437434231)
XLA Ops:
  1.6 3.1 %collective-permute-start = (bf16[24,2304]{1,0:T(8,128)(2,1)S(1)}, bf16[24,2304]{1,0:T(8,128)(2,1)S(1)}, u32[]{:S(2)}, u32[]{:S(2)}) collective-permute-start(bf16[24,2304]{1,0:T(8,128)(2,1)S(1)} %bitcast.10), channel_id=1, source_target_pairs={{0,8},{2,10},{4,12},{6,14},{8,0},{10,2},{12,4},{14,6},{16,24},{18,... | collective-permute-start | bytes 331784 | tf_op jit(solution)/shard_map/ppermute | solution.py:19
  4.7 2.6 %collective-permute-start.1 = (bf16[24,2304]{1,0:T(8,128)(2,1)S(1)}, bf16[24,2304]{1,0:T(8,128)(2,1)S(1)}, u32[]{:S(2)}, u32[]{:S(2)}) collective-permute-start(bf16[24,2304]{1,0:T(8,128)(2,1)S(1)} %bitcast.11), channel_id=1, source_target_pairs={{0,16},{2,18},{4,20},{6,22},{8,24},{10,26},{12,28},{14,30},{16,0},... | collective-permute-start | bytes 331784 | tf_op jit(solution)/shard_map/ppermute | solution.py:19
  7.3 3.7 %load.2.refs_3_.refs_2_ = bf16[2,2304,1024]{2,1,0:T(8,128)(2,1)S(1)} custom-call(bf16[2,2304,1024]{2,1,0:T(8,128)(2,1)} %refs_0_.1), custom_call_target="tpu_custom_call" | custom-call | tf_op jit(solution)/shard_map/load/pallas_call | solution.py:106
  11.0 5.0 %collective-permute-done.1.refs_1_.refs_5_.refs_8_ = bf16[24,2304]{1,0:T(8,128)(2,1)S(1)} collective-permute-done((bf16[24,2304]{1,0:T(8,128)(2,1)S(1)}, bf16[24,2304]{1,0:T(8,128)(2,1)S(1)}, u32[]{:S(2)}, u32[]{:S(2)}) %collective-permute-start.1) | collective-permute-done | bytes 110624 | tf_op jit(solution)/shard_map/ppermute | solution.py:19
  19.2 1.7 %collective-permute-start.3 = (bf16[24,2304]{1,0:T(8,128)(2,1)S(1)}, bf16[24,2304]{1,0:T(8,128)(2,1)S(1)}, u32[]{:S(2)}, u32[]{:S(2)}) collective-permute-start(bf16[24,2304]{1,0:T(8,128)(2,1)S(1)} %get-tuple-element.67.refs_5_), channel_id=1, source_target_pairs={{0,8},{2,10},{4,12},{6,14},{8,0},{10,2},{12,4},{14,6},{16,24},{18,... | collective-permute-start | bytes 331784 | tf_op jit(solution)/shard_map/ppermute | solution.py:19
  23.6 5.0 %load.3.refs_5_.refs_1_.refs_3_.refs_2_.refs_6_.refs_7_.refs_8_.refs_9_.refs_10_ = bf16[3,1024,2304]{2,1,0:T(8,128)(2,1)S(1)} custom-call(bf16[72,2304]{1,0:T(8,128)(2,1)S(1)} %get-tuple-element.69.refs_0_.refs_10_, bf16[3,1024,2304]{2,1,0:T(8,128)(2,1)} %refs_1_.1), custom_call_target="tpu_custom_call" | custom-call | tf_op jit(solution)/shard_map/load/pallas_call | solution.py:106
  28.7 1.8 %collective-permute-done.4.refs_1_.refs_7_ = bf16[24,2304]{1,0:T(8,128)(2,1)S(1)} collective-permute-done((bf16[24,2304]{1,0:T(8,128)(2,1)S(1)}, bf16[24,2304]{1,0:T(8,128)(2,1)S(1)}, u32[]{:S(2)}, u32[]{:S(2)}) %collective-permute-start.4) | collective-permute-done | bytes 110624 | tf_op jit(solution)/shard_map/ppermute | solution.py:19
  31.3 1.8 %collective-permute-done.8.refs_1_.refs_23_ = bf16[192,2304]{1,0:T(8,128)(2,1)S(1)} collective-permute-done((bf16[192,2304]{1,0:T(8,128)(2,1)S(1)}, bf16[192,2304]{1,0:T(8,128)(2,1)S(1)}, u32[]{:S(2)}, u32[]{:S(2)}) %collective-permute-start.8) | collective-permute-done | bytes 884768 | tf_op jit(solution)/shard_map/ppermute | solution.py:19
  33.1 2.1 %encode.4 = (f32[384,1024]{1,0:T(8,128)S(1)}, bf16[384,1024]{1,0:T(8,128)(2,1)S(1)}) custom-call(bf16[192,2304]{1,0:T(8,128)(2,1)S(1)} %get-tuple-element.70.refs_0_.refs_22_, bf16[192,2304]{1,0:T(8,128)(2,1)S(1)} %collective-permute-done.8.refs_1_.refs_23_, bf16[2,2304,1024]{2,1,0:T(8,128)(2,1)S(1)} %load.2.refs_3_.refs_2_, ...), custom_call_target="tpu_custom_call" | custom-call | flops 1811939328 | tf_op jit(solution)/shard_map/encode/pallas_call | solution.py:57
  35.2 2.0 %decode.3 = (bf16[192,2304]{1,0:T(8,128)(2,1)S(1)}, bf16[64,2304]{1,0:T(8,128)(2,1)S(1)}, bf16[64,2304]{1,0:T(8,128)(2,1)S(1)}, bf16[64,2304]{1,0:T(8,128)(2,1)S(1)}) custom-call(bf16[384,1024]{1,0:T(8,128)(2,1)S(1)} %get-tuple-element.71.refs_0_.refs_2_, bf16[3,1024,2304]{2,1,0:T(8,128)(2,1)S(1)} %load.3.refs_5_.refs_1_.refs_3_.refs_2_.refs_6_.refs_7_.refs_8_.refs_9_.refs_10_), custom_call_target="tpu_custom_call" | custom-call | flops 1811939328 | tf_op jit(solution)/shard_map/decode/pallas_call | solution.py:57
  37.9 3.0 %collective-permute-done.9.refs_0_.refs_8_.refs_12_ = bf16[72,2304]{1,0:T(8,128)(2,1)S(1)} collective-permute-done((bf16[72,2304]{1,0:T(8,128)(2,1)S(1)}, bf16[72,2304]{1,0:T(8,128)(2,1)S(1)}, u32[]{:S(2)}, u32[]{:S(2)}) %collective-permute-start.9) | collective-permute-done | bytes 331808 | tf_op jit(solution)/shard_map/ppermute | solution.py:19
  44.0 2.0 %decode.4.refs_0_.refs_2_ = f32[384,2304]{1,0:T(8,128)S(1)} custom-call(f32[96,2304]{1,0:T(8,128)S(1)} %get-tuple-element.78.refs_0_.refs_5_.refs_4_, bf16[192,2304]{1,0:T(8,128)(2,1)S(1)} %get-tuple-element.79.refs_1_.refs_28_, bf16[384,1024]{1,0:T(8,128)(2,1)S(1)} %get-tuple-element.71.refs_0_.refs_2_, ...), custom_call_target="tpu_custom_call" | custom-call | flops 1811939328 | tf_op jit(solution)/shard_map/decode/pallas_call | solution.py:57
  46.0 2.0 %encode.5 = (f32[384,1024]{1,0:T(8,128)S(1)}, bf16[384,1024]{1,0:T(8,128)(2,1)S(1)}) custom-call(f32[384,2304]{1,0:T(8,128)S(1)} %decode.4.refs_0_.refs_2_, bf16[192,2304]{1,0:T(8,128)(2,1)S(1)} %get-tuple-element.79.refs_1_.refs_28_, bf16[192,2304]{1,0:T(8,128)(2,1)S(1)} %collective-permute-done.15.refs_2_.refs_29_, ...), custom_call_target="tpu_custom_call" | custom-call | flops 1811939328 | tf_op jit(solution)/shard_map/encode/pallas_call | solution.py:57
  48.1 2.0 %decode.5 = (bf16[192,2304]{1,0:T(8,128)(2,1)S(1)}, bf16[64,2304]{1,0:T(8,128)(2,1)S(1)}, bf16[64,2304]{1,0:T(8,128)(2,1)S(1)}, bf16[64,2304]{1,0:T(8,128)(2,1)S(1)}) custom-call(bf16[384,1024]{1,0:T(8,128)(2,1)S(1)} %get-tuple-element.80.refs_0_.refs_5_, ...), custom_call_target="tpu_custom_call" | custom-call | flops 1811939328 | tf_op jit(solution)/shard_map/decode/pallas_call | solution.py:57
  52.4 1.8 %collective-permute-done.13.refs_0_.refs_6_.refs_5_ = bf16[96,2304]{1,0:T(8,128)(2,1)S(1)} collective-permute-done((bf16[96,2304]{1,0:T(8,128)(2,1)S(1)}, bf16[96,2304]{1,0:T(8,128)(2,1)S(1)}, u32[]{:S(2)}, u32[]{:S(2)}) %collective-permute-start.13) | collective-permute-done | bytes 442400 | tf_op jit(solution)/shard_map/ppermute | solution.py:19
  54.5 2.8 %collective-permute-start.19 = (bf16[24,2304]{1,0:T(8,128)(2,1)S(1)}, bf16[24,2304]{1,0:T(8,128)(2,1)S(1)}, u32[]{:S(2)}, u32[]{:S(2)}) collective-permute-start(bf16[24,2304]{1,0:T(8,128)(2,1)S(1)} %get-tuple-element.85), channel_id=1, source_target_pairs={{0,8},{2,10},{4,12},{6,14},{8,0},{10,2},{12,4},{14,6},{16,24},{18,... | collective-permute-start | bytes 331784 | tf_op jit(solution)/shard_map/ppermute | solution.py:19
  61.1 7.0 %collective-permute-done.20.refs_1_.refs_7_ = bf16[24,2304]{1,0:T(8,128)(2,1)S(1)} collective-permute-done((bf16[24,2304]{1,0:T(8,128)(2,1)S(1)}, bf16[24,2304]{1,0:T(8,128)(2,1)S(1)}, u32[]{:S(2)}, u32[]{:S(2)}) %collective-permute-start.20) | collective-permute-done | bytes 110624 | tf_op jit(solution)/shard_map/ppermute | solution.py:19
  68.1 2.5 %collective-permute-done.22.refs_3_.refs_11_.refs_7_ = bf16[96,2304]{1,0:T(8,128)(2,1)S(1)} collective-permute-done((bf16[96,2304]{1,0:T(8,128)(2,1)S(1)}, bf16[96,2304]{1,0:T(8,128)(2,1)S(1)}, u32[]{:S(2)}, u32[]{:S(2)}) %collective-permute-start.22) | collective-permute-done | bytes 442400 | tf_op jit(solution)/shard_map/ppermute | solution.py:19
  71.6 2.3 %collective-permute-start.24 = (bf16[48,2304]{1,0:T(8,128)(2,1)S(1)}, bf16[48,2304]{1,0:T(8,128)(2,1)S(1)}, u32[]{:S(2)}, u32[]{:S(2)}) collective-permute-start(bf16[48,2304]{1,0:T(8,128)(2,1)S(1)} %get-tuple-element.92), channel_id=1, source_target_pairs={{0,16},{2,18},{4,20},{6,22},{8,24},{10,26},{12,28},{14,30},{16,0},... | collective-permute-start | bytes 663560 | tf_op jit(solution)/shard_map/ppermute | solution.py:19
  76.6 3.5 %collective-permute-done.26.refs_3_ = bf16[24,2304]{1,0:T(8,128)(2,1)S(1)} collective-permute-done((bf16[24,2304]{1,0:T(8,128)(2,1)S(1)}, bf16[24,2304]{1,0:T(8,128)(2,1)S(1)}, u32[]{:S(2)}, u32[]{:S(2)}) %collective-permute-start.26) | collective-permute-done | bytes 110624 | tf_op jit(solution)/shard_map/ppermute | solution.py:19
  80.7 8.4 %collective-permute-done.24.refs_1_.refs_9_.refs_8_.refs_11_ = bf16[48,2304]{1,0:T(8,128)(2,1)S(1)} collective-permute-done((bf16[48,2304]{1,0:T(8,128)(2,1)S(1)}, bf16[48,2304]{1,0:T(8,128)(2,1)S(1)}, u32[]{:S(2)}, u32[]{:S(2)}) %collective-permute-start.24) | collective-permute-done | bytes 221216 | tf_op jit(solution)/shard_map/ppermute | solution.py:19
  91.3 2.9 %collective-permute-start.35 = (bf16[24,2304]{1,0:T(8,128)(2,1)S(1)}, bf16[24,2304]{1,0:T(8,128)(2,1)S(1)}, u32[]{:S(2)}, u32[]{:S(2)}) collective-permute-start(bf16[24,2304]{1,0:T(8,128)(2,1)S(1)} %error.1.refs_13_.refs_0_), channel_id=1, source_target_pairs={{0,8},{2,10},{4,12},{6,14},{8,0},{10,2},{12,4},{14,6},{16,24},{18,... | collective-permute-start | bytes 331784 | tf_op jit(solution)/shard_map/ppermute | solution.py:19
  95.9 2.2 %encode.6 = (f32[384,1024]{1,0:T(8,128)S(1)}, bf16[384,1024]{1,0:T(8,128)(2,1)S(1)}) custom-call(bf16[192,2304]{1,0:T(8,128)(2,1)S(1)} %get-tuple-element.98.refs_0_.refs_24_.refs_26_, bf16[192,2304]{1,0:T(8,128)(2,1)S(1)} %collective-permute-done.29.refs_1_.refs_25_.refs_27_, bf16[2,2304,1024]{2,1,0:T(8,128)(2,1)S(1)} %load.2.refs_3_.refs_2_, ...), custom_call_target="tpu_custom_call" | custom-call | flops 1811939328 | tf_op jit(solution)/shard_map/encode/pallas_call | solution.py:57
  99.4 2.0 %encode.7 = (f32[384,1024]{1,0:T(8,128)S(1)}, bf16[384,1024]{1,0:T(8,128)(2,1)S(1)}) custom-call(bf16[192,2304]{1,0:T(8,128)(2,1)S(1)} %get-tuple-element.100.refs_0_.refs_30_.refs_32_, bf16[192,2304]{1,0:T(8,128)(2,1)S(1)} %collective-permute-done.30.refs_1_.refs_31_.refs_33_, bf16[2,2304,1024]{2,1,0:T(8,128)(2,1)S(1)} %load.2.refs_3_.refs_2_, ...), custom_call_target="tpu_custom_call" | custom-call | flops 1811939328 | tf_op jit(solution)/shard_map/encode/pallas_call | solution.py:57
  103.0 1.9 %collective-permute-done.37.refs_3_.refs_6_ = bf16[24,2304]{1,0:T(8,128)(2,1)S(1)} collective-permute-done((bf16[24,2304]{1,0:T(8,128)(2,1)S(1)}, bf16[24,2304]{1,0:T(8,128)(2,1)S(1)}, u32[]{:S(2)}, u32[]{:S(2)}) %collective-permute-start.37) | collective-permute-done | bytes 110624 | tf_op jit(solution)/shard_map/ppermute | solution.py:19
  108.7 2.0 %first.2.refs_2_.refs_9_ = f32[384,1024]{1,0:T(8,128)S(1)} custom-call(bf16[192,2304]{1,0:T(8,128)(2,1)S(1)} %get-tuple-element.103.refs_0_.refs_3_.refs_10_, bf16[192,2304]{1,0:T(8,128)(2,1)S(1)} %collective-permute-done.33.refs_1_.refs_4_.refs_11_, bf16[3,1024,2304]{2,1,0:T(8,128)(2,1)S(1)} %load.3.refs_5_.refs_1_.refs_3_.refs_2_.refs_6_.refs_7_.refs_8_.refs_9_.refs_10_), custom_call_target="tpu_custom_call" | custom-call | flops 1811939328 | tf_op jit(solution)/shard_map/first/pallas_call | solution.py:57
  110.7 3.0 %collective-permute-done.38.refs_0_.refs_6_.refs_13_ = bf16[72,2304]{1,0:T(8,128)(2,1)S(1)} collective-permute-done((bf16[72,2304]{1,0:T(8,128)(2,1)S(1)}, bf16[72,2304]{1,0:T(8,128)(2,1)S(1)}, u32[]{:S(2)}, u32[]{:S(2)}) %collective-permute-start.38) | collective-permute-done | bytes 331808 | tf_op jit(solution)/shard_map/ppermute | solution.py:19
  117.0 2.1 %ahead.1.refs_4_.refs_40_ = f32[512,2304]{1,0:T(8,128)S(1)} custom-call(bf16[384,1024]{1,0:T(8,128)(2,1)S(1)} %get-tuple-element.71.refs_0_.refs_2_, bf16[384,1024]{1,0:T(8,128)(2,1)S(1)} %get-tuple-element.99.refs_0_.refs_1_.refs_2_.refs_3_.refs_4_, bf16[384,1024]{1,0:T(8,128)(2,1)S(1)} %get-tuple-element.99.refs_0_.refs_1_.refs_2_.refs_3_.refs_4_, ...), custom_call_target="tpu_custom_call" | custom-call | flops 1358954496 | tf_op jit(solution)/shard_map/ahead/pallas_call | solution.py:57
  119.1 3.2 %back.4 = (bf16[192,1024]{1,0:T(8,128)(2,1)S(1)}, bf16[192,1024]{1,0:T(8,128)(2,1)S(1)}, f32[2,1,1024]{2,1,0:T(1,128)S(1)}) custom-call(bf16[96,2304]{1,0:T(8,128)(2,1)S(1)} %get-tuple-element.104.refs_0_.refs_9_.refs_5_.refs_12_, bf16[96,2304]{1,0:T(8,128)(2,1)S(1)} %collective-permute-done.34.refs_1_.refs_6_.refs_13_, ...), custom_call_target="tpu_custom_call" | custom-call | flops 1811939328 | tf_op jit(solution)/shard_map/back/pallas_call | solution.py:57
  122.3 3.9 %back.3 = (bf16[384,1024]{1,0:T(8,128)(2,1)S(1)}, bf16[384,1024]{1,0:T(8,128)(2,1)S(1)}, f32[2,1,1024]{2,1,0:T(1,128)S(1)}) custom-call(bf16[192,2304]{1,0:T(8,128)(2,1)S(1)} %get-tuple-element.103.refs_0_.refs_3_.refs_10_, bf16[192,2304]{1,0:T(8,128)(2,1)S(1)} %collective-permute-done.33.refs_1_.refs_4_.refs_11_, ...), custom_call_target="tpu_custom_call" | custom-call | flops 3623878656 | tf_op jit(solution)/shard_map/back/pallas_call | solution.py:57
  130.6 4.9 %back.5 = (bf16[192,1024]{1,0:T(8,128)(2,1)S(1)}, bf16[192,1024]{1,0:T(8,128)(2,1)S(1)}, f32[2,1,1024]{2,1,0:T(1,128)S(1)}) custom-call(bf16[96,2304]{1,0:T(8,128)(2,1)S(1)} %get-tuple-element.117.refs_0_.refs_14_, bf16[96,2304]{1,0:T(8,128)(2,1)S(1)} %collective-permute-done.44.refs_1_.refs_15_, bf16[96,2304]{1,0:T(8,128)(2,1)S(1)} %get-tuple-element.118.refs_2_.refs_20_, ...), custom_call_target="tpu_custom_call" | custom-call | flops 2717908992 | tf_op jit(solution)/shard_map/back/pallas_call | solution.py:57
  135.5 10.0 %grads.1 = (bf16[3,512,2304]{2,1,0:T(8,128)(2,1)}, bf16[2,1152,1024]{2,1,0:T(8,128)(2,1)}, f32[2,512]{1,0:T(2,128)}) custom-call(bf16[384,1024]{1,0:T(8,128)(2,1)S(1)} %get-tuple-element.71.refs_0_.refs_2_, bf16[384,1024]{1,0:T(8,128)(2,1)S(1)} %get-tuple-element.99.refs_0_.refs_1_.refs_2_.refs_3_.refs_4_, ...), custom_call_target="tpu_custom_call" | custom-call | tf_op jit(solution)/shard_map/grads/pallas_call | solution.py:440
  (102 shorter events, 40.0 us)
Async XLA Ops:
  1.6 9.4 %collective-permute-start = (bf16[24,2304]{1,0:T(8,128)(2,1)S(1)}, bf16[24,2304]{1,0:T(8,128)(2,1)S(1)}, u32[]{:S(2)}, u32[]{:S(2)}) collective-permute-start(bf16[24,2304]{1,0:T(8,128)(2,1)S(1)} %bitcast.10), channel_id=1, source_target_pairs={{0,8},{2,10},{4,12},{6,14},{8,0},{10,2},{12,4},{14,6},{16,24},{18,... | collective-permute-start | bytes 331784 | tf_op jit(solution)/shard_map/ppermute | solution.py:19
  4.7 11.3 %collective-permute-start.1 = (bf16[24,2304]{1,0:T(8,128)(2,1)S(1)}, bf16[24,2304]{1,0:T(8,128)(2,1)S(1)}, u32[]{:S(2)}, u32[]{:S(2)}) collective-permute-start(bf16[24,2304]{1,0:T(8,128)(2,1)S(1)} %bitcast.11), channel_id=1, source_target_pairs={{0,16},{2,18},{4,20},{6,22},{8,24},{10,26},{12,28},{14,30},{16,0},... | collective-permute-start | bytes 331784 | tf_op jit(solution)/shard_map/ppermute | solution.py:19
  7.3 8.8 %collective-permute-start.2 = (bf16[24,2304]{1,0:T(8,128)(2,1)S(1)}, bf16[24,2304]{1,0:T(8,128)(2,1)S(1)}, u32[]{:S(2)}, u32[]{:S(2)}) collective-permute-start(bf16[24,2304]{1,0:T(8,128)(2,1)S(1)} %bitcast.12), channel_id=1, source_target_pairs={{0,24},{2,26},{4,28},{6,30},{8,16},{10,18},{12,20},{14,22},{16,8},... | collective-permute-start | bytes 331784 | tf_op jit(solution)/shard_map/ppermute | solution.py:19
  16.1 14.4 %collective-permute-start.6 = (bf16[120,2304]{1,0:T(8,128)(2,1)S(1)}, bf16[120,2304]{1,0:T(8,128)(2,1)S(1)}, u32[]{:S(2)}, u32[]{:S(2)}) collective-permute-start(bf16[120,2304]{1,0:T(8,128)(2,1)S(1)} %get-tuple-element.68), channel_id=1, source_target_pairs={{0,4},{2,6},{4,0},{6,2},{8,12},{10,14},{12,8},{14,10},{16,20},{18,... | collective-permute-start | bytes 1658888 | tf_op jit(solution)/shard_map/ppermute | solution.py:19
  17.7 12.8 %collective-permute-start.7 = (bf16[120,2304]{1,0:T(8,128)(2,1)S(1)}, bf16[120,2304]{1,0:T(8,128)(2,1)S(1)}, u32[]{:S(2)}, u32[]{:S(2)}) collective-permute-start(bf16[120,2304]{1,0:T(8,128)(2,1)S(1)} %get-tuple-element.68), channel_id=1, source_target_pairs={{0,1},{1,0},{2,3},{3,2},{4,5},{5,4},{6,7},{7,6},{8,9},{9,8},{10,11... | collective-permute-start | bytes 1658888 | tf_op jit(solution)/shard_map/ppermute | solution.py:19
  19.2 9.4 %collective-permute-start.3 = (bf16[24,2304]{1,0:T(8,128)(2,1)S(1)}, bf16[24,2304]{1,0:T(8,128)(2,1)S(1)}, u32[]{:S(2)}, u32[]{:S(2)}) collective-permute-start(bf16[24,2304]{1,0:T(8,128)(2,1)S(1)} %get-tuple-element.67.refs_5_), channel_id=1, source_target_pairs={{0,8},{2,10},{4,12},{6,14},{8,0},{10,2},{12,4},{14,6},{16,24},{18,... | collective-permute-start | bytes 331784 | tf_op jit(solution)/shard_map/ppermute | solution.py:19
  21.0 9.5 %collective-permute-start.4 = (bf16[24,2304]{1,0:T(8,128)(2,1)S(1)}, bf16[24,2304]{1,0:T(8,128)(2,1)S(1)}, u32[]{:S(2)}, u32[]{:S(2)}) collective-permute-start(bf16[24,2304]{1,0:T(8,128)(2,1)S(1)} %get-tuple-element.67.refs_5_), channel_id=1, source_target_pairs={{0,16},{2,18},{4,20},{6,22},{8,24},{10,26},{12,28},{14,30},{16,0},... | collective-permute-start | bytes 331784 | tf_op jit(solution)/shard_map/ppermute | solution.py:19
  22.3 8.2 %collective-permute-start.5 = (bf16[24,2304]{1,0:T(8,128)(2,1)S(1)}, bf16[24,2304]{1,0:T(8,128)(2,1)S(1)}, u32[]{:S(2)}, u32[]{:S(2)}) collective-permute-start(bf16[24,2304]{1,0:T(8,128)(2,1)S(1)} %get-tuple-element.67.refs_5_), channel_id=1, source_target_pairs={{0,24},{2,26},{4,28},{6,30},{8,16},{10,18},{12,20},{14,22},{16,8},... | collective-permute-start | bytes 331784 | tf_op jit(solution)/shard_map/ppermute | solution.py:19
  30.7 10.3 %collective-permute-start.9 = (bf16[72,2304]{1,0:T(8,128)(2,1)S(1)}, bf16[72,2304]{1,0:T(8,128)(2,1)S(1)}, u32[]{:S(2)}, u32[]{:S(2)}) collective-permute-start(bf16[72,2304]{1,0:T(8,128)(2,1)S(1)} %get-tuple-element.72.refs_6_), channel_id=1, source_target_pairs={{0,4},{2,6},{4,0},{6,2},{8,12},{10,14},{12,8},{14,10},{16,20},{18,... | collective-permute-start | bytes 995336 | tf_op jit(solution)/shard_map/ppermute | solution.py:19
  41.4 10.7 %collective-permute-start.14 = (bf16[72,2304]{1,0:T(8,128)(2,1)S(1)}, bf16[72,2304]{1,0:T(8,128)(2,1)S(1)}, u32[]{:S(2)}, u32[]{:S(2)}) collective-permute-start(bf16[72,2304]{1,0:T(8,128)(2,1)S(1)} %get-tuple-element.72.refs_6_), channel_id=1, source_target_pairs={{0,1},{1,0},{2,3},{3,2},{4,5},{5,4},{6,7},{7,6},{8,9},{9,8},{10,11... | collective-permute-start | bytes 995336 | tf_op jit(solution)/shard_map/ppermute | solution.py:19
  42.0 12.2 %collective-permute-start.13 = (bf16[96,2304]{1,0:T(8,128)(2,1)S(1)}, bf16[96,2304]{1,0:T(8,128)(2,1)S(1)}, u32[]{:S(2)}, u32[]{:S(2)}) collective-permute-start(bf16[96,2304]{1,0:T(8,128)(2,1)S(1)} %get-tuple-element.77.refs_4_), channel_id=1, source_target_pairs={{0,4},{2,6},{4,0},{6,2},{8,12},{10,14},{12,8},{14,10},{16,20},{18,... | collective-permute-start | bytes 1327112 | tf_op jit(solution)/shard_map/ppermute | solution.py:19
  42.5 33.4 %collective-permute-start.28 = (bf16[192,2304]{1,0:T(8,128)(2,1)S(1)}, bf16[192,2304]{1,0:T(8,128)(2,1)S(1)}, u32[]{:S(2)}, u32[]{:S(2)}) collective-permute-start(bf16[192,2304]{1,0:T(8,128)(2,1)S(1)} %get-tuple-element.95), channel_id=1, source_target_pairs={{0,1},{1,0},{2,3},{3,2},{4,5},{5,4},{6,7},{7,6},{8,9},{9,8},{10,11... | collective-permute-start | bytes 2654216 | tf_op jit(solution)/shard_map/ppermute | solution.py:19
  54.5 6.6 %collective-permute-start.19 = (bf16[24,2304]{1,0:T(8,128)(2,1)S(1)}, bf16[24,2304]{1,0:T(8,128)(2,1)S(1)}, u32[]{:S(2)}, u32[]{:S(2)}) collective-permute-start(bf16[24,2304]{1,0:T(8,128)(2,1)S(1)} %get-tuple-element.85), channel_id=1, source_target_pairs={{0,8},{2,10},{4,12},{6,14},{8,0},{10,2},{12,4},{14,6},{16,24},{18,... | collective-permute-start | bytes 331784 | tf_op jit(solution)/shard_map/ppermute | solution.py:19
  57.2 10.9 %collective-permute-start.20 = (bf16[24,2304]{1,0:T(8,128)(2,1)S(1)}, bf16[24,2304]{1,0:T(8,128)(2,1)S(1)}, u32[]{:S(2)}, u32[]{:S(2)}) collective-permute-start(bf16[24,2304]{1,0:T(8,128)(2,1)S(1)} %get-tuple-element.86), channel_id=1, source_target_pairs={{0,16},{2,18},{4,20},{6,22},{8,24},{10,26},{12,28},{14,30},{16,0},... | collective-permute-start | bytes 331784 | tf_op jit(solution)/shard_map/ppermute | solution.py:19
  58.4 9.7 %collective-permute-start.21 = (bf16[24,2304]{1,0:T(8,128)(2,1)S(1)}, bf16[24,2304]{1,0:T(8,128)(2,1)S(1)}, u32[]{:S(2)}, u32[]{:S(2)}) collective-permute-start(bf16[24,2304]{1,0:T(8,128)(2,1)S(1)} %get-tuple-element.87), channel_id=1, source_target_pairs={{0,24},{2,26},{4,28},{6,30},{8,16},{10,18},{12,20},{14,22},{16,8},... | collective-permute-start | bytes 331784 | tf_op jit(solution)/shard_map/ppermute | solution.py:19
  59.8 10.8 %collective-permute-start.22 = (bf16[96,2304]{1,0:T(8,128)(2,1)S(1)}, bf16[96,2304]{1,0:T(8,128)(2,1)S(1)}, u32[]{:S(2)}, u32[]{:S(2)}) collective-permute-start(bf16[96,2304]{1,0:T(8,128)(2,1)S(1)} %get-tuple-element.88), channel_id=1, source_target_pairs={{0,4},{2,6},{4,0},{6,2},{8,12},{10,14},{12,8},{14,10},{16,20},{18,... | collective-permute-start | bytes 1327112 | tf_op jit(solution)/shard_map/ppermute | solution.py:19
  70.9 9.8 %collective-permute-start.23 = (bf16[48,2304]{1,0:T(8,128)(2,1)S(1)}, bf16[48,2304]{1,0:T(8,128)(2,1)S(1)}, u32[]{:S(2)}, u32[]{:S(2)}) collective-permute-start(bf16[48,2304]{1,0:T(8,128)(2,1)S(1)} %get-tuple-element.91), channel_id=1, source_target_pairs={{0,8},{2,10},{4,12},{6,14},{8,0},{10,2},{12,4},{14,6},{16,24},{18,... | collective-permute-start | bytes 663560 | tf_op jit(solution)/shard_map/ppermute | solution.py:19
  71.6 17.4 %collective-permute-start.24 = (bf16[48,2304]{1,0:T(8,128)(2,1)S(1)}, bf16[48,2304]{1,0:T(8,128)(2,1)S(1)}, u32[]{:S(2)}, u32[]{:S(2)}) collective-permute-start(bf16[48,2304]{1,0:T(8,128)(2,1)S(1)} %get-tuple-element.92), channel_id=1, source_target_pairs={{0,16},{2,18},{4,20},{6,22},{8,24},{10,26},{12,28},{14,30},{16,0},... | collective-permute-start | bytes 663560 | tf_op jit(solution)/shard_map/ppermute | solution.py:19
  73.9 15.1 %collective-permute-start.25 = (bf16[48,2304]{1,0:T(8,128)(2,1)S(1)}, bf16[48,2304]{1,0:T(8,128)(2,1)S(1)}, u32[]{:S(2)}, u32[]{:S(2)}) collective-permute-start(bf16[48,2304]{1,0:T(8,128)(2,1)S(1)} %get-tuple-element.93), channel_id=1, source_target_pairs={{0,24},{2,26},{4,28},{6,30},{8,16},{10,18},{12,20},{14,22},{16,8},... | collective-permute-start | bytes 663560 | tf_op jit(solution)/shard_map/ppermute | solution.py:19
  89.3 4.9 %collective-permute-start.29 = (bf16[192,2304]{1,0:T(8,128)(2,1)S(1)}, bf16[192,2304]{1,0:T(8,128)(2,1)S(1)}, u32[]{:S(2)}, u32[]{:S(2)}) collective-permute-start(bf16[192,2304]{1,0:T(8,128)(2,1)S(1)} %get-tuple-element.98.refs_0_.refs_24_.refs_26_), channel_id=1, source_target_pairs={{0,2},{2,0},{4,6},{6,4},{8,10},{10,8},{12,14},{14,12},{16,18},{18,... | collective-permute-start | bytes 2654216 | tf_op jit(solution)/shard_map/ppermute | solution.py:19
  89.4 8.7 %collective-permute-start.30 = (bf16[192,2304]{1,0:T(8,128)(2,1)S(1)}, bf16[192,2304]{1,0:T(8,128)(2,1)S(1)}, u32[]{:S(2)}, u32[]{:S(2)}) collective-permute-start(bf16[192,2304]{1,0:T(8,128)(2,1)S(1)} %get-tuple-element.100.refs_0_.refs_30_.refs_32_), channel_id=1, source_target_pairs={{0,2},{2,0},{4,6},{6,4},{8,10},{10,8},{12,14},{14,12},{16,18},{18,... | collective-permute-start | bytes 2654216 | tf_op jit(solution)/shard_map/ppermute | solution.py:19
  89.9 12.2 %collective-permute-start.31 = (bf16[96,2304]{1,0:T(8,128)(2,1)S(1)}, bf16[96,2304]{1,0:T(8,128)(2,1)S(1)}, u32[]{:S(2)}, u32[]{:S(2)}) collective-permute-start(bf16[96,2304]{1,0:T(8,128)(2,1)S(1)} %get-tuple-element.97.refs_6_), channel_id=1, source_target_pairs={{0,4},{2,6},{4,0},{6,2},{8,12},{10,14},{12,8},{14,10},{16,20},{18,... | collective-permute-start | bytes 1327112 | tf_op jit(solution)/shard_map/ppermute | solution.py:19
  90.4 11.9 %collective-permute-start.32 = (bf16[96,2304]{1,0:T(8,128)(2,1)S(1)}, bf16[96,2304]{1,0:T(8,128)(2,1)S(1)}, u32[]{:S(2)}, u32[]{:S(2)}) collective-permute-start(bf16[96,2304]{1,0:T(8,128)(2,1)S(1)} %get-tuple-element.97.refs_6_), channel_id=1, source_target_pairs={{0,1},{1,0},{2,3},{3,2},{4,5},{5,4},{6,7},{7,6},{8,9},{9,8},{10,11... | collective-permute-start | bytes 1327112 | tf_op jit(solution)/shard_map/ppermute | solution.py:19
  91.3 11.6 %collective-permute-start.35 = (bf16[24,2304]{1,0:T(8,128)(2,1)S(1)}, bf16[24,2304]{1,0:T(8,128)(2,1)S(1)}, u32[]{:S(2)}, u32[]{:S(2)}) collective-permute-start(bf16[24,2304]{1,0:T(8,128)(2,1)S(1)} %error.1.refs_13_.refs_0_), channel_id=1, source_target_pairs={{0,8},{2,10},{4,12},{6,14},{8,0},{10,2},{12,4},{14,6},{16,24},{18,... | collective-permute-start | bytes 331784 | tf_op jit(solution)/shard_map/ppermute | solution.py:19
  94.3 8.7 %collective-permute-start.36 = (bf16[24,2304]{1,0:T(8,128)(2,1)S(1)}, bf16[24,2304]{1,0:T(8,128)(2,1)S(1)}, u32[]{:S(2)}, u32[]{:S(2)}) collective-permute-start(bf16[24,2304]{1,0:T(8,128)(2,1)S(1)} %error.1.refs_13_.refs_0_), channel_id=1, source_target_pairs={{0,16},{2,18},{4,20},{6,22},{8,24},{10,26},{12,28},{14,30},{16,0},... | collective-permute-start | bytes 331784 | tf_op jit(solution)/shard_map/ppermute | solution.py:19
  98.1 6.8 %collective-permute-start.37 = (bf16[24,2304]{1,0:T(8,128)(2,1)S(1)}, bf16[24,2304]{1,0:T(8,128)(2,1)S(1)}, u32[]{:S(2)}, u32[]{:S(2)}) collective-permute-start(bf16[24,2304]{1,0:T(8,128)(2,1)S(1)} %error.1.refs_13_.refs_0_), channel_id=1, source_target_pairs={{0,24},{2,26},{4,28},{6,30},{8,16},{10,18},{12,20},{14,22},{16,8},... | collective-permute-start | bytes 331784 | tf_op jit(solution)/shard_map/ppermute | solution.py:19
  102.4 6.3 %collective-permute-start.33 = (bf16[192,2304]{1,0:T(8,128)(2,1)S(1)}, bf16[192,2304]{1,0:T(8,128)(2,1)S(1)}, u32[]{:S(2)}, u32[]{:S(2)}) collective-permute-start(bf16[192,2304]{1,0:T(8,128)(2,1)S(1)} %get-tuple-element.103.refs_0_.refs_3_.refs_10_), channel_id=1, source_target_pairs={{0,2},{2,0},{4,6},{6,4},{8,10},{10,8},{12,14},{14,12},{16,18},{18,... | collective-permute-start | bytes 2654216 | tf_op jit(solution)/shard_map/ppermute | solution.py:19
  105.0 8.8 %collective-permute-start.38 = (bf16[72,2304]{1,0:T(8,128)(2,1)S(1)}, bf16[72,2304]{1,0:T(8,128)(2,1)S(1)}, u32[]{:S(2)}, u32[]{:S(2)}) collective-permute-start(bf16[72,2304]{1,0:T(8,128)(2,1)S(1)} %get-tuple-element.105), channel_id=1, source_target_pairs={{0,4},{2,6},{4,0},{6,2},{8,12},{10,14},{12,8},{14,10},{16,20},{18,... | collective-permute-start | bytes 995336 | tf_op jit(solution)/shard_map/ppermute | solution.py:19
  105.9 8.2 %collective-permute-start.39 = (bf16[72,2304]{1,0:T(8,128)(2,1)S(1)}, bf16[72,2304]{1,0:T(8,128)(2,1)S(1)}, u32[]{:S(2)}, u32[]{:S(2)}) collective-permute-start(bf16[72,2304]{1,0:T(8,128)(2,1)S(1)} %get-tuple-element.105), channel_id=1, source_target_pairs={{0,1},{1,0},{2,3},{3,2},{4,5},{5,4},{6,7},{7,6},{8,9},{9,8},{10,11... | collective-permute-start | bytes 995336 | tf_op jit(solution)/shard_map/ppermute | solution.py:19
  114.2 8.1 %collective-permute-start.42 = (bf16[192,2304]{1,0:T(8,128)(2,1)S(1)}, bf16[192,2304]{1,0:T(8,128)(2,1)S(1)}, u32[]{:S(2)}, u32[]{:S(2)}) collective-permute-start(bf16[192,2304]{1,0:T(8,128)(2,1)S(1)} %get-tuple-element.109.refs_2_.refs_16_), channel_id=1, source_target_pairs={{0,2},{2,0},{4,6},{6,4},{8,10},{10,8},{12,14},{14,12},{16,18},{18,... | collective-permute-start | bytes 2654216 | tf_op jit(solution)/shard_map/ppermute | solution.py:19
  114.8 12.2 %collective-permute-start.40 = (bf16[96,2304]{1,0:T(8,128)(2,1)S(1)}, bf16[96,2304]{1,0:T(8,128)(2,1)S(1)}, u32[]{:S(2)}, u32[]{:S(2)}) collective-permute-start(bf16[96,2304]{1,0:T(8,128)(2,1)S(1)} %get-tuple-element.107), channel_id=1, source_target_pairs={{0,4},{2,6},{4,0},{6,2},{8,12},{10,14},{12,8},{14,10},{16,20},{18,... | collective-permute-start | bytes 1327112 | tf_op jit(solution)/shard_map/ppermute | solution.py:19
  116.2 11.9 %collective-permute-start.41 = (bf16[96,2304]{1,0:T(8,128)(2,1)S(1)}, bf16[96,2304]{1,0:T(8,128)(2,1)S(1)}, u32[]{:S(2)}, u32[]{:S(2)}) collective-permute-start(bf16[96,2304]{1,0:T(8,128)(2,1)S(1)} %get-tuple-element.108), channel_id=1, source_target_pairs={{0,1},{1,0},{2,3},{3,2},{4,5},{5,4},{6,7},{7,6},{8,9},{9,8},{10,11... | collective-permute-start | bytes 1327112 | tf_op jit(solution)/shard_map/ppermute | solution.py:19
  (17 other events, 66.4 us)

commit v6 on v5

--- a/solution.py
+++ b/solution.py
@@ -379,13 +379,13 @@
         out[:, at] = dot(left, right[:, at], ((0,), (0,)))
 
 
-def ahead(codes, errors, own):
+def ahead(codes, errors, own, after=()):
     lists = [[some(p) for p in parts] for parts in (codes, errors)]
     rows = [[p[1:] for p in parts] for parts in lists]
     arrays = [p[0] for parts in lists for p in parts]
     out = ((own, arrays[-1].shape[1]), jnp.float32)
     flops = 2 * math.prod(out[0]) * sum(r[1] for r in rows[0])
-    return local(functools.partial(ahead_kernel, rows, own), "ahead", arrays, [out], (), flops)[0]
+    return local(functools.partial(ahead_kernel, rows, own), "ahead", arrays, [out], after, flops)[0]
 
 
 def grads_body(layers, scale, rows, own, late, *refs):
@@ -396,7 +396,7 @@
             lists[-1].append(list(zip(refs, bounds)))
             refs = refs[len(bounds):]
     codes, errors, inputs, grads = lists
-    early, sums, refs = refs[0], refs[1:-7], refs[-7:]
+    early, sums, refs = refs[:layers], refs[layers:-7], refs[-7:]
     dec_out, enc_out, bias_out, dec_held, enc_held, dec_sems, enc_sems = refs
     copies = []
     def leave(held, out, sems, slot, left, right, before=None):
@@ -417,8 +417,8 @@
         for t in range(s, layers):
             slot, before, first = pair_slot(s, t, layers), None, left
             right = errors[t]
-            if slot == 0:
-                before, first, right = early, gathered(codes[s][-late:], own[0]), right[-late:]
+            if s == 0:
+                before, first, right = early[t], gathered(codes[s][-late:], own[0]), right[-late:]
             leave(dec_held, dec_out, dec_sems, slot, first, gathered(right, dec_out.shape[2]), before)
     for s in range(layers):
         leave(enc_held, enc_out, enc_sems, s, gathered(inputs[s], own[1]), gathered(grads[s], enc_out.shape[2]))
@@ -435,7 +435,7 @@
     rows = [[[p[1:] for p in parts] for parts in each] for each in lists]
     dec = (layers * (layers + 1) // 2, own[0], lists[1][0][0][0].shape[1])
     enc = (layers, own[1], lists[3][0][0][0].shape[1])
-    arrays = [p[0] for each in lists for parts in each for p in parts] + [early, *sums]
+    arrays = [p[0] for each in lists for parts in each for p in parts] + [*early, *sums]
     arrays = [pltpu.with_memory_space_constraint(a, pltpu.VMEM) for a in arrays]
     return pl.pallas_call(
         functools.partial(grads_body, layers, scale, rows, own, late),
@@ -626,7 +626,8 @@
     left = quart - hop
     far0, far1 = join([[(x_o, 0, hop), (y_t, 0, left)], [(x_o, hop, hop), (y_t, left, left)]], done)
     far_errs = [[far0, core(far0)], [far1, core(far1)]]
-    grad_far, sum_far = back(far_errs, far_pre, dec_held, layers, True)
+    early = [early, ahead([code0] + halves(there_code0)[0], err1 + near_err1, share[0], [far0])]
+    grad_far, sum_far = back(far_errs, far_pre, dec_held, layers, True, (), early[1:])
     codes = [sum(halves(c), []) for c in (there_code0, there_code1)]
     seen = [nears(p) + fars(p) for p in (there_in0, there_in1)]
     dec_out, enc_out, bias_out = all_grads(

time: 146 us -> 146 us (level)
  waiting for transfers between devices: 47.4 us -> 43.8 us
  starting transfers between devices: 43.2 us -> 45.5 us
    ppermute x46, waiting for transfers between devices: 47.4 us -> 43.8 us  [swap(): lax.ppermute(value, axis, [(i, i ^ bits) for i in range(lax.axis_size(axi...]
    ppermute x46, starting transfers between devices: 43.2 us -> 45.5 us  [swap(): lax.ppermute(value, axis, [(i, i ^ bits) for i in range(lax.axis_size(axi...]
    pallas_call x27 -> x28, Pallas kernels: 33.8 us -> 36 us  [local(): pl.pallas_call(lambda *refs: kernel(*refs[skip:]), name=name, out_shape=[...]
  transfers between devices with their start and end apart: 46 -> 46, of which waited for: 22 -> 21; matrix products, arithmetic and copies ran while one was open for 0% -> 0% of each run, Pallas kernels for 25% -> 27%
where the time goes in v6:
time: 146 us
  Pallas kernels  53.7 us (37%)
  starting transfers between devices  45.5 us (31%)
  waiting for transfers between devices  43.8 us (30%)
    ppermute x46, starting transfers between devices, swap(): lax.ppermute(value, axis, [(i, i ^ bits) for i in range(lax.axis_size(axi...  45.5 us
    ppermute x46, waiting for transfers between devices, swap(): lax.ppermute(value, axis, [(i, i ^ bits) for i in range(lax.axis_size(axi...  43.8 us
    pallas_call x28, Pallas kernels, local(): pl.pallas_call(lambda *refs: kernel(*refs[skip:]), name=name, out_shape=[...  36 us
    pallas_call x1, Pallas kernels, all_grads(): pl.pallas_call(functools.partial(grads_body, layers, scale, rows, own, la...  8.97 us
    pallas_call x2, Pallas kernels, load(): pl.pallas_call(lambda *refs: load_kernel(count, *refs[skip:]), name='load...  8.72 us
  transfers between devices with their start and end apart: 46, of which 21 were waited for; matrix products, arithmetic and copies ran while one was open for 0% of the time, Pallas kernels for 27%

profile of v6, /device:TPU:0, one launch (start us, length us, event | category | flops | bytes accessed | tf_op | source)
XLA Modules:
  0.0 145.8 jit_solution(147243833435092808)
XLA Ops:
  1.6 5.1 %collective-permute-start.2 = (bf16[24,2304]{1,0:T(8,128)(2,1)S(1)}, bf16[24,2304]{1,0:T(8,128)(2,1)S(1)}, u32[]{:S(2)}, u32[]{:S(2)}) collective-permute-start(bf16[24,2304]{1,0:T(8,128)(2,1)S(1)} %bitcast.10), channel_id=1, source_target_pairs={{0,24},{2,26},{4,28},{6,30},{8,16},{10,18},{12,20},{14,22},{16,8},... | collective-permute-start | bytes 331784 | tf_op jit(solution)/shard_map/ppermute | solution.py:19
  7.4 3.7 %load.2.refs_3_.refs_2_ = bf16[2,2304,1024]{2,1,0:T(8,128)(2,1)S(1)} custom-call(bf16[2,2304,1024]{2,1,0:T(8,128)(2,1)} %refs_0_.1), custom_call_target="tpu_custom_call" | custom-call | tf_op jit(solution)/shard_map/load/pallas_call | solution.py:106
  11.1 4.9 %collective-permute-done.1.refs_1_.refs_5_.refs_8_ = bf16[24,2304]{1,0:T(8,128)(2,1)S(1)} collective-permute-done((bf16[24,2304]{1,0:T(8,128)(2,1)S(1)}, bf16[24,2304]{1,0:T(8,128)(2,1)S(1)}, u32[]{:S(2)}, u32[]{:S(2)}) %collective-permute-start.1) | collective-permute-done | bytes 110624 | tf_op jit(solution)/shard_map/ppermute | solution.py:19
  19.2 2.5 %collective-permute-start.5 = (bf16[24,2304]{1,0:T(8,128)(2,1)S(1)}, bf16[24,2304]{1,0:T(8,128)(2,1)S(1)}, u32[]{:S(2)}, u32[]{:S(2)}) collective-permute-start(bf16[24,2304]{1,0:T(8,128)(2,1)S(1)} %get-tuple-element.67.refs_5_), channel_id=1, source_target_pairs={{0,24},{2,26},{4,28},{6,30},{8,16},{10,18},{12,20},{14,22},{16,8},... | collective-permute-start | bytes 331784 | tf_op jit(solution)/shard_map/ppermute | solution.py:19
  21.7 1.9 %collective-permute-start.3 = (bf16[24,2304]{1,0:T(8,128)(2,1)S(1)}, bf16[24,2304]{1,0:T(8,128)(2,1)S(1)}, u32[]{:S(2)}, u32[]{:S(2)}) collective-permute-start(bf16[24,2304]{1,0:T(8,128)(2,1)S(1)} %get-tuple-element.67.refs_5_), channel_id=1, source_target_pairs={{0,8},{2,10},{4,12},{6,14},{8,0},{10,2},{12,4},{14,6},{16,24},{18,... | collective-permute-start | bytes 331784 | tf_op jit(solution)/shard_map/ppermute | solution.py:19
  23.6 5.0 %load.3.refs_5_.refs_1_.refs_3_.refs_2_.refs_6_.refs_7_.refs_8_.refs_9_.refs_10_.refs_11_ = bf16[3,1024,2304]{2,1,0:T(8,128)(2,1)S(1)} custom-call(bf16[72,2304]{1,0:T(8,128)(2,1)S(1)} %get-tuple-element.69.refs_0_.refs_10_, bf16[3,1024,2304]{2,1,0:T(8,128)(2,1)} %refs_1_.1), custom_call_target="tpu_custom_call" | custom-call | tf_op jit(solution)/shard_map/load/pallas_call | solution.py:106
  33.6 2.1 %encode.4 = (f32[384,1024]{1,0:T(8,128)S(1)}, bf16[384,1024]{1,0:T(8,128)(2,1)S(1)}) custom-call(bf16[192,2304]{1,0:T(8,128)(2,1)S(1)} %get-tuple-element.70.refs_0_.refs_22_, bf16[192,2304]{1,0:T(8,128)(2,1)S(1)} %collective-permute-done.8.refs_1_.refs_23_, bf16[2,2304,1024]{2,1,0:T(8,128)(2,1)S(1)} %load.2.refs_3_.refs_2_, ...), custom_call_target="tpu_custom_call" | custom-call | flops 1811939328 | tf_op jit(solution)/shard_map/encode/pallas_call | solution.py:57
  35.7 2.0 %decode.3 = (bf16[192,2304]{1,0:T(8,128)(2,1)S(1)}, bf16[64,2304]{1,0:T(8,128)(2,1)S(1)}, bf16[64,2304]{1,0:T(8,128)(2,1)S(1)}, bf16[64,2304]{1,0:T(8,128)(2,1)S(1)}) custom-call(bf16[384,1024]{1,0:T(8,128)(2,1)S(1)} %get-tuple-element.71.refs_0_.refs_2_.refs_1_, ...), custom_call_target="tpu_custom_call" | custom-call | flops 1811939328 | tf_op jit(solution)/shard_map/decode/pallas_call | solution.py:57
  38.4 3.0 %collective-permute-done.9.refs_0_.refs_8_.refs_12_ = bf16[72,2304]{1,0:T(8,128)(2,1)S(1)} collective-permute-done((bf16[72,2304]{1,0:T(8,128)(2,1)S(1)}, bf16[72,2304]{1,0:T(8,128)(2,1)S(1)}, u32[]{:S(2)}, u32[]{:S(2)}) %collective-permute-start.9) | collective-permute-done | bytes 331808 | tf_op jit(solution)/shard_map/ppermute | solution.py:19
  45.5 2.0 %decode.4.refs_0_.refs_2_ = f32[384,2304]{1,0:T(8,128)S(1)} custom-call(f32[96,2304]{1,0:T(8,128)S(1)} %get-tuple-element.78.refs_0_.refs_5_.refs_4_, bf16[192,2304]{1,0:T(8,128)(2,1)S(1)} %get-tuple-element.79.refs_1_.refs_28_, bf16[384,1024]{1,0:T(8,128)(2,1)S(1)} %get-tuple-element.71.refs_0_.refs_2_.refs_1_, ...), custom_call_target="tpu_custom_call" | custom-call | flops 1811939328 | tf_op jit(solution)/shard_map/decode/pallas_call | solution.py:57
  47.5 2.1 %encode.5 = (f32[384,1024]{1,0:T(8,128)S(1)}, bf16[384,1024]{1,0:T(8,128)(2,1)S(1)}) custom-call(f32[384,2304]{1,0:T(8,128)S(1)} %decode.4.refs_0_.refs_2_, bf16[192,2304]{1,0:T(8,128)(2,1)S(1)} %get-tuple-element.79.refs_1_.refs_28_, bf16[192,2304]{1,0:T(8,128)(2,1)S(1)} %collective-permute-done.15.refs_2_.refs_29_, ...), custom_call_target="tpu_custom_call" | custom-call | flops 1811939328 | tf_op jit(solution)/shard_map/encode/pallas_call | solution.py:57
  49.6 2.0 %decode.5 = (bf16[192,2304]{1,0:T(8,128)(2,1)S(1)}, bf16[64,2304]{1,0:T(8,128)(2,1)S(1)}, bf16[64,2304]{1,0:T(8,128)(2,1)S(1)}, bf16[64,2304]{1,0:T(8,128)(2,1)S(1)}) custom-call(bf16[384,1024]{1,0:T(8,128)(2,1)S(1)} %get-tuple-element.80.refs_0_.refs_5_, ...), custom_call_target="tpu_custom_call" | custom-call | flops 1811939328 | tf_op jit(solution)/shard_map/decode/pallas_call | solution.py:57
  52.9 1.8 %collective-permute-done.13.refs_0_.refs_6_.refs_5_ = bf16[96,2304]{1,0:T(8,128)(2,1)S(1)} collective-permute-done((bf16[96,2304]{1,0:T(8,128)(2,1)S(1)}, bf16[96,2304]{1,0:T(8,128)(2,1)S(1)}, u32[]{:S(2)}, u32[]{:S(2)}) %collective-permute-start.13) | collective-permute-done | bytes 442400 | tf_op jit(solution)/shard_map/ppermute | solution.py:19
  55.2 2.7 %collective-permute-start.20 = (bf16[24,2304]{1,0:T(8,128)(2,1)S(1)}, bf16[24,2304]{1,0:T(8,128)(2,1)S(1)}, u32[]{:S(2)}, u32[]{:S(2)}) collective-permute-start(bf16[24,2304]{1,0:T(8,128)(2,1)S(1)} %get-tuple-element.86), channel_id=1, source_target_pairs={{0,16},{2,18},{4,20},{6,22},{8,24},{10,26},{12,28},{14,30},{16,0},... | collective-permute-start | bytes 331784 | tf_op jit(solution)/shard_map/ppermute | solution.py:19
  61.2 5.4 %collective-permute-done.20.refs_1_.refs_7_ = bf16[24,2304]{1,0:T(8,128)(2,1)S(1)} collective-permute-done((bf16[24,2304]{1,0:T(8,128)(2,1)S(1)}, bf16[24,2304]{1,0:T(8,128)(2,1)S(1)}, u32[]{:S(2)}, u32[]{:S(2)}) %collective-permute-start.20) | collective-permute-done | bytes 110624 | tf_op jit(solution)/shard_map/ppermute | solution.py:19
  66.6 3.7 %collective-permute-done.22.refs_3_.refs_11_.refs_7_ = bf16[96,2304]{1,0:T(8,128)(2,1)S(1)} collective-permute-done((bf16[96,2304]{1,0:T(8,128)(2,1)S(1)}, bf16[96,2304]{1,0:T(8,128)(2,1)S(1)}, u32[]{:S(2)}, u32[]{:S(2)}) %collective-permute-start.22) | collective-permute-done | bytes 442400 | tf_op jit(solution)/shard_map/ppermute | solution.py:19
  70.6 2.8 %collective-permute-start.24 = (bf16[48,2304]{1,0:T(8,128)(2,1)S(1)}, bf16[48,2304]{1,0:T(8,128)(2,1)S(1)}, u32[]{:S(2)}, u32[]{:S(2)}) collective-permute-start(bf16[48,2304]{1,0:T(8,128)(2,1)S(1)} %get-tuple-element.92), channel_id=1, source_target_pairs={{0,16},{2,18},{4,20},{6,22},{8,24},{10,26},{12,28},{14,30},{16,0},... | collective-permute-start | bytes 663560 | tf_op jit(solution)/shard_map/ppermute | solution.py:19
  77.8 2.0 %collective-permute-done.27.refs_4_.refs_5_ = bf16[24,2304]{1,0:T(8,128)(2,1)S(1)} collective-permute-done((bf16[24,2304]{1,0:T(8,128)(2,1)S(1)}, bf16[24,2304]{1,0:T(8,128)(2,1)S(1)}, u32[]{:S(2)}, u32[]{:S(2)}) %collective-permute-start.27) | collective-permute-done | bytes 110624 | tf_op jit(solution)/shard_map/ppermute | solution.py:19
  81.0 7.6 %collective-permute-done.24.refs_1_.refs_9_.refs_8_.refs_11_ = bf16[48,2304]{1,0:T(8,128)(2,1)S(1)} collective-permute-done((bf16[48,2304]{1,0:T(8,128)(2,1)S(1)}, bf16[48,2304]{1,0:T(8,128)(2,1)S(1)}, u32[]{:S(2)}, u32[]{:S(2)}) %collective-permute-start.24) | collective-permute-done | bytes 221216 | tf_op jit(solution)/shard_map/ppermute | solution.py:19
  91.9 1.9 %collective-permute-start.37 = (bf16[24,2304]{1,0:T(8,128)(2,1)S(1)}, bf16[24,2304]{1,0:T(8,128)(2,1)S(1)}, u32[]{:S(2)}, u32[]{:S(2)}) collective-permute-start(bf16[24,2304]{1,0:T(8,128)(2,1)S(1)} %error.1.refs_13_.refs_0_), channel_id=1, source_target_pairs={{0,24},{2,26},{4,28},{6,30},{8,16},{10,18},{12,20},{14,22},{16,8},... | collective-permute-start | bytes 331784 | tf_op jit(solution)/shard_map/ppermute | solution.py:19
  93.8 2.6 %collective-permute-start.36 = (bf16[24,2304]{1,0:T(8,128)(2,1)S(1)}, bf16[24,2304]{1,0:T(8,128)(2,1)S(1)}, u32[]{:S(2)}, u32[]{:S(2)}) collective-permute-start(bf16[24,2304]{1,0:T(8,128)(2,1)S(1)} %error.1.refs_13_.refs_0_), channel_id=1, source_target_pairs={{0,16},{2,18},{4,20},{6,22},{8,24},{10,26},{12,28},{14,30},{16,0},... | collective-permute-start | bytes 331784 | tf_op jit(solution)/shard_map/ppermute | solution.py:19
  96.4 2.2 %encode.7 = (f32[384,1024]{1,0:T(8,128)S(1)}, bf16[384,1024]{1,0:T(8,128)(2,1)S(1)}) custom-call(bf16[192,2304]{1,0:T(8,128)(2,1)S(1)} %get-tuple-element.100.refs_0_.refs_30_.refs_32_, bf16[192,2304]{1,0:T(8,128)(2,1)S(1)} %collective-permute-done.30.refs_1_.refs_31_.refs_33_, bf16[2,2304,1024]{2,1,0:T(8,128)(2,1)S(1)} %load.2.refs_3_.refs_2_, ...), custom_call_target="tpu_custom_call" | custom-call | flops 1811939328 | tf_op jit(solution)/shard_map/encode/pallas_call | solution.py:57
  98.7 2.0 %encode.6 = (f32[384,1024]{1,0:T(8,128)S(1)}, bf16[384,1024]{1,0:T(8,128)(2,1)S(1)}) custom-call(bf16[192,2304]{1,0:T(8,128)(2,1)S(1)} %get-tuple-element.98.refs_0_.refs_24_.refs_26_, bf16[192,2304]{1,0:T(8,128)(2,1)S(1)} %collective-permute-done.29.refs_1_.refs_25_.refs_27_, bf16[2,2304,1024]{2,1,0:T(8,128)(2,1)S(1)} %load.2.refs_3_.refs_2_, ...), custom_call_target="tpu_custom_call" | custom-call | flops 1811939328 | tf_op jit(solution)/shard_map/encode/pallas_call | solution.py:57
  103.0 2.4 %collective-permute-done.36.refs_2_.refs_5_ = bf16[24,2304]{1,0:T(8,128)(2,1)S(1)} collective-permute-done((bf16[24,2304]{1,0:T(8,128)(2,1)S(1)}, bf16[24,2304]{1,0:T(8,128)(2,1)S(1)}, u32[]{:S(2)}, u32[]{:S(2)}) %collective-permute-start.36) | collective-permute-done | bytes 110624 | tf_op jit(solution)/shard_map/ppermute | solution.py:19
  109.2 2.0 %first.2.refs_2_.refs_9_ = f32[384,1024]{1,0:T(8,128)S(1)} custom-call(bf16[192,2304]{1,0:T(8,128)(2,1)S(1)} %get-tuple-element.103.refs_0_.refs_3_.refs_10_, bf16[192,2304]{1,0:T(8,128)(2,1)S(1)} %collective-permute-done.33.refs_1_.refs_4_.refs_11_, ...), custom_call_target="tpu_custom_call" | custom-call | flops 1811939328 | tf_op jit(solution)/shard_map/first/pallas_call | solution.py:57
  111.2 3.7 %collective-permute-done.39.refs_1_.refs_8_.refs_11_ = bf16[72,2304]{1,0:T(8,128)(2,1)S(1)} collective-permute-done((bf16[72,2304]{1,0:T(8,128)(2,1)S(1)}, bf16[72,2304]{1,0:T(8,128)(2,1)S(1)}, u32[]{:S(2)}, u32[]{:S(2)}) %collective-permute-start.39) | collective-permute-done | bytes 331808 | tf_op jit(solution)/shard_map/ppermute | solution.py:19
  118.0 2.1 %ahead.2.refs_4_.refs_40_ = f32[512,2304]{1,0:T(8,128)S(1)} custom-call(bf16[384,1024]{1,0:T(8,128)(2,1)S(1)} %get-tuple-element.71.refs_0_.refs_2_.refs_1_, bf16[384,1024]{1,0:T(8,128)(2,1)S(1)} %get-tuple-element.99.refs_0_.refs_1_.refs_2_.refs_3_.refs_4_, bf16[384,1024]{1,0:T(8,128)(2,1)S(1)} %get-tuple-element.99.refs_0_.refs_1_.refs_2_.refs_3_.refs_4_, ...), custom_call_target="tpu_custom_call" | custom-call | flops 1358954496 | tf_op jit(solution)/shard_map/ahead/pallas_call | solution.py:57
  120.1 3.2 %back.4 = (bf16[192,1024]{1,0:T(8,128)(2,1)S(1)}, bf16[192,1024]{1,0:T(8,128)(2,1)S(1)}, f32[2,1,1024]{2,1,0:T(1,128)S(1)}) custom-call(bf16[96,2304]{1,0:T(8,128)(2,1)S(1)} %get-tuple-element.104.refs_0_.refs_9_.refs_5_.refs_12_, bf16[96,2304]{1,0:T(8,128)(2,1)S(1)} %collective-permute-done.34.refs_1_.refs_6_.refs_13_, ...), custom_call_target="tpu_custom_call" | custom-call | flops 1811939328 | tf_op jit(solution)/shard_map/back/pallas_call | solution.py:57
  123.3 3.9 %back.3 = (bf16[384,1024]{1,0:T(8,128)(2,1)S(1)}, bf16[384,1024]{1,0:T(8,128)(2,1)S(1)}, f32[2,1,1024]{2,1,0:T(1,128)S(1)}) custom-call(bf16[192,2304]{1,0:T(8,128)(2,1)S(1)} %get-tuple-element.103.refs_0_.refs_3_.refs_10_, bf16[192,2304]{1,0:T(8,128)(2,1)S(1)} %collective-permute-done.33.refs_1_.refs_4_.refs_11_, ...), custom_call_target="tpu_custom_call" | custom-call | flops 3623878656 | tf_op jit(solution)/shard_map/back/pallas_call | solution.py:57
  129.5 2.3 %ahead.3.refs_0_.refs_41_ = f32[512,2304]{1,0:T(8,128)S(1)} custom-call(bf16[96,2304]{1,0:T(8,128)(2,1)S(1)} %get-tuple-element.117.refs_0_.refs_1_.refs_14_, bf16[384,1024]{1,0:T(8,128)(2,1)S(1)} %get-tuple-element.71.refs_0_.refs_2_.refs_1_, bf16[384,1024]{1,0:T(8,128)(2,1)S(1)} %get-tuple-element.99.refs_0_.refs_1_.refs_2_.refs_3_.refs_4_, ...), custom_call_target="tpu_custom_call" | custom-call | flops 1358954496 | tf_op jit(solution)/shard_map/ahead/pallas_call | solution.py:57
  131.9 4.7 %back.5 = (bf16[192,1024]{1,0:T(8,128)(2,1)S(1)}, bf16[192,1024]{1,0:T(8,128)(2,1)S(1)}, f32[2,1,1024]{2,1,0:T(1,128)S(1)}) custom-call(f32[512,2304]{1,0:T(8,128)S(1)} %ahead.3.refs_0_.refs_41_, bf16[96,2304]{1,0:T(8,128)(2,1)S(1)} %get-tuple-element.117.refs_0_.refs_1_.refs_14_, bf16[96,2304]{1,0:T(8,128)(2,1)S(1)} %collective-permute-done.44.refs_2_.refs_15_, ...), custom_call_target="tpu_custom_call" | custom-call | flops 2717908992 | tf_op jit(solution)/shard_map/back/pallas_call | solution.py:57
  136.7 9.0 %grads.1 = (bf16[3,512,2304]{2,1,0:T(8,128)(2,1)}, bf16[2,1152,1024]{2,1,0:T(8,128)(2,1)}, f32[2,512]{1,0:T(2,128)}) custom-call(bf16[384,1024]{1,0:T(8,128)(2,1)S(1)} %get-tuple-element.71.refs_0_.refs_2_.refs_1_, bf16[384,1024]{1,0:T(8,128)(2,1)S(1)} %get-tuple-element.99.refs_0_.refs_1_.refs_2_.refs_3_.refs_4_, ...), custom_call_target="tpu_custom_call" | custom-call | tf_op jit(solution)/shard_map/grads/pallas_call | solution.py:440
  (127 shorter events, 39.8 us)
Async XLA Ops:
  1.6 9.5 %collective-permute-start.2 = (bf16[24,2304]{1,0:T(8,128)(2,1)S(1)}, bf16[24,2304]{1,0:T(8,128)(2,1)S(1)}, u32[]{:S(2)}, u32[]{:S(2)}) collective-permute-start(bf16[24,2304]{1,0:T(8,128)(2,1)S(1)} %bitcast.10), channel_id=1, source_target_pairs={{0,24},{2,26},{4,28},{6,30},{8,16},{10,18},{12,20},{14,22},{16,8},... | collective-permute-start | bytes 331784 | tf_op jit(solution)/shard_map/ppermute | solution.py:19
  6.7 9.3 %collective-permute-start.1 = (bf16[24,2304]{1,0:T(8,128)(2,1)S(1)}, bf16[24,2304]{1,0:T(8,128)(2,1)S(1)}, u32[]{:S(2)}, u32[]{:S(2)}) collective-permute-start(bf16[24,2304]{1,0:T(8,128)(2,1)S(1)} %bitcast.11), channel_id=1, source_target_pairs={{0,16},{2,18},{4,20},{6,22},{8,24},{10,26},{12,28},{14,30},{16,0},... | collective-permute-start | bytes 331784 | tf_op jit(solution)/shard_map/ppermute | solution.py:19
  6.7 9.3 %collective-permute-start = (bf16[24,2304]{1,0:T(8,128)(2,1)S(1)}, bf16[24,2304]{1,0:T(8,128)(2,1)S(1)}, u32[]{:S(2)}, u32[]{:S(2)}) collective-permute-start(bf16[24,2304]{1,0:T(8,128)(2,1)S(1)} %bitcast.12), channel_id=1, source_target_pairs={{0,8},{2,10},{4,12},{6,14},{8,0},{10,2},{12,4},{14,6},{16,24},{18,... | collective-permute-start | bytes 331784 | tf_op jit(solution)/shard_map/ppermute | solution.py:19
  16.1 14.4 %collective-permute-start.7 = (bf16[120,2304]{1,0:T(8,128)(2,1)S(1)}, bf16[120,2304]{1,0:T(8,128)(2,1)S(1)}, u32[]{:S(2)}, u32[]{:S(2)}) collective-permute-start(bf16[120,2304]{1,0:T(8,128)(2,1)S(1)} %get-tuple-element.68), channel_id=1, source_target_pairs={{0,1},{1,0},{2,3},{3,2},{4,5},{5,4},{6,7},{7,6},{8,9},{9,8},{10,11... | collective-permute-start | bytes 1658888 | tf_op jit(solution)/shard_map/ppermute | solution.py:19
  17.7 13.3 %collective-permute-start.6 = (bf16[120,2304]{1,0:T(8,128)(2,1)S(1)}, bf16[120,2304]{1,0:T(8,128)(2,1)S(1)}, u32[]{:S(2)}, u32[]{:S(2)}) collective-permute-start(bf16[120,2304]{1,0:T(8,128)(2,1)S(1)} %get-tuple-element.68), channel_id=1, source_target_pairs={{0,4},{2,6},{4,0},{6,2},{8,12},{10,14},{12,8},{14,10},{16,20},{18,... | collective-permute-start | bytes 1658888 | tf_op jit(solution)/shard_map/ppermute | solution.py:19
  19.2 9.4 %collective-permute-start.5 = (bf16[24,2304]{1,0:T(8,128)(2,1)S(1)}, bf16[24,2304]{1,0:T(8,128)(2,1)S(1)}, u32[]{:S(2)}, u32[]{:S(2)}) collective-permute-start(bf16[24,2304]{1,0:T(8,128)(2,1)S(1)} %get-tuple-element.67.refs_5_), channel_id=1, source_target_pairs={{0,24},{2,26},{4,28},{6,30},{8,16},{10,18},{12,20},{14,22},{16,8},... | collective-permute-start | bytes 331784 | tf_op jit(solution)/shard_map/ppermute | solution.py:19
  21.7 8.8 %collective-permute-start.4 = (bf16[24,2304]{1,0:T(8,128)(2,1)S(1)}, bf16[24,2304]{1,0:T(8,128)(2,1)S(1)}, u32[]{:S(2)}, u32[]{:S(2)}) collective-permute-start(bf16[24,2304]{1,0:T(8,128)(2,1)S(1)} %get-tuple-element.67.refs_5_), channel_id=1, source_target_pairs={{0,16},{2,18},{4,20},{6,22},{8,24},{10,26},{12,28},{14,30},{16,0},... | collective-permute-start | bytes 331784 | tf_op jit(solution)/shard_map/ppermute | solution.py:19
  21.7 8.8 %collective-permute-start.3 = (bf16[24,2304]{1,0:T(8,128)(2,1)S(1)}, bf16[24,2304]{1,0:T(8,128)(2,1)S(1)}, u32[]{:S(2)}, u32[]{:S(2)}) collective-permute-start(bf16[24,2304]{1,0:T(8,128)(2,1)S(1)} %get-tuple-element.67.refs_5_), channel_id=1, source_target_pairs={{0,8},{2,10},{4,12},{6,14},{8,0},{10,2},{12,4},{14,6},{16,24},{18,... | collective-permute-start | bytes 331784 | tf_op jit(solution)/shard_map/ppermute | solution.py:19
  31.2 10.3 %collective-permute-start.9 = (bf16[72,2304]{1,0:T(8,128)(2,1)S(1)}, bf16[72,2304]{1,0:T(8,128)(2,1)S(1)}, u32[]{:S(2)}, u32[]{:S(2)}) collective-permute-start(bf16[72,2304]{1,0:T(8,128)(2,1)S(1)} %get-tuple-element.72.refs_6_), channel_id=1, source_target_pairs={{0,4},{2,6},{4,0},{6,2},{8,12},{10,14},{12,8},{14,10},{16,20},{18,... | collective-permute-start | bytes 995336 | tf_op jit(solution)/shard_map/ppermute | solution.py:19
  41.8 5.7 %collective-permute-start.15 = (bf16[192,2304]{1,0:T(8,128)(2,1)S(1)}, bf16[192,2304]{1,0:T(8,128)(2,1)S(1)}, u32[]{:S(2)}, u32[]{:S(2)}) collective-permute-start(bf16[192,2304]{1,0:T(8,128)(2,1)S(1)} %get-tuple-element.79.refs_1_.refs_28_), channel_id=1, source_target_pairs={{0,2},{2,0},{4,6},{6,4},{8,10},{10,8},{12,14},{14,12},{16,18},{18,... | collective-permute-start | bytes 2654216 | tf_op jit(solution)/shard_map/ppermute | solution.py:19
  41.9 10.7 %collective-permute-start.14 = (bf16[72,2304]{1,0:T(8,128)(2,1)S(1)}, bf16[72,2304]{1,0:T(8,128)(2,1)S(1)}, u32[]{:S(2)}, u32[]{:S(2)}) collective-permute-start(bf16[72,2304]{1,0:T(8,128)(2,1)S(1)} %get-tuple-element.72.refs_6_), channel_id=1, source_target_pairs={{0,1},{1,0},{2,3},{3,2},{4,5},{5,4},{6,7},{7,6},{8,9},{9,8},{10,11... | collective-permute-start | bytes 995336 | tf_op jit(solution)/shard_map/ppermute | solution.py:19
  42.5 12.2 %collective-permute-start.13 = (bf16[96,2304]{1,0:T(8,128)(2,1)S(1)}, bf16[96,2304]{1,0:T(8,128)(2,1)S(1)}, u32[]{:S(2)}, u32[]{:S(2)}) collective-permute-start(bf16[96,2304]{1,0:T(8,128)(2,1)S(1)} %get-tuple-element.77.refs_4_), channel_id=1, source_target_pairs={{0,4},{2,6},{4,0},{6,2},{8,12},{10,14},{12,8},{14,10},{16,20},{18,... | collective-permute-start | bytes 1327112 | tf_op jit(solution)/shard_map/ppermute | solution.py:19
  43.9 32.3 %collective-permute-start.28 = (bf16[192,2304]{1,0:T(8,128)(2,1)S(1)}, bf16[192,2304]{1,0:T(8,128)(2,1)S(1)}, u32[]{:S(2)}, u32[]{:S(2)}) collective-permute-start(bf16[192,2304]{1,0:T(8,128)(2,1)S(1)} %get-tuple-element.95), channel_id=1, source_target_pairs={{0,1},{1,0},{2,3},{3,2},{4,5},{5,4},{6,7},{7,6},{8,9},{9,8},{10,11... | collective-permute-start | bytes 2654216 | tf_op jit(solution)/shard_map/ppermute | solution.py:19
  55.0 6.2 %collective-permute-start.19 = (bf16[24,2304]{1,0:T(8,128)(2,1)S(1)}, bf16[24,2304]{1,0:T(8,128)(2,1)S(1)}, u32[]{:S(2)}, u32[]{:S(2)}) collective-permute-start(bf16[24,2304]{1,0:T(8,128)(2,1)S(1)} %get-tuple-element.85), channel_id=1, source_target_pairs={{0,8},{2,10},{4,12},{6,14},{8,0},{10,2},{12,4},{14,6},{16,24},{18,... | collective-permute-start | bytes 331784 | tf_op jit(solution)/shard_map/ppermute | solution.py:19
  55.2 11.4 %collective-permute-start.20 = (bf16[24,2304]{1,0:T(8,128)(2,1)S(1)}, bf16[24,2304]{1,0:T(8,128)(2,1)S(1)}, u32[]{:S(2)}, u32[]{:S(2)}) collective-permute-start(bf16[24,2304]{1,0:T(8,128)(2,1)S(1)} %get-tuple-element.86), channel_id=1, source_target_pairs={{0,16},{2,18},{4,20},{6,22},{8,24},{10,26},{12,28},{14,30},{16,0},... | collective-permute-start | bytes 331784 | tf_op jit(solution)/shard_map/ppermute | solution.py:19
  57.9 8.7 %collective-permute-start.21 = (bf16[24,2304]{1,0:T(8,128)(2,1)S(1)}, bf16[24,2304]{1,0:T(8,128)(2,1)S(1)}, u32[]{:S(2)}, u32[]{:S(2)}) collective-permute-start(bf16[24,2304]{1,0:T(8,128)(2,1)S(1)} %get-tuple-element.87), channel_id=1, source_target_pairs={{0,24},{2,26},{4,28},{6,30},{8,16},{10,18},{12,20},{14,22},{16,8},... | collective-permute-start | bytes 331784 | tf_op jit(solution)/shard_map/ppermute | solution.py:19
  59.5 10.8 %collective-permute-start.22 = (bf16[96,2304]{1,0:T(8,128)(2,1)S(1)}, bf16[96,2304]{1,0:T(8,128)(2,1)S(1)}, u32[]{:S(2)}, u32[]{:S(2)}) collective-permute-start(bf16[96,2304]{1,0:T(8,128)(2,1)S(1)} %get-tuple-element.88), channel_id=1, source_target_pairs={{0,4},{2,6},{4,0},{6,2},{8,12},{10,14},{12,8},{14,10},{16,20},{18,... | collective-permute-start | bytes 1327112 | tf_op jit(solution)/shard_map/ppermute | solution.py:19
  70.6 10.5 %collective-permute-start.23 = (bf16[48,2304]{1,0:T(8,128)(2,1)S(1)}, bf16[48,2304]{1,0:T(8,128)(2,1)S(1)}, u32[]{:S(2)}, u32[]{:S(2)}) collective-permute-start(bf16[48,2304]{1,0:T(8,128)(2,1)S(1)} %get-tuple-element.91), channel_id=1, source_target_pairs={{0,8},{2,10},{4,12},{6,14},{8,0},{10,2},{12,4},{14,6},{16,24},{18,... | collective-permute-start | bytes 663560 | tf_op jit(solution)/shard_map/ppermute | solution.py:19
  70.6 17.9 %collective-permute-start.24 = (bf16[48,2304]{1,0:T(8,128)(2,1)S(1)}, bf16[48,2304]{1,0:T(8,128)(2,1)S(1)}, u32[]{:S(2)}, u32[]{:S(2)}) collective-permute-start(bf16[48,2304]{1,0:T(8,128)(2,1)S(1)} %get-tuple-element.92), channel_id=1, source_target_pairs={{0,16},{2,18},{4,20},{6,22},{8,24},{10,26},{12,28},{14,30},{16,0},... | collective-permute-start | bytes 663560 | tf_op jit(solution)/shard_map/ppermute | solution.py:19
  73.5 15.1 %collective-permute-start.25 = (bf16[48,2304]{1,0:T(8,128)(2,1)S(1)}, bf16[48,2304]{1,0:T(8,128)(2,1)S(1)}, u32[]{:S(2)}, u32[]{:S(2)}) collective-permute-start(bf16[48,2304]{1,0:T(8,128)(2,1)S(1)} %get-tuple-element.93), channel_id=1, source_target_pairs={{0,24},{2,26},{4,28},{6,30},{8,16},{10,18},{12,20},{14,22},{16,8},... | collective-permute-start | bytes 663560 | tf_op jit(solution)/shard_map/ppermute | solution.py:19
  89.0 9.7 %collective-permute-start.29 = (bf16[192,2304]{1,0:T(8,128)(2,1)S(1)}, bf16[192,2304]{1,0:T(8,128)(2,1)S(1)}, u32[]{:S(2)}, u32[]{:S(2)}) collective-permute-start(bf16[192,2304]{1,0:T(8,128)(2,1)S(1)} %get-tuple-element.98.refs_0_.refs_24_.refs_26_), channel_id=1, source_target_pairs={{0,2},{2,0},{4,6},{6,4},{8,10},{10,8},{12,14},{14,12},{16,18},{18,... | collective-permute-start | bytes 2654216 | tf_op jit(solution)/shard_map/ppermute | solution.py:19
  89.4 12.2 %collective-permute-start.32 = (bf16[96,2304]{1,0:T(8,128)(2,1)S(1)}, bf16[96,2304]{1,0:T(8,128)(2,1)S(1)}, u32[]{:S(2)}, u32[]{:S(2)}) collective-permute-start(bf16[96,2304]{1,0:T(8,128)(2,1)S(1)} %get-tuple-element.97.refs_6_), channel_id=1, source_target_pairs={{0,1},{1,0},{2,3},{3,2},{4,5},{5,4},{6,7},{7,6},{8,9},{9,8},{10,11... | collective-permute-start | bytes 1327112 | tf_op jit(solution)/shard_map/ppermute | solution.py:19
  90.4 11.9 %collective-permute-start.31 = (bf16[96,2304]{1,0:T(8,128)(2,1)S(1)}, bf16[96,2304]{1,0:T(8,128)(2,1)S(1)}, u32[]{:S(2)}, u32[]{:S(2)}) collective-permute-start(bf16[96,2304]{1,0:T(8,128)(2,1)S(1)} %get-tuple-element.97.refs_6_), channel_id=1, source_target_pairs={{0,4},{2,6},{4,0},{6,2},{8,12},{10,14},{12,8},{14,10},{16,20},{18,... | collective-permute-start | bytes 1327112 | tf_op jit(solution)/shard_map/ppermute | solution.py:19
  91.9 11.0 %collective-permute-start.37 = (bf16[24,2304]{1,0:T(8,128)(2,1)S(1)}, bf16[24,2304]{1,0:T(8,128)(2,1)S(1)}, u32[]{:S(2)}, u32[]{:S(2)}) collective-permute-start(bf16[24,2304]{1,0:T(8,128)(2,1)S(1)} %error.1.refs_13_.refs_0_), channel_id=1, source_target_pairs={{0,24},{2,26},{4,28},{6,30},{8,16},{10,18},{12,20},{14,22},{16,8},... | collective-permute-start | bytes 331784 | tf_op jit(solution)/shard_map/ppermute | solution.py:19
  93.8 11.6 %collective-permute-start.36 = (bf16[24,2304]{1,0:T(8,128)(2,1)S(1)}, bf16[24,2304]{1,0:T(8,128)(2,1)S(1)}, u32[]{:S(2)}, u32[]{:S(2)}) collective-permute-start(bf16[24,2304]{1,0:T(8,128)(2,1)S(1)} %error.1.refs_13_.refs_0_), channel_id=1, source_target_pairs={{0,16},{2,18},{4,20},{6,22},{8,24},{10,26},{12,28},{14,30},{16,0},... | collective-permute-start | bytes 331784 | tf_op jit(solution)/shard_map/ppermute | solution.py:19
  98.7 7.2 %collective-permute-start.35 = (bf16[24,2304]{1,0:T(8,128)(2,1)S(1)}, bf16[24,2304]{1,0:T(8,128)(2,1)S(1)}, u32[]{:S(2)}, u32[]{:S(2)}) collective-permute-start(bf16[24,2304]{1,0:T(8,128)(2,1)S(1)} %error.1.refs_13_.refs_0_), channel_id=1, source_target_pairs={{0,8},{2,10},{4,12},{6,14},{8,0},{10,2},{12,4},{14,6},{16,24},{18,... | collective-permute-start | bytes 331784 | tf_op jit(solution)/shard_map/ppermute | solution.py:19
  102.4 6.8 %collective-permute-start.33 = (bf16[192,2304]{1,0:T(8,128)(2,1)S(1)}, bf16[192,2304]{1,0:T(8,128)(2,1)S(1)}, u32[]{:S(2)}, u32[]{:S(2)}) collective-permute-start(bf16[192,2304]{1,0:T(8,128)(2,1)S(1)} %get-tuple-element.103.refs_0_.refs_3_.refs_10_), channel_id=1, source_target_pairs={{0,2},{2,0},{4,6},{6,4},{8,10},{10,8},{12,14},{14,12},{16,18},{18,... | collective-permute-start | bytes 2654216 | tf_op jit(solution)/shard_map/ppermute | solution.py:19
  105.9 9.1 %collective-permute-start.39 = (bf16[72,2304]{1,0:T(8,128)(2,1)S(1)}, bf16[72,2304]{1,0:T(8,128)(2,1)S(1)}, u32[]{:S(2)}, u32[]{:S(2)}) collective-permute-start(bf16[72,2304]{1,0:T(8,128)(2,1)S(1)} %get-tuple-element.105), channel_id=1, source_target_pairs={{0,1},{1,0},{2,3},{3,2},{4,5},{5,4},{6,7},{7,6},{8,9},{9,8},{10,11... | collective-permute-start | bytes 995336 | tf_op jit(solution)/shard_map/ppermute | solution.py:19
  106.9 8.8 %collective-permute-start.38 = (bf16[72,2304]{1,0:T(8,128)(2,1)S(1)}, bf16[72,2304]{1,0:T(8,128)(2,1)S(1)}, u32[]{:S(2)}, u32[]{:S(2)}) collective-permute-start(bf16[72,2304]{1,0:T(8,128)(2,1)S(1)} %get-tuple-element.105), channel_id=1, source_target_pairs={{0,4},{2,6},{4,0},{6,2},{8,12},{10,14},{12,8},{14,10},{16,20},{18,... | collective-permute-start | bytes 995336 | tf_op jit(solution)/shard_map/ppermute | solution.py:19
  115.8 7.5 %collective-permute-start.42 = (bf16[192,2304]{1,0:T(8,128)(2,1)S(1)}, bf16[192,2304]{1,0:T(8,128)(2,1)S(1)}, u32[]{:S(2)}, u32[]{:S(2)}) collective-permute-start(bf16[192,2304]{1,0:T(8,128)(2,1)S(1)} %get-tuple-element.109.refs_2_.refs_4_.refs_16_), channel_id=1, source_target_pairs={{0,2},{2,0},{4,6},{6,4},{8,10},{10,8},{12,14},{14,12},{16,18},{18,... | collective-permute-start | bytes 2654216 | tf_op jit(solution)/shard_map/ppermute | solution.py:19
  116.4 12.2 %collective-permute-start.40 = (bf16[96,2304]{1,0:T(8,128)(2,1)S(1)}, bf16[96,2304]{1,0:T(8,128)(2,1)S(1)}, u32[]{:S(2)}, u32[]{:S(2)}) collective-permute-start(bf16[96,2304]{1,0:T(8,128)(2,1)S(1)} %get-tuple-element.107), channel_id=1, source_target_pairs={{0,4},{2,6},{4,0},{6,2},{8,12},{10,14},{12,8},{14,10},{16,20},{18,... | collective-permute-start | bytes 1327112 | tf_op jit(solution)/shard_map/ppermute | solution.py:19
  117.0 11.9 %collective-permute-start.41 = (bf16[96,2304]{1,0:T(8,128)(2,1)S(1)}, bf16[96,2304]{1,0:T(8,128)(2,1)S(1)}, u32[]{:S(2)}, u32[]{:S(2)}) collective-permute-start(bf16[96,2304]{1,0:T(8,128)(2,1)S(1)} %get-tuple-element.108), channel_id=1, source_target_pairs={{0,1},{1,0},{2,3},{3,2},{4,5},{5,4},{6,7},{7,6},{8,9},{9,8},{10,11... | collective-permute-start | bytes 1327112 | tf_op jit(solution)/shard_map/ppermute | solution.py:19
  (29 other events, 113.0 us)
